TPU v7x, 128 devices: a whole 4x4x4 slice. The times are simulated.
128 devices in a mesh: dp: 64 (over y, z_hi, x, core), tensor: 2 (over z_lo).
Axes of the slice: x: 4, y: 4, z: 4 (z_hi: 2, z_lo: 2; z = z_hi * 2 + z_lo), core: 2. Of those that a mesh axis runs over, the one named last changes fastest.
Arguments:
- layer_input: bfloat16 [32768, 1024], P('dp'), may hold values from -6 to 6
- segments: int32 [64, 512], P('dp'), may hold values from 0 to 3, never falling along the last dimension, each value on 1 to 256 neighbouring positions
- input_gain: float32 [1024], replicated, may hold values from 0.5 to 1.5
- mixer_proj: bfloat16 [1024, 2, 1536], P(None, None, 'tensor'), may hold values from -0.1875 to 0.1875
- state_proj: bfloat16 [1024, 256], replicated, may hold values from -0.1875 to 0.1875
- step_proj: bfloat16 [1024, 24], P(None, 'tensor'), may hold values from -0.1875 to 0.1875
- step_bias: float32 [24], P('tensor'), may hold values from -3 to -0.5
- decay_log: float32 [24], P('tensor'), may hold values from -6 to -1.5
- skip_gain: float32 [24], P('tensor'), may hold values from 0.5 to 1.5
- conv_kernel: float32 [4, 1536], P(None, 'tensor'), may hold values from -3 to 3
- conv_bias: float32 [1536], P('tensor'), may hold values from -3 to 3
- state_kernel: float32 [4, 256], replicated, may hold values from -3 to 3
- state_bias: float32 [256], replicated, may hold values from -3 to 3
- gated_gain: float32 [1536], P('tensor'), may hold values from 0.5 to 1.5
- mixer_out: bfloat16 [1536, 1024], P('tensor'), may hold values from -0.15625 to 0.15625
- query_proj: bfloat16 [1024, 512], P(None, 'tensor'), may hold values from -0.1875 to 0.1875
- key_value_weight: bfloat16 [1024, 2, 128], P(None, 'tensor'), may hold values from -0.1875 to 0.1875
- attn_out: bfloat16 [512, 1024], P('tensor'), may hold values from -0.75 to 0.75
- ffn_gain: float32 [1024], replicated, may hold values from 0.5 to 1.5
- ffn_gate: bfloat16 [1024, 2048], P(None, 'tensor'), may hold values from -0.1875 to 0.1875
- ffn_up: bfloat16 [1024, 2048], P(None, 'tensor'), may hold values from -0.1875 to 0.1875
- ffn_down: bfloat16 [2048, 1024], P('tensor'), may hold values from -0.125 to 0.125
- cotangent: bfloat16 [32768, 1024], P('dp'), may hold values from -6 to 6
Outputs:
- layer_output: bfloat16 [32768, 1024], P('dp')
- input_grad: float32 [32768, 1024], P('dp')
- grad_input_gain: float32 [1024], replicated
- grad_mixer_proj: float32 [1024, 2, 1536], P(None, None, 'tensor')
- grad_state_proj: float32 [1024, 256], replicated
- grad_step_proj: float32 [1024, 24], P(None, 'tensor')
- grad_step_bias: float32 [24], P('tensor')
- grad_decay_log: float32 [24], P('tensor')
- grad_skip_gain: float32 [24], P('tensor')
- grad_conv_kernel: float32 [4, 1536], P(None, 'tensor')
- grad_conv_bias: float32 [1536], P('tensor')
- grad_state_kernel: float32 [4, 256], replicated
- grad_state_bias: float32 [256], replicated
- grad_gated_gain: float32 [1536], P('tensor')
- grad_mixer_out: float32 [1536, 1024], P('tensor')
- grad_query_proj: float32 [1024, 512], P(None, 'tensor')
- grad_keyval_proj: float32 [1024, 2, 128], P(None, 'tensor')
- grad_attn_out: float32 [512, 1024], P('tensor')
- grad_ffn_gain: float32 [1024], replicated
- grad_ffn_gate: float32 [1024, 2048], P(None, 'tensor')
- grad_ffn_up: float32 [1024, 2048], P(None, 'tensor')
- grad_ffn_down: float32 [2048, 1024], P('tensor')
Inputs may be any that keep to these rules, and one draw needn't show every extreme that they name: `segments`: along each row the numbers never fall; each number names one document of at most half of 512 tokens.
All inputs are finite; a program needn't handle non-finite values.
Results may differ from a plain program's by a relative error of at most 0.013.
Values sent between devices are 32-bit elements; how exact they have to be, the bound alone decides.
No kernel may reach another device: no remote copies, remote signals or barrier semaphores. Data moves between devices by JAX's collectives and lax.ppermute only.
A program may use at most 192 MiB of HBM per device.

v0:
```python
import jax
import jax.numpy as jnp
from jax import lax
from jax.sharding import PartitionSpec as P

HEAD_DIM = 64
DSSM = 1536


norm_eps = 1e-05
rope_base = 10000.0
masked_score = -1e30
highest = lax.Precision.HIGHEST


def silu_slope(argument):
    logistic = jax.nn.sigmoid(argument)
    return logistic * (1.0 + argument * (1.0 - logistic))


def rope_tables(document_length, head_size):
    half_size = head_size // 2
    inverse = rope_base ** (-(2.0 * jnp.arange(half_size, dtype=jnp.float32)) / head_size)
    angles = jnp.arange(document_length, dtype=jnp.float32)[:, None] * inverse[None, :]
    return (jnp.cos(angles)[:, None, :], jnp.sin(angles)[:, None, :])


def rotate(argument, cosine, sine):
    half_size = argument.shape[-1] // 2
    first_half = argument[..., :half_size]
    second_half = argument[..., half_size:]
    return jnp.concatenate(
        [first_half * cosine - second_half * sine, second_half * cosine + first_half * sine],
        axis=-1,
    )


def shift_down(values, offset):
    return jnp.concatenate(
        [jnp.zeros((offset, values.shape[1]), values.dtype), values[:-offset]], axis=0
    )


def shift_up(values, offset):
    return jnp.concatenate(
        [values[offset:], jnp.zeros((offset, values.shape[1]), values.dtype)], axis=0
    )


def lag_keep(segment, offset):
    previous = jnp.concatenate([jnp.full((offset,), -1, jnp.int32), segment[:-offset]])
    return (previous == segment).astype(jnp.float32)[:, None]


def conv_forward(values, kernel, conv_shift, segment):
    tap_count = kernel.shape[0]
    summed = conv_shift[None, :] + kernel[tap_count - 1][None, :] * values
    for offset in range(1, tap_count):
        summed = summed + kernel[tap_count - 1 - offset][None, :] * shift_down(
            values, offset
        ) * lag_keep(segment, offset)
    return summed


def conv_backward(grad_pre, values, kernel, segment):
    tap_count = kernel.shape[0]
    grad_values = kernel[tap_count - 1][None, :] * grad_pre
    kernel_rows = [jnp.sum(grad_pre * values, axis=0)]
    for offset in range(1, tap_count):
        masked = grad_pre * lag_keep(segment, offset)
        grad_values = grad_values + kernel[tap_count - 1 - offset][None, :] * shift_up(
            masked, offset
        )
        kernel_rows.append(jnp.sum(masked * shift_down(values, offset), axis=0))
    return (grad_values, jnp.stack(kernel_rows[::-1], axis=0), jnp.sum(grad_pre, axis=0))


def decay_weights(step_size, decay_rate, segment):
    document_length = step_size.shape[0]
    cumulative = jnp.cumsum(step_size * decay_rate[None, :], axis=0).T
    positions = jnp.arange(document_length)
    allowed = (positions[:, None] >= positions[None, :]) & (segment[:, None] == segment[None, :])
    spread = cumulative[:, :, None] - cumulative[:, None, :]
    return jnp.where(allowed[None], jnp.exp(jnp.where(allowed[None], spread, 0.0)), 0.0)


def norm_backward(grad_unit, unit_rows, inv_rms):
    return inv_rms * (
        grad_unit - unit_rows * jnp.mean(grad_unit * unit_rows, axis=-1, keepdims=True)
    )


def on_device(
    layer_input,
    segments,
    input_gain,
    mixer_proj,
    state_proj,
    step_proj,
    step_bias,
    decay_log,
    skip_gain,
    conv_kernel,
    conv_bias,
    state_kernel,
    state_bias,
    gated_gain,
    mixer_out,
    query_proj,
    key_value_weight,
    attn_out,
    ffn_gain,
    ffn_gate,
    ffn_up,
    ffn_down,
    cotangent,
):
    segment = segments.reshape(-1)
    tokens = layer_input.astype(jnp.float32)
    document_length = tokens.shape[0]
    model_width = tokens.shape[1]
    width = mixer_proj.shape[2]
    heads = step_proj.shape[1]
    head_size = width // heads
    state_size = state_proj.shape[1] // 2
    kv_heads = key_value_weight.shape[1]
    query_heads = query_proj.shape[1] // HEAD_DIM
    group_width = query_heads // kv_heads
    score_scale = HEAD_DIM ** (-0.5)
    mixer_flat = mixer_proj.reshape(model_width, 2 * width)
    keyval_flat = key_value_weight.reshape(model_width, kv_heads * 2 * HEAD_DIM)
    inv_rms_in = lax.rsqrt(jnp.mean(tokens * tokens, axis=-1, keepdims=True) + norm_eps)
    unit_in = tokens * inv_rms_in
    normed_input = (unit_in * input_gain).astype(jnp.bfloat16)
    gate_input = jnp.dot(normed_input, mixer_flat, preferred_element_type=jnp.float32)
    gate_branch = gate_input[:, :width]
    conv_in = gate_input[:, width:]
    state_in = jnp.dot(normed_input, state_proj, preferred_element_type=jnp.float32)
    step_raw = jnp.dot(normed_input, step_proj, preferred_element_type=jnp.float32)
    conv_pre = conv_forward(conv_in, conv_kernel, conv_bias, segment)
    conv_out = jax.nn.silu(conv_pre)
    state_pre = conv_forward(state_in, state_kernel, state_bias, segment)
    state_conv = jax.nn.silu(state_pre)
    in_state = state_conv[:, :state_size]
    out_state = state_conv[:, state_size:]
    step_arg = step_raw + step_bias
    step_size = jax.nn.softplus(step_arg)
    decay_rate = -jnp.exp(decay_log)
    heads_in = conv_out.reshape(document_length, heads, head_size)
    decay_mat = decay_weights(step_size, decay_rate, segment)
    intersection = jnp.dot(out_state, in_state.T, precision=highest)
    mixing = decay_mat * intersection[None]
    scaled_in = heads_in * step_size[:, :, None]
    scan_heads = jnp.einsum("hts,shd->thd", mixing, scaled_in, precision=highest)
    scan_out = (scan_heads + skip_gain[None, :, None] * heads_in).reshape(document_length, width)
    gate_act = jax.nn.silu(gate_branch)
    gated = scan_out * gate_act
    squares = lax.psum(jnp.sum(gated * gated, axis=-1, keepdims=True), "tensor")
    inv_rms_gated = lax.rsqrt(squares / DSSM + norm_eps)
    unit_gated = gated * inv_rms_gated
    mixer_rows = (unit_gated * gated_gain).astype(jnp.bfloat16)
    cosine, sine = rope_tables(document_length, HEAD_DIM)
    query_raw = jnp.dot(normed_input, query_proj, preferred_element_type=jnp.float32).reshape(
        document_length, query_heads, HEAD_DIM
    )
    pair_rows = jnp.dot(normed_input, keyval_flat, preferred_element_type=jnp.float32).reshape(
        document_length, kv_heads, 2, HEAD_DIM
    )
    query_matrix = (
        rotate(query_raw, cosine, sine)
        .astype(jnp.bfloat16)
        .reshape(document_length, kv_heads, group_width, HEAD_DIM)
    )
    key_rows = rotate(pair_rows[:, :, 0], cosine, sine).astype(jnp.bfloat16)
    value_rows = pair_rows[:, :, 1].astype(jnp.bfloat16)
    positions = jnp.arange(document_length)
    allowed = ((positions[:, None] >= positions[None, :]) & (segment[:, None] == segment[None, :]))[
        None, None
    ]
    scores = jnp.where(
        allowed,
        jnp.einsum("tkgd,skd->kgts", query_matrix, key_rows, preferred_element_type=jnp.float32)
        * score_scale,
        masked_score,
    )
    row_max = jnp.max(scores, axis=-1, keepdims=True)
    log_total = row_max + jnp.log(jnp.sum(jnp.exp(scores - row_max), axis=-1, keepdims=True))
    prob_rows = jnp.exp(scores - log_total).astype(jnp.bfloat16)
    attended = jnp.einsum(
        "kgts,skd->tkgd", prob_rows, value_rows, preferred_element_type=jnp.float32
    )
    attended = attended.reshape(document_length, query_heads * HEAD_DIM).astype(jnp.bfloat16)
    partial_branch = jnp.dot(mixer_rows, mixer_out, preferred_element_type=jnp.float32) + jnp.dot(
        attended, attn_out, preferred_element_type=jnp.float32
    )
    branch = lax.psum(partial_branch, "tensor")
    hidden = tokens + branch
    inv_rms_ffn = lax.rsqrt(jnp.mean(hidden * hidden, axis=-1, keepdims=True) + norm_eps)
    unit_ffn = hidden * inv_rms_ffn
    normed_ffn = (unit_ffn * ffn_gain).astype(jnp.bfloat16)
    gate_rows = jnp.dot(normed_ffn, ffn_gate, preferred_element_type=jnp.float32)
    up_rows = jnp.dot(normed_ffn, ffn_up, preferred_element_type=jnp.float32)
    gate_silu = jax.nn.silu(gate_rows)
    activated = (gate_silu * up_rows).astype(jnp.bfloat16)
    down_rows = lax.psum(jnp.dot(activated, ffn_down, preferred_element_type=jnp.float32), "tensor")
    layer_output = (hidden + down_rows).astype(jnp.bfloat16)
    grad_out = cotangent.astype(jnp.float32)
    grad_ffn_down = jnp.dot(activated.T, cotangent, preferred_element_type=jnp.float32)
    grad_activated = jnp.dot(cotangent, ffn_down.T, preferred_element_type=jnp.float32)
    grad_gate_rows = (grad_activated * up_rows * silu_slope(gate_rows)).astype(jnp.bfloat16)
    grad_up_rows = (grad_activated * gate_silu).astype(jnp.bfloat16)
    grad_ffn_gate = jnp.dot(normed_ffn.T, grad_gate_rows, preferred_element_type=jnp.float32)
    grad_ffn_up = jnp.dot(normed_ffn.T, grad_up_rows, preferred_element_type=jnp.float32)
    partial_ffn = jnp.dot(grad_gate_rows, ffn_gate.T, preferred_element_type=jnp.float32) + jnp.dot(
        grad_up_rows, ffn_up.T, preferred_element_type=jnp.float32
    )
    grad_normed_ffn = lax.psum(partial_ffn, "tensor")
    grad_ffn_gain = jnp.sum(grad_normed_ffn * unit_ffn, axis=0)
    grad_hidden = grad_out + norm_backward(grad_normed_ffn * ffn_gain, unit_ffn, inv_rms_ffn)
    grad_branch = grad_hidden.astype(jnp.bfloat16)
    grad_mixer_out = jnp.dot(mixer_rows.T, grad_branch, preferred_element_type=jnp.float32)
    grad_attn_out = jnp.dot(attended.T, grad_branch, preferred_element_type=jnp.float32)
    grad_mixer_rows = jnp.dot(grad_branch, mixer_out.T, preferred_element_type=jnp.float32)
    grad_attended = jnp.dot(grad_branch, attn_out.T, preferred_element_type=jnp.float32).astype(
        jnp.bfloat16
    )
    grad_attended = grad_attended.reshape(document_length, kv_heads, group_width, HEAD_DIM)
    scores_again = jnp.where(
        allowed,
        jnp.einsum("tkgd,skd->kgts", query_matrix, key_rows, preferred_element_type=jnp.float32)
        * score_scale,
        masked_score,
    )
    probs = jnp.exp(scores_again - log_total)
    grad_probs = jnp.einsum(
        "tkgd,skd->kgts", grad_attended, value_rows, preferred_element_type=jnp.float32
    )
    grad_values = jnp.einsum(
        "kgts,tkgd->skd",
        probs.astype(jnp.bfloat16),
        grad_attended,
        preferred_element_type=jnp.float32,
    )
    row_dot = jnp.sum(probs * grad_probs, axis=-1, keepdims=True)
    grad_scores = (probs * (grad_probs - row_dot)).astype(jnp.bfloat16)
    grad_queries = (
        jnp.einsum("kgts,skd->tkgd", grad_scores, key_rows, preferred_element_type=jnp.float32)
        * score_scale
    )
    grad_keys = (
        jnp.einsum("kgts,tkgd->skd", grad_scores, query_matrix, preferred_element_type=jnp.float32)
        * score_scale
    )
    grad_queries = rotate(
        grad_queries.reshape(document_length, query_heads, HEAD_DIM), cosine, -sine
    )
    grad_queries = grad_queries.astype(jnp.bfloat16).reshape(
        document_length, query_heads * HEAD_DIM
    )
    grad_pairs = jnp.stack([rotate(grad_keys, cosine, -sine), grad_values], axis=2)
    grad_pairs = grad_pairs.astype(jnp.bfloat16).reshape(document_length, kv_heads * 2 * HEAD_DIM)
    grad_query_proj = jnp.dot(normed_input.T, grad_queries, preferred_element_type=jnp.float32)
    grad_keyval_proj = jnp.dot(
        normed_input.T, grad_pairs, preferred_element_type=jnp.float32
    ).reshape(key_value_weight.shape)
    grad_gated_gain = jnp.sum(grad_mixer_rows * unit_gated, axis=0)
    grad_unit_gated = grad_mixer_rows * gated_gain
    gated_dot = lax.psum(jnp.sum(grad_unit_gated * unit_gated, axis=-1, keepdims=True), "tensor")
    grad_gated = inv_rms_gated * (grad_unit_gated - unit_gated * gated_dot / DSSM)
    grad_scan = (grad_gated * gate_act).reshape(document_length, heads, head_size)
    grad_gate_branch = grad_gated * scan_out * silu_slope(gate_branch)
    grad_mix = jnp.einsum("thd,shd->hts", grad_scan, scaled_in, precision=highest)
    grad_scaled = jnp.einsum("hts,thd->shd", mixing, grad_scan, precision=highest)
    grad_skip_gain = jnp.sum(grad_scan * heads_in, axis=(0, 2))
    grad_heads = grad_scaled * step_size[:, :, None] + grad_scan * skip_gain[None, :, None]
    grad_intersection = jnp.sum(grad_mix * decay_mat, axis=0)
    decay_flow = grad_mix * mixing
    grad_cumulative = (jnp.sum(decay_flow, axis=2) - jnp.sum(decay_flow, axis=1)).T
    grad_log = jnp.cumsum(grad_cumulative[::-1], axis=0)[::-1]
    grad_step = jnp.sum(grad_scaled * heads_in, axis=-1) + grad_log * decay_rate[None, :]
    grad_decay_log = jnp.sum(grad_log * step_size, axis=0) * decay_rate
    grad_out_state = jnp.dot(grad_intersection, in_state, precision=highest)
    grad_in_state = jnp.dot(grad_intersection.T, out_state, precision=highest)
    grad_state = lax.psum(jnp.concatenate([grad_in_state, grad_out_state], axis=1), "tensor")
    grad_state_in, grad_state_kernel, grad_state_bias = conv_backward(
        grad_state * silu_slope(state_pre), state_in, state_kernel, segment
    )
    grad_state_rows = grad_state_in.astype(jnp.bfloat16)
    grad_state_proj = jnp.dot(normed_input.T, grad_state_rows, preferred_element_type=jnp.float32)
    grad_step_arg = grad_step * jax.nn.sigmoid(step_arg)
    grad_step_bias = jnp.sum(grad_step_arg, axis=0)
    grad_step_rows = grad_step_arg.astype(jnp.bfloat16)
    grad_step_proj = jnp.dot(normed_input.T, grad_step_rows, preferred_element_type=jnp.float32)
    grad_conv_in, grad_conv_kernel, grad_conv_bias = conv_backward(
        grad_heads.reshape(document_length, width) * silu_slope(conv_pre),
        conv_in,
        conv_kernel,
        segment,
    )
    grad_gate_input = jnp.concatenate([grad_gate_branch, grad_conv_in], axis=1).astype(jnp.bfloat16)
    grad_mixer_proj = jnp.dot(
        normed_input.T, grad_gate_input, preferred_element_type=jnp.float32
    ).reshape(mixer_proj.shape)
    partial_normed = jnp.dot(grad_gate_input, mixer_flat.T, preferred_element_type=jnp.float32)
    partial_normed = partial_normed + jnp.dot(
        grad_step_rows, step_proj.T, preferred_element_type=jnp.float32
    )
    partial_normed = partial_normed + jnp.dot(
        grad_queries, query_proj.T, preferred_element_type=jnp.float32
    )
    partial_normed = partial_normed + jnp.dot(
        grad_pairs, keyval_flat.T, preferred_element_type=jnp.float32
    )
    grad_normed = lax.psum(partial_normed, "tensor")
    grad_normed = grad_normed + jnp.dot(
        grad_state_rows, state_proj.T, preferred_element_type=jnp.float32
    )
    grad_input_gain = jnp.sum(grad_normed * unit_in, axis=0)
    input_grad = grad_hidden + norm_backward(grad_normed * input_gain, unit_in, inv_rms_in)
    summed = lax.psum(
        (
            grad_input_gain,
            grad_mixer_proj,
            grad_state_proj,
            grad_step_proj,
            grad_step_bias,
            grad_decay_log,
            grad_skip_gain,
            grad_conv_kernel,
            grad_conv_bias,
            grad_state_kernel,
            grad_state_bias,
            grad_gated_gain,
            grad_mixer_out,
            grad_query_proj,
            grad_keyval_proj,
            grad_attn_out,
            grad_ffn_gain,
            grad_ffn_gate,
            grad_ffn_up,
            grad_ffn_down,
        ),
        "dp",
    )
    return (
        layer_output,
        input_grad,
        summed[0],
        summed[1],
        summed[2],
        summed[3],
        summed[4],
        summed[5],
        summed[6],
        summed[7],
        summed[8],
        summed[9],
        summed[10],
        summed[11],
        summed[12],
        summed[13],
        summed[14],
        summed[15],
        summed[16],
        summed[17],
        summed[18],
        summed[19],
    )


def solution(mesh):
    in_specs = (
        P("dp", None),
        P("dp", None),
        P(),
        P(None, None, "tensor"),
        P(),
        P(None, "tensor"),
        P("tensor"),
        P("tensor"),
        P("tensor"),
        P(None, "tensor"),
        P("tensor"),
        P(),
        P(),
        P("tensor"),
        P("tensor", None),
        P(None, "tensor"),
        P(None, "tensor", None),
        P("tensor", None),
        P(),
        P(None, "tensor"),
        P(None, "tensor"),
        P("tensor", None),
        P("dp", None),
    )
    out_specs = (
        P("dp", None),
        P("dp", None),
        P(),
        P(None, None, "tensor"),
        P(),
        P(None, "tensor"),
        P("tensor"),
        P("tensor"),
        P("tensor"),
        P(None, "tensor"),
        P("tensor"),
        P(),
        P(),
        P("tensor"),
        P("tensor", None),
        P(None, "tensor"),
        P(None, "tensor", None),
        P("tensor", None),
        P(),
        P(None, "tensor"),
        P(None, "tensor"),
        P("tensor", None),
    )
    return jax.shard_map(
        on_device, mesh=mesh, in_specs=in_specs, out_specs=out_specs, check_vma=False
    )
```

profile of v0, /device:TPU:1, one launch (start us, length us, event | category | flops | bytes accessed | tf_op | source)
XLA Modules:
  0.0 1797.2 jit_solution(5187822099085839022)
XLA Ops:
  9.0 2.6 copy.106
  11.6 1.9 fusion.118
  28.1 2.0 fusion.115
  32.9 2.0 fusion.61
  35.0 2.9 fusion.40
  37.9 3.1 copy.82
  41.0 17.9 bitcast_add_fusion
  58.9 3.0 copy.86
  61.9 3.5 multiply_reduce_fusion.11
  65.5 4.8 psum.189
  80.0 73.1 %all-reduce.23.cloned.1.call-done = f32[512,1024]{1,0:T(8,128)} async-done(((f32[512,1024]{1,0:T(8,128)}), f32[512,1024]{1,0:T(8,128)}) %all-reduce.23.cloned.1.call-update) | async-done | bytes 2097168 | tf_op jit(solution)/shard_map/psum | solution.py:196
  153.1 2.2 multiply_reduce_fusion.3
  155.6 2.1 copy-done.150
  160.9 3.0 multiply_convert_fusion
  165.2 2.6 convolution_add_fusion.2
  168.1 3.8 fusion.128
  171.9 66.8 %all-reduce.25.cloned.1.call-done = f32[512,1024]{1,0:T(8,128)} async-done(((f32[512,1024]{1,0:T(8,128)}), f32[512,1024]{1,0:T(8,128)}) %all-reduce.25.cloned.1.call-update) | async-done | bytes 2097168 | tf_op jit(solution)/shard_map/psum | solution.py:217
  238.7 3.6 multiply_reduce_fusion.1
  242.3 2.0 fusion.104
  245.6 2.9 multiply_reduce_fusion.4
  248.4 4.5 psum.193
  252.9 5.6 multiply_reduce_fusion.9
  258.4 3.0 copy.90
  261.5 18.5 %fusion.6 = (f32[12,512]{1,0:T(8,128)}, f32[12,512]{1,0:T(8,128)}, f32[512,512]{1,0:T(8,128)S(1)}) fusion(f32[512,512]{1,0:T(8,128)} %fusion.61, f32[12,512]{1,0:T(8,128)} %bitcast.265, pred[512,512]{1,0:T(8,128)(4,1)} %copy.83, f32[512,12,64]{0,2,1:T(8,128)} %bitcast.237, f32[512,12,64]{0,2,1:T(8,128)} %bitcast.234, f32[512,12]{0,1:T(8,128)} %compare_select_fusion.1), kind=kOutput, calls=%fused_computation.6 | convolution fusion | flops 2444349440 | bytes 5603328 | tf_op jit(solution)/shard_map/thd,shd->hts/dot_general | solution.py:272
  280.1 13.1 fusion.38
  294.9 2.9 fusion.63
  297.8 1.8 convolution_bitcast_fusion.2
  303.7 3.0 copy.91
  306.8 5.0 multiply_reduce_fusion.8
  311.8 3.0 fusion.120
  328.2 1.8 add_add_fusion
  330.3 5.0 fusion.133
  335.3 3.3 fusion.132
  338.7 3.5 fusion.131
  343.0 6.3 fusion.51
  349.3 8.3 reshape.530
  358.3 2.7 convolution_bitcast_fusion
  365.7 2.8 fusion.102
  368.4 90.5 %all-reduce.31.cloned.1.call-done = (f32[512,1024]{1,0:T(8,128)}, f32[512,1024]{1,0:T(8,128)}, f32[512,256]{1,0:T(8,128)}) async-done(((f32[512,1024]{1,0:T(8,128)}, f32[512,1024]{1,0:T(8,128)}, f32[512,256]{1,0:T(8,128)}), (f32[512,1024]{1,0:T(8,128)}, f32[512,1024]{1,0:T(8,128)}, f32[512,256]{1,0:T(8,128)})) %all-reduce.31.cloned.1.call-update) | async-done | bytes 4718608 | tf_op jit(solution)/shard_map/psum | solution.py:205
  463.3 2.7 fusion.32
  466.9 2.8 fusion.109
  470.4 5.2 fusion.31
  475.5 564.5 %all-reduce.27.cloned.1.call-done = (f32[1024]{0:T(1024)}, f32[1024,12]{0,1:T(8,128)}, f32[12]{0:T(128)}, f32[12]{0:T(128)}, f32[12]{0:T(128)}, /*index=5*/f32[4...) async-done(((f32[1024]{0:T(1024)}, f32[1024,12]{0,1:T(8,128)}, f32[12]{0:T(128)}, f32[12]{0:T(128)}, ...) | async-done | bytes 81056 | tf_op jit(solution)/shard_map/psum | solution.py:320
  1040.0 719.4 %all-reduce.29.cloned.1.call-done = (f32[1024,2,768]{2,1,0:T(2,128)}, f32[1024,256]{1,0:T(8,128)}, f32[768,1024]{1,0:T(8,128)}, f32[1024,256]{1,0:T(8,128)}, f32...) async-done(((f32[1024,2,768]{2,1,0:T(2,128)}, f32[1024,256]{1,0:T(8,128)}, ...) | async-done | bytes 25690128 | tf_op jit(solution)/shard_map/psum | solution.py:320
  1760.7 7.8 copy.135
  1779.9 2.1 copy.151
  1783.6 2.1 copy.152
  1787.3 2.1 copy.153
  (440 shorter events, 82.4 us)
Async XLA Ops:
  7.2 153.7 %copy-start = (bf16[1024,1024]{1,0:T(8,128)(2,1)S(1)}, bf16[1024,1024]{1,0:T(8,128)(2,1)}, u32[]{:S(2)}) copy-start(bf16[1024,1024]{1,0:T(8,128)(2,1)} %param.44) | copy-start | bytes 6291460
  7.2 145.9 %all-reduce.23.cloned.1.call-start = ((), (), s32[]{:S(2)}) async-start(), calls=%async_computation | async-start | bytes 4194304 | tf_op jit(solution)/shard_map/psum | solution.py:196
  7.3 19.2 %copy-start.136 = (f32[32]{0:T(128)}, f32[32]{0:T(128)S(1)}, u32[]{:S(2)}) copy-start(f32[32]{0:T(128)S(1)} %multiply_power_fusion) | copy-start | bytes 388
  8.9 15.7 copy-start.113
  17.5 5.8 copy-start.79
  17.5 7.0 copy-start.45
  18.7 16.2 copy-start.98
  18.7 16.2 copy-start.100
  18.7 16.2 copy-start.102
  19.2 5.4 copy-start.77
  28.1 6.8 copy-start.23
  30.1 4.8 copy-start.21
  70.2 6.2 copy-start.92
  79.9 75.5 %copy-start.80 = (f32[1024]{0:T(1024)S(1)}, f32[1024]{0:T(1024)}, u32[]{:S(2)}) copy-start(f32[1024]{0:T(1024)} %param.41) | copy-start | bytes 12292
  79.9 158.7 %all-reduce.25.cloned.1.call-start = ((), (), s32[]{:S(2)}) async-start(), calls=%async_computation.1 | async-start | bytes 4194304 | tf_op jit(solution)/shard_map/psum | solution.py:217
  167.9 291.1 %all-reduce.31.cloned.1.call-start = ((), (), s32[]{:S(2)}) async-start(), calls=%async_computation.4 | async-start | bytes 9437184 | tf_op jit(solution)/shard_map/psum | solution.py:205
  171.9 70.3 %copy-start.3 = (f32[512,1024]{1,0:T(8,128)S(1)}, f32[512,1024]{1,0:T(8,128)}, u32[]{:S(2)}) copy-start(f32[512,1024]{1,0:T(8,128)} %copy-done.2) | copy-start | bytes 6291460
  261.5 18.6 %copy-start.39 = (f32[512,768]{0,1:T(8,128)S(1)}, f32[512,768]{0,1:T(8,128)}, u32[]{:S(2)}) copy-start(f32[512,768]{0,1:T(8,128)} %copy.82) | copy-start | bytes 4718596
  261.5 18.6 %copy-start.40 = (f32[512,768]{0,1:T(8,128)S(1)}, f32[512,768]{0,1:T(8,128)}, u32[]{:S(2)}) copy-start(f32[512,768]{0,1:T(8,128)} %copy.90) | copy-start | bytes 4718596
  261.5 18.6 %copy-start.47 = (f32[512,512]{1,0:T(8,128)S(1)}, f32[512,512]{1,0:T(8,128)}, u32[]{:S(2)}) copy-start(f32[512,512]{1,0:T(8,128)} %fusion.61) | copy-start | bytes 3145732
  261.5 18.6 %copy-start.73 = (pred[512,512]{1,0:T(8,128)(4,1)S(1)}, pred[512,512]{1,0:T(8,128)(4,1)}, u32[]{:S(2)}) copy-start(pred[512,512]{1,0:T(8,128)(4,1)} %copy.83) | copy-start | bytes 786436
  261.5 18.6 %copy-start.111 = (f32[2,8,4,128]{3,1,2,0:T(8,128)S(1)}, f32[2,8,4,128]{3,1,2,0:T(8,128)}, u32[]{:S(2)}) copy-start(f32[2,8,4,128]{3,1,2,0:T(8,128)} %copy.107) | copy-start | bytes 98308
  261.5 18.6 %copy-start.112 = (f32[512,12]{0,1:T(8,128)S(1)}, f32[512,12]{0,1:T(8,128)}, u32[]{:S(2)}) copy-start(f32[512,12]{0,1:T(8,128)} %compare_select_fusion.1) | copy-start | bytes 73732
  261.5 18.6 %copy-start.153 = (f32[12]{0:T(128)S(1)}, f32[12]{0:T(128)}, u32[]{:S(2)}) copy-start(f32[12]{0:T(128)} %param.31) | copy-start | bytes 148
  280.1 17.8 copy-start.8
  293.2 4.6 copy-start.72
  306.8 5.0 copy-start.6
  306.8 5.0 copy-start.20
  306.8 5.0 copy-start.22
  306.8 5.0 copy-start.86
  306.8 5.0 copy-start.88
  330.1 709.9 %all-reduce.27.cloned.1.call-start = ((), (), s32[]{:S(2)}) async-start(), calls=%async_computation.2 | async-start | bytes 201728 | tf_op jit(solution)/shard_map/psum | solution.py:320
  330.3 5.0 copy-start.25
  330.3 5.0 copy-start.56
  338.7 4.3 copy-start.115
  349.3 11.7 copy-start.148
  349.3 11.7 copy-start.155
  349.3 12.2 copy-start.82
  357.7 5.0 copy-start.27
  357.7 5.0 copy-start.44
  365.7 93.3 %copy-start.38 = (f32[512,256]{1,0:T(8,128)S(1)}, f32[512,256]{1,0:T(8,128)}, u32[]{:S(2)}) copy-start(f32[512,256]{1,0:T(8,128)} %get-tuple-element.151) | copy-start | bytes 1572868
  365.7 93.3 %copy-start.97 = (f32[512]{0:T(512)S(1)}, f32[512]{0:T(512)}, u32[]{:S(2)}) copy-start(f32[512]{0:T(512)} %copy-done.95) | copy-start | bytes 6148
  466.6 1292.8 %all-reduce.29.cloned.1.call-start = ((), (), s32[]{:S(2)}) async-start(), calls=%async_computation.3 | async-start | bytes 51380224 | tf_op jit(solution)/shard_map/psum | solution.py:320
  1760.7 7.8 copy-start.50
  1760.7 14.0 copy-start.36
  1768.5 4.4 copy-start.142
  1768.5 5.0 copy-start.145
  1768.5 5.5 copy-start.141
  (116 other events, 284.0 us)
Sparse Core Ops, SparseCore 0:
  80.0 73.0 all-reduce.22
  168.0 70.6 all-reduce.24
  330.2 128.7 all-reduce.30
  466.7 573.2 all-reduce.26
  1044.8 714.5 all-reduce.28
where the time goes:
time: 1800 us
  waiting for transfers between devices  1510 us (84%)
  matrix products  129 us (7%)
  local copies, waits for them, and re-layouts  75.8 us (4%)
  other arithmetic  52.3 us (3%)
    psum x2, waiting for transfers between devices, on_device(): lax.psum((grad_input_gain, grad_mixer_proj, grad_state_proj, grad_step_pr...  1280 us
    psum x1, waiting for transfers between devices, on_device(): lax.psum(jnp.dot(activated, ffn_down, preferred_element_type=jnp.float32)...  90.5 us
    psum x1, waiting for transfers between devices, on_device(): branch = lax.psum(partial_branch, 'tensor')  73.1 us
    psum x1, waiting for transfers between devices, on_device(): grad_normed_ffn = lax.psum(partial_ffn, 'tensor')  66.8 us
    unnamed x344, local copies, waits for them, and re-layouts  46.1 us
  transfers between devices with their start and end apart: 5, of which 5 were waited for; matrix products, arithmetic and copies ran while one was open for 3% of the time, Pallas kernels for 0%

commit v1 on v0

--- a/solution.py
+++ b/solution.py
@@ -5,6 +5,12 @@
 
 HEAD_DIM = 64
 DSSM = 1536
+DP = ("y", "zh", "x", "core")
+PAIR = [(0, 1), (1, 0)]
+LINKS = {
+    "A": [(0, 1), (1, 0), (2, 3), (3, 2)],
+    "B": [(1, 2), (2, 1), (3, 0), (0, 3)],
+}
 
 
 norm_eps = 1e-05
@@ -88,6 +94,78 @@
     return inv_rms * (
         grad_unit - unit_rows * jnp.mean(grad_unit * unit_rows, axis=-1, keepdims=True)
     )
+
+
+def exchange(values, name):
+    return values + lax.ppermute(values, name, PAIR)
+
+
+def take(values, index, axis):
+    return lax.dynamic_slice_in_dim(values, index, 1, axis)
+
+
+def first_halving(values, name, axis, link):
+    place = lax.axis_index(name)
+    if link == "A":
+        side = ((place + 1) // 2) % 2
+        kept = jnp.concatenate([take(values, side, axis), take(values, 3 - side, axis)], axis)
+        sent = jnp.concatenate([take(values, 1 - side, axis), take(values, 2 + side, axis)], axis)
+    else:
+        side = place // 2
+        kept = lax.dynamic_slice_in_dim(values, 2 * side, 2, axis)
+        sent = lax.dynamic_slice_in_dim(values, 2 - 2 * side, 2, axis)
+    return kept + lax.ppermute(sent, name, LINKS[link])
+
+
+def second_halving(values, name, axis, link):
+    place = lax.axis_index(name)
+    index = place // 2 if link == "B" else place % 2
+    sent = take(values, 1 - index, axis)
+    return take(values, index, axis) + lax.ppermute(sent, name, LINKS[link])
+
+
+def reduce_blocks(values):
+    count, rows, columns = values.shape
+    blocks = values.reshape(count, 4, 2, 4, rows // 32, columns)
+    tiles = columns // 128
+    sizes = [128 * (tiles // 4 + (1 if k < tiles % 4 else 0)) for k in range(4)]
+    orders = [
+        (("x", "A"), ("x", "B"), ("y", "A"), ("y", "B")),
+        (("x", "B"), ("y", "A"), ("y", "B"), ("x", "A")),
+        (("y", "A"), ("y", "B"), ("x", "A"), ("x", "B")),
+        (("y", "B"), ("x", "A"), ("x", "B"), ("y", "A")),
+    ]
+    parts, start = [], 0
+    for size in sizes:
+        parts.append(blocks[..., start : start + size])
+        start += size
+    seen = [set() for _ in range(4)]
+    for step in range(4):
+        for k in range(4):
+            name, link = orders[k][step]
+            axis = {"y": 1, "x": 3}[name]
+            halving = second_halving if name in seen[k] else first_halving
+            parts[k] = halving(parts[k], name, axis, link)
+            seen[k].add(name)
+    merged = jnp.concatenate(parts, axis=-1)
+    place = lax.axis_index("zh")
+    own = take(merged, place, 2) + lax.ppermute(take(merged, 1 - place, 2), "zh", PAIR)
+    return own.reshape(count, rows // 32, columns)
+
+
+def core_halves(left, right):
+    place = lax.axis_index("core")
+    half = left.shape[2] // 2
+
+    def rows_of(index):
+        part = lax.dynamic_slice_in_dim(left, index * half, half, 2)
+        return jnp.einsum("btm,btn->bmn", part, right, preferred_element_type=jnp.float32)
+
+    return rows_of(place) + lax.ppermute(rows_of(1 - place), "core", PAIR)
+
+
+def gather_blocks(values):
+    return lax.all_gather(values, ("core", "y", "zh", "x"), axis=1, tiled=True)
 
 
 def on_device(
@@ -155,7 +233,7 @@
     scan_out = (scan_heads + skip_gain[None, :, None] * heads_in).reshape(document_length, width)
     gate_act = jax.nn.silu(gate_branch)
     gated = scan_out * gate_act
-    squares = lax.psum(jnp.sum(gated * gated, axis=-1, keepdims=True), "tensor")
+    squares = exchange(jnp.sum(gated * gated, axis=-1, keepdims=True), "tensor")
     inv_rms_gated = lax.rsqrt(squares / DSSM + norm_eps)
     unit_gated = gated * inv_rms_gated
     mixer_rows = (unit_gated * gated_gain).astype(jnp.bfloat16)
@@ -193,7 +271,7 @@
     partial_branch = jnp.dot(mixer_rows, mixer_out, preferred_element_type=jnp.float32) + jnp.dot(
         attended, attn_out, preferred_element_type=jnp.float32
     )
-    branch = lax.psum(partial_branch, "tensor")
+    branch = exchange(partial_branch, "tensor")
     hidden = tokens + branch
     inv_rms_ffn = lax.rsqrt(jnp.mean(hidden * hidden, axis=-1, keepdims=True) + norm_eps)
     unit_ffn = hidden * inv_rms_ffn
@@ -202,24 +280,19 @@
     up_rows = jnp.dot(normed_ffn, ffn_up, preferred_element_type=jnp.float32)
     gate_silu = jax.nn.silu(gate_rows)
     activated = (gate_silu * up_rows).astype(jnp.bfloat16)
-    down_rows = lax.psum(jnp.dot(activated, ffn_down, preferred_element_type=jnp.float32), "tensor")
+    down_rows = exchange(jnp.dot(activated, ffn_down, preferred_element_type=jnp.float32), "tensor")
     layer_output = (hidden + down_rows).astype(jnp.bfloat16)
     grad_out = cotangent.astype(jnp.float32)
-    grad_ffn_down = jnp.dot(activated.T, cotangent, preferred_element_type=jnp.float32)
     grad_activated = jnp.dot(cotangent, ffn_down.T, preferred_element_type=jnp.float32)
     grad_gate_rows = (grad_activated * up_rows * silu_slope(gate_rows)).astype(jnp.bfloat16)
     grad_up_rows = (grad_activated * gate_silu).astype(jnp.bfloat16)
-    grad_ffn_gate = jnp.dot(normed_ffn.T, grad_gate_rows, preferred_element_type=jnp.float32)
-    grad_ffn_up = jnp.dot(normed_ffn.T, grad_up_rows, preferred_element_type=jnp.float32)
     partial_ffn = jnp.dot(grad_gate_rows, ffn_gate.T, preferred_element_type=jnp.float32) + jnp.dot(
         grad_up_rows, ffn_up.T, preferred_element_type=jnp.float32
     )
-    grad_normed_ffn = lax.psum(partial_ffn, "tensor")
+    grad_normed_ffn = exchange(partial_ffn, "tensor")
     grad_ffn_gain = jnp.sum(grad_normed_ffn * unit_ffn, axis=0)
     grad_hidden = grad_out + norm_backward(grad_normed_ffn * ffn_gain, unit_ffn, inv_rms_ffn)
     grad_branch = grad_hidden.astype(jnp.bfloat16)
-    grad_mixer_out = jnp.dot(mixer_rows.T, grad_branch, preferred_element_type=jnp.float32)
-    grad_attn_out = jnp.dot(attended.T, grad_branch, preferred_element_type=jnp.float32)
     grad_mixer_rows = jnp.dot(grad_branch, mixer_out.T, preferred_element_type=jnp.float32)
     grad_attended = jnp.dot(grad_branch, attn_out.T, preferred_element_type=jnp.float32).astype(
         jnp.bfloat16
@@ -259,13 +332,9 @@
     )
     grad_pairs = jnp.stack([rotate(grad_keys, cosine, -sine), grad_values], axis=2)
     grad_pairs = grad_pairs.astype(jnp.bfloat16).reshape(document_length, kv_heads * 2 * HEAD_DIM)
-    grad_query_proj = jnp.dot(normed_input.T, grad_queries, preferred_element_type=jnp.float32)
-    grad_keyval_proj = jnp.dot(
-        normed_input.T, grad_pairs, preferred_element_type=jnp.float32
-    ).reshape(key_value_weight.shape)
     grad_gated_gain = jnp.sum(grad_mixer_rows * unit_gated, axis=0)
     grad_unit_gated = grad_mixer_rows * gated_gain
-    gated_dot = lax.psum(jnp.sum(grad_unit_gated * unit_gated, axis=-1, keepdims=True), "tensor")
+    gated_dot = exchange(jnp.sum(grad_unit_gated * unit_gated, axis=-1, keepdims=True), "tensor")
     grad_gated = inv_rms_gated * (grad_unit_gated - unit_gated * gated_dot / DSSM)
     grad_scan = (grad_gated * gate_act).reshape(document_length, heads, head_size)
     grad_gate_branch = grad_gated * scan_out * silu_slope(gate_branch)
@@ -281,16 +350,14 @@
     grad_decay_log = jnp.sum(grad_log * step_size, axis=0) * decay_rate
     grad_out_state = jnp.dot(grad_intersection, in_state, precision=highest)
     grad_in_state = jnp.dot(grad_intersection.T, out_state, precision=highest)
-    grad_state = lax.psum(jnp.concatenate([grad_in_state, grad_out_state], axis=1), "tensor")
+    grad_state = exchange(jnp.concatenate([grad_in_state, grad_out_state], axis=1), "tensor")
     grad_state_in, grad_state_kernel, grad_state_bias = conv_backward(
         grad_state * silu_slope(state_pre), state_in, state_kernel, segment
     )
     grad_state_rows = grad_state_in.astype(jnp.bfloat16)
-    grad_state_proj = jnp.dot(normed_input.T, grad_state_rows, preferred_element_type=jnp.float32)
     grad_step_arg = grad_step * jax.nn.sigmoid(step_arg)
     grad_step_bias = jnp.sum(grad_step_arg, axis=0)
     grad_step_rows = grad_step_arg.astype(jnp.bfloat16)
-    grad_step_proj = jnp.dot(normed_input.T, grad_step_rows, preferred_element_type=jnp.float32)
     grad_conv_in, grad_conv_kernel, grad_conv_bias = conv_backward(
         grad_heads.reshape(document_length, width) * silu_slope(conv_pre),
         conv_in,
@@ -298,9 +365,6 @@
         segment,
     )
     grad_gate_input = jnp.concatenate([grad_gate_branch, grad_conv_in], axis=1).astype(jnp.bfloat16)
-    grad_mixer_proj = jnp.dot(
-        normed_input.T, grad_gate_input, preferred_element_type=jnp.float32
-    ).reshape(mixer_proj.shape)
     partial_normed = jnp.dot(grad_gate_input, mixer_flat.T, preferred_element_type=jnp.float32)
     partial_normed = partial_normed + jnp.dot(
         grad_step_rows, step_proj.T, preferred_element_type=jnp.float32
@@ -311,67 +375,92 @@
     partial_normed = partial_normed + jnp.dot(
         grad_pairs, keyval_flat.T, preferred_element_type=jnp.float32
     )
-    grad_normed = lax.psum(partial_normed, "tensor")
+    grad_normed = exchange(partial_normed, "tensor")
     grad_normed = grad_normed + jnp.dot(
         grad_state_rows, state_proj.T, preferred_element_type=jnp.float32
     )
     grad_input_gain = jnp.sum(grad_normed * unit_in, axis=0)
     input_grad = grad_hidden + norm_backward(grad_normed * input_gain, unit_in, inv_rms_in)
-    summed = lax.psum(
-        (
-            grad_input_gain,
-            grad_mixer_proj,
-            grad_state_proj,
-            grad_step_proj,
-            grad_step_bias,
-            grad_decay_log,
-            grad_skip_gain,
-            grad_conv_kernel,
-            grad_conv_bias,
-            grad_state_kernel,
-            grad_state_bias,
-            grad_gated_gain,
-            grad_mixer_out,
-            grad_query_proj,
-            grad_keyval_proj,
-            grad_attn_out,
-            grad_ffn_gain,
-            grad_ffn_gate,
-            grad_ffn_up,
-            grad_ffn_down,
-        ),
-        "dp",
-    )
+    first = core_halves(
+        jnp.stack([normed_ffn, normed_ffn, activated, jnp.concatenate([mixer_rows, attended], axis=1)]),
+        jnp.stack([grad_gate_rows, grad_up_rows, cotangent, grad_branch]),
+    )
+    first = gather_blocks(reduce_blocks(first))
+    flat = [
+        grad_input_gain,
+        grad_step_bias,
+        grad_decay_log,
+        grad_skip_gain,
+        grad_conv_kernel,
+        grad_conv_bias,
+        grad_state_kernel,
+        grad_state_bias,
+        grad_gated_gain,
+        grad_ffn_gain,
+    ]
+    small = jnp.concatenate([part.reshape(-1) for part in flat])
+    small = jnp.pad(small, (0, 16 * model_width - small.shape[0])).reshape(16, model_width).T
+    right = jnp.concatenate(
+        [
+            grad_gate_input,
+            grad_state_rows,
+            grad_queries,
+            grad_pairs,
+            grad_step_rows,
+            jnp.zeros((document_length, 128 - heads), jnp.bfloat16),
+        ],
+        axis=1,
+    )
+    second = core_halves(normed_input[None], right[None])
+    place = lax.axis_index("core")
+    half = model_width // 2
+    small_kept = lax.dynamic_slice_in_dim(small, place * half, half, 0)
+    small_sent = lax.dynamic_slice_in_dim(small, (1 - place) * half, half, 0)
+    small_kept = small_kept + lax.ppermute(small_sent, "core", PAIR)
+    width_in = right.shape[1]
+    at_small = width_in - 128 + heads
+    second = second + jnp.pad(small_kept, ((0, 0), (at_small, 128 - heads - 16)))[None]
+    second = gather_blocks(reduce_blocks(second))[0]
+    small = second[:, at_small : at_small + 16].T.reshape(-1)
+    small_out, start = [], 0
+    for part in flat:
+        small_out.append(small[start : start + part.size].reshape(part.shape))
+        start += part.size
+    ends = [2 * width, 2 * state_size, query_heads * HEAD_DIM, kv_heads * 2 * HEAD_DIM, heads]
+    big_out, start = [], 0
+    for end in ends:
+        big_out.append(second[:, start : start + end])
+        start += end
     return (
         layer_output,
         input_grad,
-        summed[0],
-        summed[1],
-        summed[2],
-        summed[3],
-        summed[4],
-        summed[5],
-        summed[6],
-        summed[7],
-        summed[8],
-        summed[9],
-        summed[10],
-        summed[11],
-        summed[12],
-        summed[13],
-        summed[14],
-        summed[15],
-        summed[16],
-        summed[17],
-        summed[18],
-        summed[19],
+        small_out[0],
+        big_out[0].reshape(mixer_proj.shape),
+        big_out[1],
+        big_out[4],
+        small_out[1],
+        small_out[2],
+        small_out[3],
+        small_out[4],
+        small_out[5],
+        small_out[6],
+        small_out[7],
+        small_out[8],
+        first[3, :width],
+        big_out[2],
+        big_out[3].reshape(key_value_weight.shape),
+        first[3, width:],
+        small_out[9],
+        first[0],
+        first[1],
+        first[2],
     )
 
 
 def solution(mesh):
     in_specs = (
-        P("dp", None),
-        P("dp", None),
+        P(DP, None),
+        P(DP, None),
         P(),
         P(None, None, "tensor"),
         P(),
@@ -392,11 +481,11 @@
         P(None, "tensor"),
         P(None, "tensor"),
         P("tensor", None),
-        P("dp", None),
+        P(DP, None),
     )
     out_specs = (
-        P("dp", None),
-        P("dp", None),
+        P(DP, None),
+        P(DP, None),
         P(),
         P(None, None, "tensor"),
         P(),
@@ -418,6 +507,9 @@
         P(None, "tensor"),
         P("tensor", None),
     )
+    mesh = jax.sharding.Mesh(
+        mesh.devices.reshape(4, 2, 4, 2, 2), ("y", "zh", "x", "core", "tensor")
+    )
     return jax.shard_map(
         on_device, mesh=mesh, in_specs=in_specs, out_specs=out_specs, check_vma=False
     )

time: 1800 us -> 692 us (0.38)
  waiting for transfers between devices: 1510 us -> 360 us
  starting transfers between devices: 0.76 us -> 54.9 us
  matrix products: 129 us -> 109 us
    psum x5 -> x0, waiting for transfers between devices: 1510 us -> none  [the longest x2 1280 us: on_device(): lax.psum((grad_input_gain, grad_mixer_proj, grad_state_proj, grad_step_pr...]
    ppermute x0 -> x44, waiting for transfers between devices: none -> 279 us  [the longest x7 174 us: exchange(): return values + lax.ppermute(values, name, PAIR)]
    all_gather x0 -> x2, waiting for transfers between devices: none -> 81.2 us  [gather_blocks(): return lax.all_gather(values, ('core', 'y', 'zh', 'x'), axis=1, tiled=True)]
    ppermute x0 -> x44, starting transfers between devices: none -> 54.8 us  [the longest x16 13.1 us: second_halving(): return take(values, index, axis) + lax.ppermute(sent, name, LINKS[link])]
    unnamed x344 -> x303, local copies, waits for them, and re-layouts: 46.1 us -> 12.7 us
  transfers between devices with their start and end apart: 5 -> 46, of which waited for: 5 -> 29; matrix products, arithmetic and copies ran while one was open for 3% -> 12% of each run, Pallas kernels for 0% -> 0%
where the time goes in v1:
time: 692 us; the launch traced here: 687 us
  waiting for transfers between devices  360 us (52%)
  matrix products  109 us (16%)
  local copies, waits for them, and re-layouts  86.5 us (12%)
  other arithmetic  59.9 us (9%)
  starting transfers between devices  54.9 us (8%)
  between operations  17.1 us (2%)
    ppermute x7, waiting for transfers between devices, exchange(): return values + lax.ppermute(values, name, PAIR)  174 us
    all_gather x2, waiting for transfers between devices, gather_blocks(): return lax.all_gather(values, ('core', 'y', 'zh', 'x'), axis=1, tiled=True)  81.2 us
    ppermute x16, waiting for transfers between devices, first_halving(): return kept + lax.ppermute(sent, name, LINKS[link])  58.7 us
    ppermute x16, waiting for transfers between devices, second_halving(): return take(values, index, axis) + lax.ppermute(sent, name, LINKS[link])  27.6 us
    dot_general x1, matrix products, on_device(): jnp.einsum('thd,shd->hts', grad_scan, scaled_in, precision=highest)  18.3 us
    dot_general x1, matrix products, on_device(): jnp.einsum('hts,shd->thd', mixing, scaled_in, precision=highest)  17.5 us
    dot_general x4, matrix products, rows_of(): jnp.einsum('btm,btn->bmn', part, right, preferred_element_type=jnp.float32)  17.3 us
  transfers between devices with their start and end apart: 46, of which 29 were waited for; matrix products, arithmetic and copies ran while one was open for 12% of the time, Pallas kernels for 0%

profile of v1, /device:TPU:1, one launch (start us, length us, event | category | flops | bytes accessed | tf_op | source)
XLA Modules:
  0.0 687.1 jit_solution(9993218000289298684)
XLA Ops:
  27.4 4.3 fusion.49
  31.7 3.1 copy.157
  34.8 17.5 %bitcast_add_fusion = f32[512,12,64]{0,2,1:T(8,128)} fusion(f32[512,12,64]{0,2,1:T(8,128)} %bitcast.284, f32[512,512]{1,0:T(8,128)} %fusion.70, f32[12,512]{1,0:T(8,128)S(1)} %bitcast.320, pred[512,512]{1,0:T(8,128)(4,1)} %copy.158, f32[12]{0:T(128)S(1)} %copy-done.142, f32[512,12]{0,1:T(8,128)S(1)} %copy-done.100), kind=kOutput, calls=%fused_computation.80 | convolution fusion | flops 2429681664 | bytes 4505648 | tf_op jit(solution)/shard_map/hts,shd->thd/dot_general | solution.py:232
  52.3 3.0 copy.161
  55.4 4.0 multiply_reduce_fusion.11
  59.4 2.8 collective-permute-start
  78.3 44.1 %collective-permute-done.1 = f32[512,1024]{1,0:T(8,128)S(1)} collective-permute-done((f32[512,1024]{1,0:T(8,128)S(1)}, f32[512,1024]{1,0:T(8,128)S(1)}, u32[]{:S(2)}, u32[]{:S(2)}) %collective-permute-start.1) | collective-permute-done | bytes 2097184 | tf_op jit(solution)/shard_map/ppermute | solution.py:100
  134.6 41.3 %collective-permute-done.3 = f32[512,1024]{1,0:T(8,128)} collective-permute-done((f32[512,1024]{1,0:T(8,128)}, f32[512,1024]{1,0:T(8,128)}, u32[]{:S(2)}, u32[]{:S(2)}) %collective-permute-start.3) | collective-permute-done | bytes 2097184 | tf_op jit(solution)/shard_map/ppermute | solution.py:100
  176.0 3.5 multiply_reduce_fusion.1
  179.4 41.5 %collective-permute-done.2 = f32[512,1024]{1,0:T(8,128)} collective-permute-done((f32[512,1024]{1,0:T(8,128)}, f32[512,1024]{1,0:T(8,128)}, u32[]{:S(2)}, u32[]{:S(2)}) %collective-permute-start.2) | collective-permute-done | bytes 2097184 | tf_op jit(solution)/shard_map/ppermute | solution.py:100
  220.9 5.9 convert_bitcast_fusion
  229.0 2.9 multiply_reduce_fusion.4
  241.0 5.2 multiply_reduce_fusion.9
  246.2 3.1 copy.165
  249.3 18.3 %fusion.6 = (f32[12,512]{1,0:T(8,128)}, f32[12,512]{1,0:T(8,128)}, f32[512,512]{1,0:T(8,128)S(1)}) fusion(f32[512,512]{1,0:T(8,128)S(1)} %copy-done.55, f32[12,512]{1,0:T(8,128)} %bitcast.321, pred[512,512]{1,0:T(8,128)(4,1)S(1)} %copy-done.65, f32[512,12,64]{0,2,1:T(8,128)} %bitcast.287, f32[512,12,64]{0,2,1:T(8,128)} %bitcast.285, ...), kind=kOutput, calls=%fused_computation.6 | convolution fusion | flops 2444349440 | bytes 5603328 | tf_op jit(solution)/shard_map/thd,shd->hts/dot_general | solution.py:341
  267.7 12.9 %fusion.47 = (f32[512,12]{0,1:T(8,128)}, f32[512,12,64]{0,2,1:T(8,128)}) fusion(f32[512,12,64]{0,2,1:T(8,128)S(1)} %bitcast.286, f32[512,12,64]{0,2,1:T(8,128)S(1)} %bitcast.288, f32[12]{0:T(128)S(1)} %copy-done.143, f32[512,12]{0,1:T(8,128)S(1)} %copy-done.101, f32[512,512]{1,0:T(8,128)S(1)} %copy-done.55, f32[12,512]{1,0:T(8,128)S(1)} %bitcast.322, ...), kind=kOutput, calls=%fused_computation.79 | convolution fusion | flops 2430461952 | bytes 6103088 | tf_op jit(solution)/shard_map/hts,thd->shd/dot_general | solution.py:342
  283.6 3.0 copy.166
  286.6 4.9 multiply_reduce_fusion.8
  297.7 3.3 fusion.115
  307.9 4.1 concatenate.219
  312.1 5.3 convolution_bitcast_fusion
  317.4 4.9 collective-permute-start.7
  328.6 45.0 %collective-permute-done.5 = f32[512,1024]{1,0:T(8,128)} collective-permute-done((f32[512,1024]{1,0:T(8,128)}, f32[512,1024]{1,0:T(8,128)}, u32[]{:S(2)}, u32[]{:S(2)}) %collective-permute-start.5) | collective-permute-done | bytes 2097184 | tf_op jit(solution)/shard_map/ppermute | solution.py:100
  373.6 4.5 fusion.34
  382.6 4.6 fusion.19
  387.6 2.8 collective-permute-start.21
  393.5 8.7 %collective-permute-done.21 = f32[1,2,2,4,16,512]{5,4,3,2,1,0:T(8,128)S(1)} collective-permute-done((f32[1,2,2,4,16,512]{5,4,3,2,1,0:T(8,128)S(1)}, f32[1,2,2,4,16,512]{5,4,3,2,1,0:T(8,128)S(1)}, u32[]{:S(2)}, u32[]{:S(2)}) %collective-permute-start.21) | collective-permute-done | bytes 524320 | tf_op jit(solution)/shard_map/ppermute | solution.py:117
  414.9 6.4 collective-permute-done.23
  430.9 2.9 collective-permute-done.12
  434.2 3.3 collective-permute-start.25
  440.9 2.7 pad_maximum_fusion
  446.7 7.7 %collective-permute-start.26 = (f32[4,512,1024]{2,1,0:T(8,128)S(1)}, f32[4,512,1024]{2,1,0:T(8,128)}, u32[]{:S(2)}, u32[]{:S(2)}) collective-permute-start(f32[4,512,1024]{2,1,0:T(8,128)S(1)} %fusion.38), channel_id=1, source_target_pairs={{0,2},{2,0},{1,3},{3,1},{4,6},{6,4},{5,7},{7,5},{8,10},{10,8},{9,1... | collective-permute-start | bytes 25165832 | tf_op jit(solution)/shard_map/ppermute | solution.py:164
  454.5 12.9 %collective-permute-done.26 = f32[4,512,1024]{2,1,0:T(8,128)} collective-permute-done((f32[4,512,1024]{2,1,0:T(8,128)S(1)}, f32[4,512,1024]{2,1,0:T(8,128)}, u32[]{:S(2)}, u32[]{:S(2)}) %collective-permute-start.26) | collective-permute-done | bytes 8388640 | tf_op jit(solution)/shard_map/ppermute | solution.py:164
  467.4 5.0 convolution_add_fusion
  477.2 24.2 %collective-permute-done.27 = f32[4,4,2,2,16,256]{5,4,3,2,1,0:T(8,128)S(1)} collective-permute-done((f32[4,4,2,2,16,256]{5,4,3,2,1,0:T(8,128)S(1)}, f32[4,4,2,2,16,256]{5,4,3,2,1,0:T(8,128)S(1)}, u32[]{:S(2)}, u32[]{:S(2)}) %collective-permute-start.27) | collective-permute-done | bytes 1048608 | tf_op jit(solution)/shard_map/ppermute | solution.py:117
  504.0 6.2 collective-permute-done.35
  512.4 10.0 %collective-permute-done.28 = f32[4,4,2,1,16,256]{5,4,3,2,1,0:T(8,128)S(1)} collective-permute-done((f32[4,4,2,1,16,256]{5,4,3,2,1,0:T(8,128)S(1)}, f32[4,4,2,1,16,256]{5,4,3,2,1,0:T(8,128)S(1)}, u32[]{:S(2)}, u32[]{:S(2)}) %collective-permute-start.28) | collective-permute-done | bytes 524320 | tf_op jit(solution)/shard_map/ppermute | solution.py:124
  522.7 3.3 collective-permute-done.32
  527.5 9.2 %collective-permute-done.29 = f32[4,2,2,1,16,256]{5,4,3,2,1,0:T(8,128)S(1)} collective-permute-done((f32[4,2,2,1,16,256]{5,4,3,2,1,0:T(8,128)S(1)}, f32[4,2,2,1,16,256]{5,4,3,2,1,0:T(8,128)S(1)}, u32[]{:S(2)}, u32[]{:S(2)}) %collective-permute-start.29) | collective-permute-done | bytes 262176 | tf_op jit(solution)/shard_map/ppermute | solution.py:117
  544.0 3.3 collective-permute-start.43
  547.3 3.8 collective-permute-done.43
  551.9 3.4 fusion.33
  560.4 5.9 slice.357
  569.0 8.3 %reshape.578 = f32[1024,2,768]{2,1,0:T(2,128)} reshape(f32[1024,1536]{1,0:T(8,128)} %slice.357) | data formatting | bytes 12582912 | tf_op jit(solution)/shard_map/reshape | solution.py:438
  579.3 3.0 fusion.120
  582.3 81.2 %all-gather.7.cloned.1.call-done = f32[4,1,1,1,1024,1024]{5,4,3,2,1,0:T(8,128)} async-done(((f32[4,1,1,1,16,1024]{5,4,3,2,1,0:T(8,128)}), f32[4,1,1,1,1024,1024]{5,4,3,2,1,0:T(8,128)}) %all-gather.7.cloned.1.call-update) | async-done | bytes 16777232 | tf_op jit(solution)/shard_map/all_gather | solution.py:168
  665.8 4.0 slice_bitcast_fusion.3
  669.8 10.3 %slice_bitcast_fusion = (f32[1024,1024]{1,0:T(8,128)}, f32[1024,1024]{1,0:T(8,128)}, f32[1024,1024]{1,0:T(8,128)}) fusion(f32[4,1,1,1,1024,1024]{5,4,3,2,1,0:T(8,128)} %all-gather.7.cloned.1.call-done), kind=kLoop, calls=%fused_computation.22 | loop fusion | bytes 25165824 | tf_op jit(solution)/shard_map/squeeze | solution.py:456
  (589 shorter events, 148.7 us)
Async XLA Ops:
  7.2 117.0 %copy-start = (bf16[1024,1024]{1,0:T(8,128)(2,1)S(1)}, bf16[1024,1024]{1,0:T(8,128)(2,1)}, u32[]{:S(2)}) copy-start(bf16[1024,1024]{1,0:T(8,128)(2,1)} %param.42) | copy-start | bytes 6291460
  7.2 548.1 %all-gather.5.cloned.1.call-start = ((), (), s32[]{:S(2)}) async-start(), calls=%async_computation | async-start | bytes 9584640 | tf_op jit(solution)/shard_map/all_gather | solution.py:168
  24.1 262.5 %copy-start.77 = (f32[512]{0:T(512)}, f32[512]{0:T(512)S(1)}, u32[]{:S(2)}) copy-start(f32[512]{0:T(512)S(1)} %get-tuple-element.277) | copy-start | bytes 6148
  59.4 12.7 %collective-permute-start = (f32[512,1]{0,1:T(1,128)}, f32[512,1]{0,1:T(1,128)}, u32[]{:S(2)}, u32[]{:S(2)}) collective-permute-start(f32[512,1]{0,1:T(1,128)} %bitcast.12), channel_id=1, source_target_pairs={{0,1},{1,0},{2,3},{3,2},{4,5},{5,4},{6,7},{7,6},{8,9},{9,8},{10,11... | collective-permute-start | bytes 6152 | tf_op jit(solution)/shard_map/ppermute | solution.py:100
  75.5 46.8 %collective-permute-start.1 = (f32[512,1024]{1,0:T(8,128)S(1)}, f32[512,1024]{1,0:T(8,128)S(1)}, u32[]{:S(2)}, u32[]{:S(2)}) collective-permute-start(f32[512,1024]{1,0:T(8,128)S(1)} %convolution_add_fusion.1), channel_id=1, source_target_pairs={{0,1},{1,0},{2,3},{3,2},{4,5},{5,4},{6,7},{7,6},{8,9},{9,8},{10,11... | collective-permute-start | bytes 6291464 | tf_op jit(solution)/shard_map/ppermute | solution.py:100
  130.4 45.6 %collective-permute-start.3 = (f32[512,1024]{1,0:T(8,128)}, f32[512,1024]{1,0:T(8,128)}, u32[]{:S(2)}, u32[]{:S(2)}) collective-permute-start(f32[512,1024]{1,0:T(8,128)} %convolution_add_fusion.2), channel_id=1, source_target_pairs={{0,1},{1,0},{2,3},{3,2},{4,5},{5,4},{6,7},{7,6},{8,9},{9,8},{10,11... | collective-permute-start | bytes 6291464 | tf_op jit(solution)/shard_map/ppermute | solution.py:100
  133.3 87.6 %collective-permute-start.2 = (f32[512,1024]{1,0:T(8,128)}, f32[512,1024]{1,0:T(8,128)}, u32[]{:S(2)}, u32[]{:S(2)}) collective-permute-start(f32[512,1024]{1,0:T(8,128)} %fusion.133), channel_id=1, source_target_pairs={{0,1},{1,0},{2,3},{3,2},{4,5},{5,4},{6,7},{7,6},{8,9},{9,8},{10,11... | collective-permute-start | bytes 6291464 | tf_op jit(solution)/shard_map/ppermute | solution.py:100
  237.2 3.1 collective-permute-start.4
  295.2 9.6 %collective-permute-start.6 = (f32[512,256]{1,0:T(8,128)S(1)}, f32[512,256]{1,0:T(8,128)S(1)}, u32[]{:S(2)}, u32[]{:S(2)}) collective-permute-start(f32[512,256]{1,0:T(8,128)S(1)} %pad_maximum_fusion.7), channel_id=1, source_target_pairs={{0,1},{1,0},{2,3},{3,2},{4,5},{5,4},{6,7},{7,6},{8,9},{9,8},{10,11... | collective-permute-start | bytes 1572872 | tf_op jit(solution)/shard_map/ppermute | solution.py:100
  317.4 65.2 %collective-permute-start.7 = (f32[1,512,2304]{2,1,0:T(8,128)}, f32[1,512,2304]{2,1,0:T(8,128)}, u32[]{:S(2)}, u32[]{:S(2)}) collective-permute-start(f32[1,512,2304]{2,1,0:T(8,128)} %convolution_bitcast_fusion), channel_id=1, source_target_pairs={{0,2},{2,0},{1,3},{3,1},{4,6},{6,4},{5,7},{7,5},{8,10},{10,8},{9,1... | collective-permute-start | bytes 14155784 | tf_op jit(solution)/shard_map/ppermute | solution.py:164
  327.1 46.5 %collective-permute-start.5 = (f32[512,1024]{1,0:T(8,128)}, f32[512,1024]{1,0:T(8,128)}, u32[]{:S(2)}, u32[]{:S(2)}) collective-permute-start(f32[512,1024]{1,0:T(8,128)} %add_add_fusion.1), channel_id=1, source_target_pairs={{0,1},{1,0},{2,3},{3,2},{4,5},{5,4},{6,7},{7,6},{8,9},{9,8},{10,11... | collective-permute-start | bytes 6291464 | tf_op jit(solution)/shard_map/ppermute | solution.py:100
  379.1 3.4 collective-permute-start.8
  387.6 14.6 %collective-permute-start.21 = (f32[1,2,2,4,16,512]{5,4,3,2,1,0:T(8,128)S(1)}, f32[1,2,2,4,16,512]{5,4,3,2,1,0:T(8,128)S(1)}, u32[]{:S(2)}, u32[]{:S(2)}) collective-permute-start(f32[1,2,2,4,16,512]{5,4,3,2,1,0:T(8,128)S(1)} %constant_dynamic-slice_fusion.42), channel_id=1, source_target_pairs={{32,64},{64,32},{96,0},{0,96},{33,65},{65,33},{97,1},{1,97},{34,66... | collective-permute-start | bytes 1572872 | tf_op jit(solution)/shard_map/ppermute | solution.py:117
  390.6 13.1 %collective-permute-start.17 = (f32[1,2,2,4,16,512]{5,4,3,2,1,0:T(8,128)S(1)}, f32[1,2,2,4,16,512]{5,4,3,2,1,0:T(8,128)S(1)}, u32[]{:S(2)}, u32[]{:S(2)}) collective-permute-start(f32[1,2,2,4,16,512]{5,4,3,2,1,0:T(8,128)S(1)} %pad_maximum_fusion.8), channel_id=1, source_target_pairs={{0,32},{32,0},{64,96},{96,64},{1,33},{33,1},{65,97},{97,65},{2,34}... | collective-permute-start | bytes 1572872 | tf_op jit(solution)/shard_map/ppermute | solution.py:117
  390.7 16.8 %collective-permute-start.13 = (f32[1,4,2,2,16,640]{5,4,3,2,1,0:T(8,128)S(1)}, f32[1,4,2,2,16,640]{5,4,3,2,1,0:T(8,128)S(1)}, u32[]{:S(2)}, u32[]{:S(2)}) collective-permute-start(f32[1,4,2,2,16,640]{5,4,3,2,1,0:T(8,128)S(1)} %constant_dynamic-slice_fusion.59), channel_id=1, source_target_pairs={{4,8},{8,4},{12,0},{0,12},{5,9},{9,5},{13,1},{1,13},{6,10},{10,6},... | collective-permute-start | bytes 1966088 | tf_op jit(solution)/shard_map/ppermute | solution.py:117
  393.4 15.6 %collective-permute-start.9 = (f32[1,4,2,2,16,640]{5,4,3,2,1,0:T(8,128)S(1)}, f32[1,4,2,2,16,640]{5,4,3,2,1,0:T(8,128)S(1)}, u32[]{:S(2)}, u32[]{:S(2)}) collective-permute-start(f32[1,4,2,2,16,640]{5,4,3,2,1,0:T(8,128)S(1)} %pad_maximum_fusion.6), channel_id=1, source_target_pairs={{0,4},{4,0},{8,12},{12,8},{1,5},{5,1},{9,13},{13,9},{2,6},{6,2},{1... | collective-permute-start | bytes 1966088 | tf_op jit(solution)/shard_map/ppermute | solution.py:117
  402.4 11.9 %collective-permute-start.22 = (f32[1,2,2,2,16,512]{5,4,3,2,1,0:T(8,128)S(1)}, f32[1,2,2,2,16,512]{5,4,3,2,1,0:T(8,128)S(1)}, u32[]{:S(2)}, u32[]{:S(2)}) collective-permute-start(f32[1,2,2,2,16,512]{5,4,3,2,1,0:T(8,128)S(1)} %pad_maximum_fusion.16), channel_id=1, source_target_pairs={{0,4},{4,0},{8,12},{12,8},{1,5},{5,1},{9,13},{13,9},{2,6},{6,2},{1... | collective-permute-start | bytes 786440 | tf_op jit(solution)/shard_map/ppermute | solution.py:117
  403.8 10.9 %collective-permute-start.18 = (f32[1,1,2,4,16,512]{5,4,3,2,1,0:T(8,128)S(1)}, f32[1,1,2,4,16,512]{5,4,3,2,1,0:T(8,128)S(1)}, u32[]{:S(2)}, u32[]{:S(2)}) collective-permute-start(f32[1,1,2,4,16,512]{5,4,3,2,1,0:T(8,128)S(1)} %constant_dynamic-slice_fusion.48), channel_id=1, source_target_pairs={{32,64},{64,32},{96,0},{0,96},{33,65},{65,33},{97,1},{1,97},{34,66... | collective-permute-start | bytes 786440 | tf_op jit(solution)/shard_map/ppermute | solution.py:124
  407.7 15.4 %collective-permute-start.14 = (f32[1,2,2,2,16,640]{5,4,3,2,1,0:T(8,128)S(1)}, f32[1,2,2,2,16,640]{5,4,3,2,1,0:T(8,128)S(1)}, u32[]{:S(2)}, u32[]{:S(2)}) collective-permute-start(f32[1,2,2,2,16,640]{5,4,3,2,1,0:T(8,128)S(1)} %pad_maximum_fusion.12), channel_id=1, source_target_pairs={{0,32},{32,0},{64,96},{96,64},{1,33},{33,1},{65,97},{97,65},{2,34}... | collective-permute-start | bytes 983048 | tf_op jit(solution)/shard_map/ppermute | solution.py:117
  409.2 14.7 %collective-permute-start.10 = (f32[1,4,2,1,16,640]{5,4,3,2,1,0:T(8,128)S(1)}, f32[1,4,2,1,16,640]{5,4,3,2,1,0:T(8,128)S(1)}, u32[]{:S(2)}, u32[]{:S(2)}) collective-permute-start(f32[1,4,2,1,16,640]{5,4,3,2,1,0:T(8,128)S(1)} %constant_dynamic-slice_fusion.65), channel_id=1, source_target_pairs={{4,8},{8,4},{12,0},{0,12},{5,9},{9,5},{13,1},{1,13},{6,10},{10,6},... | collective-permute-start | bytes 983048 | tf_op jit(solution)/shard_map/ppermute | solution.py:124
  414.4 6.9 collective-permute-start.23
  414.8 7.8 %collective-permute-start.19 = (f32[1,1,2,2,16,512]{5,4,3,2,1,0:T(8,128)S(1)}, f32[1,1,2,2,16,512]{5,4,3,2,1,0:T(8,128)S(1)}, u32[]{:S(2)}, u32[]{:S(2)}) collective-permute-start(f32[1,1,2,2,16,512]{5,4,3,2,1,0:T(8,128)S(1)} %pad_maximum_fusion.22), channel_id=1, source_target_pairs={{0,4},{4,0},{8,12},{12,8},{1,5},{5,1},{9,13},{13,9},{2,6},{6,2},{1... | collective-permute-start | bytes 393224 | tf_op jit(solution)/shard_map/ppermute | solution.py:117
  421.3 5.8 collective-permute-start.24
  422.7 4.4 collective-permute-start.20
  423.2 7.6 %collective-permute-start.15 = (f32[1,1,2,2,16,640]{5,4,3,2,1,0:T(8,128)S(1)}, f32[1,1,2,2,16,640]{5,4,3,2,1,0:T(8,128)S(1)}, u32[]{:S(2)}, u32[]{:S(2)}) collective-permute-start(f32[1,1,2,2,16,640]{5,4,3,2,1,0:T(8,128)S(1)} %constant_dynamic-slice_fusion.54), channel_id=1, source_target_pairs={{32,64},{64,32},{96,0},{0,96},{33,65},{65,33},{97,1},{1,97},{34,66... | collective-permute-start | bytes 491528 | tf_op jit(solution)/shard_map/ppermute | solution.py:124
  424.0 4.9 collective-permute-start.11
  429.0 4.8 collective-permute-start.12
  430.8 3.4 collective-permute-start.16
  434.2 5.9 collective-permute-start.25
  440.8 222.7 %all-gather.7.cloned.1.call-start = ((), (), s32[]{:S(2)}) async-start(), calls=%async_computation.1 | async-start | bytes 17039360 | tf_op jit(solution)/shard_map/all_gather | solution.py:168
  446.7 20.6 %collective-permute-start.26 = (f32[4,512,1024]{2,1,0:T(8,128)S(1)}, f32[4,512,1024]{2,1,0:T(8,128)}, u32[]{:S(2)}, u32[]{:S(2)}) collective-permute-start(f32[4,512,1024]{2,1,0:T(8,128)S(1)} %fusion.38), channel_id=1, source_target_pairs={{0,2},{2,0},{1,3},{3,1},{4,6},{6,4},{5,7},{7,5},{8,10},{10,8},{9,1... | collective-permute-start | bytes 25165832 | tf_op jit(solution)/shard_map/ppermute | solution.py:164
  473.8 27.6 %collective-permute-start.27 = (f32[4,4,2,2,16,256]{5,4,3,2,1,0:T(8,128)S(1)}, f32[4,4,2,2,16,256]{5,4,3,2,1,0:T(8,128)S(1)}, u32[]{:S(2)}, u32[]{:S(2)}) collective-permute-start(f32[4,4,2,2,16,256]{5,4,3,2,1,0:T(8,128)S(1)} %pad_maximum_fusion.2), channel_id=1, source_target_pairs={{0,4},{4,0},{8,12},{12,8},{1,5},{5,1},{9,13},{13,9},{2,6},{6,2},{1... | collective-permute-start | bytes 3145736 | tf_op jit(solution)/shard_map/ppermute | solution.py:117
  474.0 29.5 %collective-permute-start.31 = (f32[4,4,2,2,16,256]{5,4,3,2,1,0:T(8,128)S(1)}, f32[4,4,2,2,16,256]{5,4,3,2,1,0:T(8,128)S(1)}, u32[]{:S(2)}, u32[]{:S(2)}) collective-permute-start(f32[4,4,2,2,16,256]{5,4,3,2,1,0:T(8,128)S(1)} %constant_dynamic-slice_fusion.24), channel_id=1, source_target_pairs={{4,8},{8,4},{12,0},{0,12},{5,9},{9,5},{13,1},{1,13},{6,10},{10,6},... | collective-permute-start | bytes 3145736 | tf_op jit(solution)/shard_map/ppermute | solution.py:117
  476.1 34.1 %collective-permute-start.35 = (f32[4,2,2,4,16,256]{5,4,3,2,1,0:T(8,128)S(1)}, f32[4,2,2,4,16,256]{5,4,3,2,1,0:T(8,128)S(1)}, u32[]{:S(2)}, u32[]{:S(2)}) collective-permute-start(f32[4,2,2,4,16,256]{5,4,3,2,1,0:T(8,128)S(1)} %pad_maximum_fusion.3), channel_id=1, source_target_pairs={{0,32},{32,0},{64,96},{96,64},{1,33},{33,1},{65,97},{97,65},{2,34}... | collective-permute-start | bytes 3145736 | tf_op jit(solution)/shard_map/ppermute | solution.py:117
  476.3 35.7 %collective-permute-start.39 = (f32[4,2,2,4,16,256]{5,4,3,2,1,0:T(8,128)S(1)}, f32[4,2,2,4,16,256]{5,4,3,2,1,0:T(8,128)S(1)}, u32[]{:S(2)}, u32[]{:S(2)}) collective-permute-start(f32[4,2,2,4,16,256]{5,4,3,2,1,0:T(8,128)S(1)} %constant_dynamic-slice_fusion.7), channel_id=1, source_target_pairs={{32,64},{64,32},{96,0},{0,96},{33,65},{65,33},{97,1},{1,97},{34,66... | collective-permute-start | bytes 3145736 | tf_op jit(solution)/shard_map/ppermute | solution.py:117
  501.6 20.7 %collective-permute-start.28 = (f32[4,4,2,1,16,256]{5,4,3,2,1,0:T(8,128)S(1)}, f32[4,4,2,1,16,256]{5,4,3,2,1,0:T(8,128)S(1)}, u32[]{:S(2)}, u32[]{:S(2)}) collective-permute-start(f32[4,4,2,1,16,256]{5,4,3,2,1,0:T(8,128)S(1)} %constant_dynamic-slice_fusion.30), channel_id=1, source_target_pairs={{4,8},{8,4},{12,0},{0,12},{5,9},{9,5},{13,1},{1,13},{6,10},{10,6},... | collective-permute-start | bytes 1572872 | tf_op jit(solution)/shard_map/ppermute | solution.py:124
  503.9 22.1 %collective-permute-start.32 = (f32[4,2,2,2,16,256]{5,4,3,2,1,0:T(8,128)S(1)}, f32[4,2,2,2,16,256]{5,4,3,2,1,0:T(8,128)S(1)}, u32[]{:S(2)}, u32[]{:S(2)}) collective-permute-start(f32[4,2,2,2,16,256]{5,4,3,2,1,0:T(8,128)S(1)} %pad_maximum_fusion.9), channel_id=1, source_target_pairs={{0,32},{32,0},{64,96},{96,64},{1,33},{33,1},{65,97},{97,65},{2,34}... | collective-permute-start | bytes 1572872 | tf_op jit(solution)/shard_map/ppermute | solution.py:117
  510.5 15.8 %collective-permute-start.36 = (f32[4,1,2,4,16,256]{5,4,3,2,1,0:T(8,128)S(1)}, f32[4,1,2,4,16,256]{5,4,3,2,1,0:T(8,128)S(1)}, u32[]{:S(2)}, u32[]{:S(2)}) collective-permute-start(f32[4,1,2,4,16,256]{5,4,3,2,1,0:T(8,128)S(1)} %constant_dynamic-slice_fusion.13), channel_id=1, source_target_pairs={{32,64},{64,32},{96,0},{0,96},{33,65},{65,33},{97,1},{1,97},{34,66... | collective-permute-start | bytes 1572872 | tf_op jit(solution)/shard_map/ppermute | solution.py:124
  512.3 14.9 %collective-permute-start.40 = (f32[4,2,2,2,16,256]{5,4,3,2,1,0:T(8,128)S(1)}, f32[4,2,2,2,16,256]{5,4,3,2,1,0:T(8,128)S(1)}, u32[]{:S(2)}, u32[]{:S(2)}) collective-permute-start(f32[4,2,2,2,16,256]{5,4,3,2,1,0:T(8,128)S(1)} %pad_maximum_fusion.10), channel_id=1, source_target_pairs={{0,4},{4,0},{8,12},{12,8},{1,5},{5,1},{9,13},{13,9},{2,6},{6,2},{1... | collective-permute-start | bytes 1572872 | tf_op jit(solution)/shard_map/ppermute | solution.py:117
  522.5 14.2 %collective-permute-start.29 = (f32[4,2,2,1,16,256]{5,4,3,2,1,0:T(8,128)S(1)}, f32[4,2,2,1,16,256]{5,4,3,2,1,0:T(8,128)S(1)}, u32[]{:S(2)}, u32[]{:S(2)}) collective-permute-start(f32[4,2,2,1,16,256]{5,4,3,2,1,0:T(8,128)S(1)} %pad_maximum_fusion.17), channel_id=1, source_target_pairs={{0,32},{32,0},{64,96},{96,64},{1,33},{33,1},{65,97},{97,65},{2,34}... | collective-permute-start | bytes 786440 | tf_op jit(solution)/shard_map/ppermute | solution.py:117
  526.1 12.4 %collective-permute-start.33 = (f32[4,1,2,2,16,256]{5,4,3,2,1,0:T(8,128)S(1)}, f32[4,1,2,2,16,256]{5,4,3,2,1,0:T(8,128)S(1)}, u32[]{:S(2)}, u32[]{:S(2)}) collective-permute-start(f32[4,1,2,2,16,256]{5,4,3,2,1,0:T(8,128)S(1)} %constant_dynamic-slice_fusion.19), channel_id=1, source_target_pairs={{32,64},{64,32},{96,0},{0,96},{33,65},{65,33},{97,1},{1,97},{34,66... | collective-permute-start | bytes 786440 | tf_op jit(solution)/shard_map/ppermute | solution.py:124
  526.4 12.2 %collective-permute-start.37 = (f32[4,1,2,2,16,256]{5,4,3,2,1,0:T(8,128)S(1)}, f32[4,1,2,2,16,256]{5,4,3,2,1,0:T(8,128)S(1)}, u32[]{:S(2)}, u32[]{:S(2)}) collective-permute-start(f32[4,1,2,2,16,256]{5,4,3,2,1,0:T(8,128)S(1)} %pad_maximum_fusion.18), channel_id=1, source_target_pairs={{0,4},{4,0},{8,12},{12,8},{1,5},{5,1},{9,13},{13,9},{2,6},{6,2},{1... | collective-permute-start | bytes 786440 | tf_op jit(solution)/shard_map/ppermute | solution.py:117
  527.3 11.7 %collective-permute-start.41 = (f32[4,2,2,1,16,256]{5,4,3,2,1,0:T(8,128)S(1)}, f32[4,2,2,1,16,256]{5,4,3,2,1,0:T(8,128)S(1)}, u32[]{:S(2)}, u32[]{:S(2)}) collective-permute-start(f32[4,2,2,1,16,256]{5,4,3,2,1,0:T(8,128)S(1)} %constant_dynamic-slice_fusion.2), channel_id=1, source_target_pairs={{4,8},{8,4},{12,0},{0,12},{5,9},{9,5},{13,1},{1,13},{6,10},{10,6},... | collective-permute-start | bytes 786440 | tf_op jit(solution)/shard_map/ppermute | solution.py:124
  536.7 5.4 collective-permute-start.30
  538.5 4.2 collective-permute-start.34
  538.7 5.2 collective-permute-start.38
  539.1 4.8 collective-permute-start.42
  544.0 7.1 %collective-permute-start.43 = (f32[4,1,1,1,16,1024]{5,4,3,2,1,0:T(8,128)S(1)}, f32[4,1,1,1,16,1024]{5,4,3,2,1,0:T(8,128)S(1)}, u32[]{:S(2)}, u32[]{:S(2)}) collective-permute-start(f32[4,1,1,1,16,1024]{5,4,3,2,1,0:T(8,128)S(1)} %constant_dynamic-slice_fusion), channel_id=1, source_target_pairs={{0,16},{16,0},{1,17},{17,1},{2,18},{18,2},{3,19},{19,3},{4,20},{20... | collective-permute-start | bytes 786440 | tf_op jit(solution)/shard_map/ppermute | solution.py:152
  (144 other events, 1566.9 us)
Sparse Core Ops, SparseCore 0:
  440.9 96.9 all-gather.4
  552.0 111.4 all-gather.6

commit v2 on v1

v2 whole, which is shorter than its diff:
```python
import functools

import jax
import jax.numpy as jnp
import numpy as np
from jax import lax
from jax.experimental import pallas as pl
from jax.experimental.pallas import tpu as pltpu
from jax.sharding import PartitionSpec as P

HEAD_DIM = 64
DSSM = 1536
DP = ("y", "zh", "x", "core")
PAIR = [(0, 1), (1, 0)]
LINKS = {
    "A": [(0, 1), (1, 0), (2, 3), (3, 2)],
    "B": [(1, 2), (2, 1), (3, 0), (0, 3)],
}
ORDERS = (
    (("x", "A"), ("x", "B"), ("y", "A"), ("y", "B")),
    (("x", "B"), ("y", "A"), ("y", "B"), ("x", "A")),
    (("y", "A"), ("y", "B"), ("x", "A"), ("x", "B")),
    (("y", "B"), ("x", "A"), ("x", "B"), ("y", "A")),
)
AXIS = {"y": 1, "x": 3}
LOG2E = 1.4426950408889634
hidden_bias = -1e30
norm_eps = 1e-05
rope_base = 10000.0
LEN = 128


def dot_nn(left, right):
    return lax.dot_general(
        left, right, (((1,), (0,)), ((), ())), preferred_element_type=jnp.float32
    )


def dot_nt(left, right):
    return lax.dot_general(
        left, right, (((1,), (1,)), ((), ())), preferred_element_type=jnp.float32
    )


def dot_tn(left, right):
    return lax.dot_general(
        left, right, (((0,), (0,)), ((), ())), preferred_element_type=jnp.float32
    )


def two_terms(v):
    high = v.astype(jnp.bfloat16)
    return high, (v - high.astype(jnp.float32)).astype(jnp.bfloat16)


def three_dots(dot, left, right):
    left_high, left_low = two_terms(left)
    right_high, right_low = two_terms(right)
    return dot(left_high, right_high) + dot(left_high, right_low) + dot(left_low, right_high)


def sigmoid(v):
    return 1.0 / (1.0 + jnp.exp(-v))


def block(index):
    return slice(index * LEN, (index + 1) * LEN)


def lane_iota(rows=LEN):
    return lax.broadcasted_iota(jnp.int32, (rows, LEN), 1)


def mask_ts(seg_col, seg_row, i, j):
    same = seg_col[block(i), :] == seg_row[:, block(j)]
    if i != j:
        return same
    down = lax.broadcasted_iota(jnp.int32, (LEN, LEN), 0)
    return same & (down >= lane_iota())


def mask_st(seg_col, seg_row, j, i):
    same = seg_col[block(j), :] == seg_row[:, block(i)]
    if i != j:
        return same
    down = lax.broadcasted_iota(jnp.int32, (LEN, LEN), 0)
    return same & (down <= lane_iota())


def conv_rows(pad_ref, keep_ref, kernel, bias, start, lanes):
    summed = bias + kernel[3:4] * pad_ref[8 + start : 8 + start + LEN, lanes]
    for lag in (1, 2, 3):
        moved = pad_ref[8 + start - lag : 8 + start - lag + LEN, lanes]
        summed = summed + kernel[3 - lag : 4 - lag] * (moved * keep_ref[lag - 1, start : start + LEN, :])
    return summed


def widen(keep_ref, wide_ref):
    rows = keep_ref.shape[0]
    for lag in (1, 2, 3):
        wide_ref[lag - 1, :, :] = jnp.broadcast_to(keep_ref[:, lag : lag + 1], (rows, LEN))


def prep_kernel(
    conv_ref,
    small_ref,
    cos_ref,
    sin_ref,
    keep_ref,
    conv_kernel_ref,
    conv_bias_ref,
    state_kernel_ref,
    state_bias_ref,
    step_bias_ref,
    rate_ref,
    x_ref,
    xb_ref,
    slope_ref,
    state_ref,
    state_slope_ref,
    cum_ref,
    lag_ref,
    cum_row_ref,
    lag_row_ref,
    step_row_ref,
    sig_row_ref,
    q_ref,
    kv_ref,
    pad_ref,
    state_pad_ref,
    wide_ref,
):
    rows = conv_ref.shape[0]
    blocks = rows // LEN
    pad_ref[0:8, :] = jnp.zeros((8, pad_ref.shape[1]), jnp.float32)
    pad_ref[8 : rows + 8, :] = conv_ref[...]
    state_pad_ref[0:8, :] = jnp.zeros((8, state_pad_ref.shape[1]), jnp.float32)
    state_pad_ref[8 : rows + 8, :] = small_ref[:, : 2 * LEN]
    widen(keep_ref, wide_ref)

    def channel_tile(c, _):
        lanes = pl.ds(pl.multiple_of(c * LEN, LEN), LEN)
        for i in range(blocks):
            pre = conv_rows(pad_ref, wide_ref, conv_kernel_ref[:, lanes], conv_bias_ref[:, lanes], i * LEN, lanes)
            sig = sigmoid(pre)
            x = pre * sig
            x_ref[block(i), lanes] = x
            xb_ref[block(i), lanes] = x.astype(jnp.bfloat16)
            slope_ref[block(i), lanes] = sig * (1.0 + pre * (1.0 - sig))
        return 0

    lax.fori_loop(0, conv_ref.shape[1] // LEN, channel_tile, 0)

    def state_tile(c, _):
        lanes = pl.ds(pl.multiple_of(c * LEN, LEN), LEN)
        for i in range(blocks):
            pre = conv_rows(
                state_pad_ref, wide_ref, state_kernel_ref[:, lanes], state_bias_ref[:, lanes], i * LEN, lanes
            )
            sig = sigmoid(pre)
            state_ref[block(i), lanes] = pre * sig
            state_slope_ref[block(i), lanes] = sig * (1.0 + pre * (1.0 - sig))
        return 0

    lax.fori_loop(0, 2, state_tile, 0)

    down = lax.broadcasted_iota(jnp.int32, (LEN, LEN), 0)
    lower = jnp.where(down >= lane_iota(), 1.0, 0.0).astype(jnp.bfloat16)
    left_half = lane_iota() < HEAD_DIM
    carry = jnp.zeros((1, LEN), jnp.float32)
    heads = cum_row_ref.shape[0]
    for i in range(blocks):
        argument = small_ref[block(i), block(5)] + step_bias_ref[...]
        tail = jnp.exp(-jnp.abs(argument))
        grown = jnp.where(tail < 1e-3, tail - 0.5 * tail * tail, jnp.log(1.0 + tail))
        step = jnp.maximum(argument, 0.0) + grown
        first, rest = two_terms(step * rate_ref[...] * LOG2E)
        last = step * rate_ref[...] * LOG2E - first.astype(jnp.float32) - rest.astype(jnp.float32)
        cum = dot_nn(lower, first) + dot_nn(lower, rest) + dot_nn(lower, last.astype(jnp.bfloat16)) + carry
        carry = cum[LEN - 1 : LEN, :]
        lag = cum - jnp.log(step) * LOG2E
        cum_ref[block(i), :] = cum
        lag_ref[block(i), :] = lag
        cum_t, lag_t = cum.T, lag.T
        step_row_ref[:, block(i)] = step.T[:heads]
        sig_row_ref[:, block(i)] = sigmoid(argument).T[:heads]
        for h in range(heads):
            cum_row_ref[h, :, block(i)] = cum_t[h : h + 1]
            lag_row_ref[h, :, block(i)] = lag_t[h : h + 1]
        cosine, sine = cos_ref[block(i), :], sin_ref[block(i), :]
        kv = small_ref[block(i), block(4)]
        kv_ref[block(i), :] = jnp.where(left_half, rotate_tile(kv, cosine, sine), kv).astype(jnp.bfloat16)
        for p in range(q_ref.shape[1] // LEN):
            q_ref[block(i), block(p)] = rotate_tile(small_ref[block(i), block(2 + p)], cosine, sine).astype(jnp.bfloat16)


def rotate_tile(v, cosine, sine):
    first = lax.rem(lane_iota(v.shape[0]), HEAD_DIM) < HEAD_DIM // 2
    swapped = jnp.where(first, pltpu.roll(v, LEN - HEAD_DIM // 2, 1), pltpu.roll(v, HEAD_DIM // 2, 1))
    return v * cosine + swapped * sine


def scan_kernel(
    chunks,
    heads,
    gate_ref,
    x_ref,
    xb_ref,
    state_ref,
    cum_ref,
    lag_row_ref,
    seg_col_ref,
    seg_row_ref,
    skip_ref,
    y_ref,
    gated_ref,
    row_ref,
    wide_ref,
    cross_ref,
    bias_ref,
    mix_ref,
    square_ref,
):
    first = chunks[0]
    for h in range(heads):
        for i in chunks:
            wide_ref[h, block(i - first), :] = jnp.broadcast_to(cum_ref[block(i), h : h + 1], (LEN, LEN))
    pairs = [(i, j) for i in chunks for j in range(max(0, i - 2), i + 1)]
    for i in chunks:
        low = max(0, i - 2)
        cross = three_dots(dot_nt, state_ref[block(i), LEN:], state_ref[low * LEN : (i + 1) * LEN, :LEN])
        for n, (i2, j) in enumerate(pairs):
            if i2 == i:
                cross_ref[n] = cross[:, block(j - low)]
                allowed = mask_ts(seg_col_ref, seg_row_ref, i, j)
                bias_ref[n] = jnp.where(allowed, 0.0, hidden_bias)
    left_half = lane_iota() < HEAD_DIM
    square_ref[...] = jnp.zeros(square_ref.shape, jnp.float32)

    def head_pair(hp, _):
        lanes = pl.ds(pl.multiple_of(hp * LEN, LEN), LEN)
        for i in chunks:
            at = block(i - first)
            low = max(0, i - 2)
            for n, (i2, j) in enumerate(pairs):
                if i2 != i:
                    continue
                for e in range(2):
                    spread = wide_ref[2 * hp + e, at, :] - lag_row_ref[2 * hp + e, :, block(j)]
                    decay = jnp.exp2(spread + bias_ref[n])
                    mix_ref[block(e), block(j - low)] = (decay * cross_ref[n]).astype(jnp.bfloat16)
            both = dot_nn(mix_ref[:, : (i + 1 - low) * LEN], xb_ref[low * LEN : (i + 1) * LEN, lanes])
            y = jnp.where(left_half, both[:LEN], both[LEN:])
            y_ref[at, lanes] = y
            gate = gate_ref[block(i), lanes]
            gated = (y + skip_ref[:, lanes] * x_ref[block(i), lanes]) * (gate * sigmoid(gate))
            gated_ref[at, lanes] = gated
            square_ref[at, :] = square_ref[at, :] + gated * gated
        return 0

    lax.fori_loop(0, heads // 2, head_pair, 0)
    for i in chunks:
        at = block(i - first)
        total = jnp.sum(square_ref[at, :], axis=1, keepdims=True)
        row_ref[0:1, at] = jnp.broadcast_to(total, (LEN, LEN)).T[0:1]


def attention_kernel(chunks, q_ref, kv_ref, seg_col_ref, seg_row_ref, out_ref, lse_ref):
    scale = HEAD_DIM ** (-0.5) * LOG2E
    first = chunks[0]
    left_half = lane_iota() < HEAD_DIM
    zero = jnp.zeros((LEN, LEN), jnp.bfloat16)
    lse_ref[...] = jnp.zeros(lse_ref.shape, jnp.float32)
    for i in chunks:
        at = block(i - first)
        low = max(0, i - 2) * LEN
        span = (i + 1) * LEN - low
        allowed = jnp.concatenate([mask_ts(seg_col_ref, seg_row_ref, i, j) for j in range(low // LEN, i + 1)], axis=1)
        keys = kv_ref[low : low + span, :]
        turned = pltpu.roll(keys.astype(jnp.float32), HEAD_DIM, 1).astype(jnp.bfloat16)
        for p in range(q_ref.shape[1] // LEN):
            queries = q_ref[block(i), block(p)]
            result = []
            for e in range(2):
                masked = jnp.where(left_half == (e == 0), queries, zero)
                scores = dot_nt(masked, keys if e == 0 else turned) * scale
                scores = jnp.where(allowed, scores, hidden_bias)
                top = jnp.max(scores, axis=1, keepdims=True)
                weights = jnp.exp2(scores - top)
                total = jnp.sum(weights, axis=1, keepdims=True)
                probs = (weights * (1.0 / total)).astype(jnp.bfloat16)
                result.append(dot_nn(probs, turned if e == 0 else keys))
                lse = jnp.broadcast_to(top + jnp.log(total) * LOG2E, (LEN, LEN))
                lse_ref[2 * p + e : 2 * p + e + 1, at] = lse.T[0:1]
            out_ref[at, block(p)] = jnp.where(left_half, result[0], result[1]).astype(jnp.bfloat16)


def attention_back_kernel(chunks, final, *refs):
    q_ref, kv_ref, do_ref, lse_ref, seg_col_ref, seg_row_ref, cos_ref, sin_ref = refs[:8]
    if final:
        dk_in_ref, dv_in_ref, dq_ref, dkv_ref, dk_ref, dv_ref, turned_ref, key_t_ref = refs[8:]
    else:
        dq_ref, dk_ref, dv_ref, turned_ref, key_t_ref = refs[8:]
    scale = HEAD_DIM ** (-0.5)
    blocks = q_ref.shape[0] // LEN
    first = chunks[0]
    left_half = lane_iota() < HEAD_DIM
    zero = jnp.zeros((LEN, LEN), jnp.bfloat16)
    for i in range(chunks[-1] + 1):
        kv = kv_ref[block(i), :].astype(jnp.float32)
        turned_ref[block(i), :] = pltpu.roll(kv, HEAD_DIM, 1).astype(jnp.bfloat16)
        key_t_ref[:, block(i)] = kv.T[:HEAD_DIM].astype(jnp.bfloat16)
    if final:
        dk_ref[...] = dk_in_ref[...]
        dv_ref[...] = dv_in_ref[...]
    else:
        dk_ref[...] = jnp.zeros(dk_ref.shape, jnp.float32)
        dv_ref[...] = jnp.zeros(dv_ref.shape, jnp.float32)
    for i in chunks:
        at = block(i - first)
        low = max(0, i - 2) * LEN
        span = (i + 1) * LEN - low
        window = slice(low, low + span)
        allowed = jnp.concatenate([mask_st(seg_col_ref, seg_row_ref, j, i) for j in range(low // LEN, i + 1)], axis=0)
        keys, turned = kv_ref[window, :], turned_ref[window, :]
        for p in range(q_ref.shape[1] // LEN):
            queries, douts = q_ref[block(i), block(p)], do_ref[at, block(p)]
            back = []
            for e in range(2):
                side = left_half == (e == 0)
                q_half = jnp.where(side, queries, zero)
                do_half = jnp.where(side, douts, zero)
                h = 2 * p + e
                scores = dot_nt(keys if e == 0 else turned, q_half) * (scale * LOG2E)
                probs = jnp.exp2(jnp.where(allowed, scores, hidden_bias) - lse_ref[h : h + 1, at])
                dprobs = dot_nt(turned if e == 0 else keys, do_half)
                inner = jnp.sum(probs * dprobs, axis=0, keepdims=True)
                dscores = (probs * (dprobs - inner)).astype(jnp.bfloat16)
                dv_ref[window, :] = dv_ref[window, :] + dot_nn(probs.astype(jnp.bfloat16), do_half)
                dk_ref[window, :] = dk_ref[window, :] + dot_nn(dscores, q_half)
                back.append(dot_nn(key_t_ref[:, window], dscores))
            dq = jnp.concatenate(back, axis=0).T * scale
            dq_ref[at, block(p)] = rotate_tile(dq, cos_ref[block(i), :], -sin_ref[block(i), :]).astype(jnp.bfloat16)
    if not final:
        return
    for i in range(blocks):
        dk = dk_ref[block(i), :]
        dk = (dk + pltpu.roll(dk, HEAD_DIM, 1)) * scale
        dk = rotate_tile(dk, cos_ref[block(i), :], -sin_ref[block(i), :])
        dv = dv_ref[block(i), :]
        dv = dv + pltpu.roll(dv, HEAD_DIM, 1)
        dkv_ref[block(i), :] = jnp.where(left_half, dk, dv).astype(jnp.bfloat16)


def scan_back_kernel(
    chunks,
    heads,
    gmr_ref,
    gated_ref,
    inv_ref,
    dot_ref,
    gain_ref,
    gate_ref,
    y_ref,
    x_ref,
    xb_ref,
    state_ref,
    lag_ref,
    cum_row_ref,
    skip_ref,
    seg_col_ref,
    seg_row_ref,
    select_ref,
    dgate_ref,
    gy_ref,
    dx_ref,
    p_ref,
    grad_in_ref,
    grad_out_ref,
    skip_sum_ref,
    gyb_ref,
    wide_ref,
    cross_ref,
    bias_ref,
    dcross_ref,
    high_ref,
    rest_ref,
    inv_wide_ref,
    dot_wide_ref,
    inner_ref,
    mix_ref,
):
    first = chunks[0]
    half = len(chunks) * LEN
    sources = chunks[-1] + 1
    left_half = lane_iota() < HEAD_DIM
    zero = jnp.zeros((LEN, LEN), jnp.bfloat16)
    inv_wide_ref[...] = jnp.broadcast_to(inv_ref[...], (half, LEN))
    dot_wide_ref[...] = jnp.broadcast_to(dot_ref[...], (half, LEN))
    for h in range(heads):
        wide_ref[h] = jnp.broadcast_to(lag_ref[: sources * LEN, h : h + 1], (sources * LEN, LEN))
    spans = [(j, max(j, first), min(j + 3, sources)) for j in range(sources)]
    pairs = [(j, i) for j, start, stop in spans for i in range(start, stop)]
    for j, start, stop in spans:
        cross = three_dots(dot_nt, state_ref[block(j), :LEN], state_ref[start * LEN : stop * LEN, LEN:])
        for n, (j2, i) in enumerate(pairs):
            if j2 == j:
                cross_ref[n] = cross[:, block(i - start)]
                allowed = mask_st(seg_col_ref, seg_row_ref, j, i)
                bias_ref[n] = jnp.where(allowed, 0.0, hidden_bias)
                dcross_ref[n] = jnp.zeros((LEN, LEN), jnp.float32)

    def prelude(hp, _):
        lanes = pl.ds(pl.multiple_of(hp * LEN, LEN), LEN)
        skip = skip_ref[:, lanes]
        gain = gain_ref[:, lanes]
        skip_sum = jnp.zeros((1, LEN), jnp.float32)
        gain_sum = jnp.zeros((1, LEN), jnp.float32)
        for i in chunks:
            at = block(i - first)
            inv = inv_wide_ref[at, :]
            unit = gated_ref[at, lanes] * inv
            grad = inv * (gmr_ref[at, lanes] * gain - unit * dot_wide_ref[at, :])
            gate = gate_ref[block(i), lanes]
            sig = sigmoid(gate)
            y = y_ref[at, lanes]
            x = x_ref[block(i), lanes]
            gy = grad * (gate * sig)
            dgate_ref[at, lanes] = (grad * (y + skip * x) * (sig * (1.0 + gate * (1.0 - sig)))).astype(jnp.bfloat16)
            gyb = gy.astype(jnp.bfloat16)
            gy_ref[at, lanes] = gy
            gyb_ref[at, lanes] = gyb
            high_ref[at, lanes], rest_ref[at, lanes] = two_terms(gyb.astype(jnp.float32) * y)
            skip_sum = skip_sum + jnp.sum(gy * x, axis=0, keepdims=True)
            gain_sum = gain_sum + jnp.sum(gmr_ref[at, lanes] * unit, axis=0, keepdims=True)
        skip_sum_ref[0:1, lanes] = skip_sum
        skip_sum_ref[1:2, lanes] = gain_sum
        return 0

    lax.fori_loop(0, heads // 2, prelude, 0)
    p_ref[...] = dot_nt(select_ref[...], high_ref[...]) + dot_nt(select_ref[...], rest_ref[...])

    def head_pair(hp, _):
        lanes = pl.ds(pl.multiple_of(hp * LEN, LEN), LEN)
        for j, start, stop in spans:
            x_pair = xb_ref[block(j), lanes]
            x_both = jnp.concatenate([jnp.where(left_half, x_pair, zero), jnp.where(left_half, zero, x_pair)], axis=0)
            wide = (stop - start) * LEN
            gy_rows = gyb_ref[(start - first) * LEN : (stop - first) * LEN, lanes]
            inner_ref[:, :wide] = dot_nt(x_both, gy_rows)
            for n, (j2, i) in enumerate(pairs):
                if j2 != j:
                    continue
                grown = dcross_ref[n]
                for e in range(2):
                    spread = cum_row_ref[2 * hp + e, :, block(i)] - wide_ref[2 * hp + e, block(j), :]
                    decay = jnp.exp2(spread + bias_ref[n])
                    grown = grown + inner_ref[block(e), block(i - start)] * decay
                    mix_ref[block(e), block(i - start)] = (decay * cross_ref[n]).astype(jnp.bfloat16)
                dcross_ref[n] = grown
            both = dot_nn(mix_ref[:, :wide], gy_rows)
            dx_ref[block(j), lanes] = jnp.where(left_half, both[:LEN], both[LEN:])
        return 0

    lax.fori_loop(0, heads // 2, head_pair, 0)

    grad_out = {i: jnp.zeros((LEN, LEN), jnp.float32) for i in chunks}
    for j in range(sources):
        grad_in = jnp.zeros((LEN, LEN), jnp.float32)
        for n, (j2, i) in enumerate(pairs):
            if j2 != j:
                continue
            high, rest = two_terms(dcross_ref[n])
            out_high, out_rest = two_terms(state_ref[block(i), LEN:])
            in_high, in_rest = two_terms(state_ref[block(j), :LEN])
            grad_in = grad_in + dot_nn(high, out_high) + dot_nn(high, out_rest) + dot_nn(rest, out_high)
            grad_out[i] = grad_out[i] + dot_tn(high, in_high) + dot_tn(high, in_rest) + dot_tn(rest, in_high)
        grad_in_ref[block(j), :] = grad_in
    for i in chunks:
        grad_out_ref[block(i - first), :] = grad_out[i]


def conv_back(grad_ref, value_pad_ref, keep_ref, kernel_ref, out_ref, kernel_grad_ref, bias_grad_ref, lanes, blocks):
    taps = kernel_ref[:, lanes]
    totals = [jnp.zeros((1, LEN), jnp.float32) for _ in range(5)]
    for i in range(blocks):
        here = grad_ref[i * LEN : (i + 1) * LEN, lanes]
        grad = taps[3:4] * here
        totals[4] = totals[4] + jnp.sum(here, axis=0, keepdims=True)
        totals[3] = totals[3] + jnp.sum(here * value_pad_ref[8 + i * LEN : 8 + (i + 1) * LEN, lanes], axis=0, keepdims=True)
        for lag in (1, 2, 3):
            ahead = grad_ref[i * LEN + lag : (i + 1) * LEN + lag, lanes]
            grad = grad + taps[3 - lag : 4 - lag] * (ahead * keep_ref[lag - 1, i * LEN + lag : (i + 1) * LEN + lag, :])
            moved = value_pad_ref[8 + i * LEN - lag : 8 + (i + 1) * LEN - lag, lanes]
            masked = here * keep_ref[lag - 1, i * LEN : (i + 1) * LEN, :]
            totals[3 - lag] = totals[3 - lag] + jnp.sum(masked * moved, axis=0, keepdims=True)
        out_ref[block(i), lanes] = grad.astype(jnp.bfloat16)
    for tap in range(4):
        kernel_grad_ref[tap : tap + 1, lanes] = totals[tap]
    bias_grad_ref[0:1, lanes] = totals[4]


def scan_end_kernel(
    heads,
    gy_a_ref,
    gy_b_ref,
    dx_a_ref,
    dx_b_ref,
    p_a_ref,
    p_b_ref,
    in_a_ref,
    in_b_ref,
    out_a_ref,
    out_b_ref,
    xb_ref,
    slope_ref,
    state_slope_ref,
    conv_ref,
    small_ref,
    step_row_ref,
    sig_row_ref,
    rate_ref,
    skip_ref,
    keep_ref,
    seg_col_ref,
    seg_row_ref,
    select_ref,
    conv_kernel_ref,
    state_kernel_ref,
    dconv_ref,
    dstate_ref,
    dstep_ref,
    conv_kernel_sum_ref,
    conv_bias_sum_ref,
    state_kernel_sum_ref,
    state_bias_sum_ref,
    step_sum_ref,
    grad_pad_ref,
    value_pad_ref,
    state_grad_ref,
    state_value_ref,
    wide_ref,
    high_ref,
    rest_ref,
    flow_ref,
):
    rows, width = conv_ref.shape
    blocks = rows // LEN
    half = rows // 2
    value_pad_ref[0:8, :] = jnp.zeros((8, width), jnp.float32)
    value_pad_ref[8 : rows + 8, :] = conv_ref[...]
    grad_pad_ref[rows : rows + 8, :] = jnp.zeros((8, width), jnp.float32)
    state_value_ref[0:8, :] = jnp.zeros((8, 2 * LEN), jnp.float32)
    state_value_ref[8 : rows + 8, :] = small_ref[:, : 2 * LEN]
    state_grad_ref[rows : rows + 8, :] = jnp.zeros((8, 2 * LEN), jnp.float32)
    widen(keep_ref, wide_ref)

    def epilogue(hp, _):
        lanes = pl.ds(pl.multiple_of(hp * LEN, LEN), LEN)
        for j in range(blocks):
            dx = dx_b_ref[block(j), lanes]
            if j < blocks // 2:
                dx = dx + dx_a_ref[block(j), lanes]
                gy = gy_a_ref[block(j), lanes]
            else:
                gy = gy_b_ref[block(j - blocks // 2), lanes]
            high_ref[block(j), lanes], rest_ref[block(j), lanes] = two_terms(
                dx * xb_ref[block(j), lanes].astype(jnp.float32)
            )
            grad_pad_ref[block(j), lanes] = (dx + gy * skip_ref[:, lanes]) * slope_ref[block(j), lanes]
        conv_back(
            grad_pad_ref,
            value_pad_ref,
            wide_ref,
            conv_kernel_ref,
            dconv_ref,
            conv_kernel_sum_ref,
            conv_bias_sum_ref,
            lanes,
            blocks,
        )
        return 0

    lax.fori_loop(0, heads // 2, epilogue, 0)

    state_grad_ref[0:half, 0:LEN] = (in_a_ref[...] + in_b_ref[0:half, :]) * state_slope_ref[0:half, 0:LEN]
    state_grad_ref[half:rows, 0:LEN] = in_b_ref[half:rows, :] * state_slope_ref[half:rows, 0:LEN]
    state_grad_ref[0:half, LEN:] = out_a_ref[...] * state_slope_ref[0:half, LEN:]
    state_grad_ref[half:rows, LEN:] = out_b_ref[...] * state_slope_ref[half:rows, LEN:]
    for c in range(2):
        conv_back(
            state_grad_ref,
            state_value_ref,
            wide_ref,
            state_kernel_ref,
            dstate_ref,
            state_kernel_sum_ref,
            state_bias_sum_ref,
            block(c),
            blocks,
        )

    q = dot_nt(select_ref[...], high_ref[...]) + dot_nt(select_ref[...], rest_ref[...])
    flow_ref[:, 0:half] = p_a_ref[...] - q[:, 0:half]
    flow_ref[:, half:rows] = p_b_ref[...] - q[:, half:rows]
    rate = jnp.broadcast_to(rate_ref[...], (LEN, LEN)).T[: flow_ref.shape[0]]
    bias_total = jnp.zeros((flow_ref.shape[0], LEN), jnp.float32)
    decay_total = jnp.zeros((flow_ref.shape[0], LEN), jnp.float32)
    step_sum_ref[...] = jnp.zeros(step_sum_ref.shape, jnp.float32)
    for j in range(blocks):
        log_grad = jnp.zeros((flow_ref.shape[0], LEN), jnp.float32)
        for i in range(j, min(j + 3, blocks)):
            chosen = jnp.where(mask_st(seg_col_ref, seg_row_ref, j, i), 1.0, 0.0).astype(jnp.bfloat16)
            high, rest = two_terms(flow_ref[:, block(i)])
            log_grad = log_grad + dot_nt(high, chosen) + dot_nt(rest, chosen)
        step = step_row_ref[:, block(j)]
        grad_step = jnp.where(step > 1e-30, q[:, block(j)] / step, 0.0) + log_grad * rate
        grad_arg = grad_step * sig_row_ref[:, block(j)]
        bias_total = bias_total + grad_arg
        decay_total = decay_total + log_grad * step
        tall = jnp.concatenate([grad_arg, jnp.zeros((LEN - grad_arg.shape[0], LEN), jnp.float32)], axis=0)
        dstep_ref[block(j), :] = tall.T.astype(jnp.bfloat16)
    count = flow_ref.shape[0]
    step_sum_ref[0:count, :] = jnp.broadcast_to(jnp.sum(bias_total, axis=1, keepdims=True), (count, LEN))
    step_sum_ref[count : 2 * count, :] = jnp.broadcast_to(
        jnp.sum(decay_total * rate, axis=1, keepdims=True), (count, LEN)
    )


def vmem(count):
    return [pl.BlockSpec(memory_space=pltpu.VMEM)] * count


def call(kernel, out_shape, scratch, operands, flops):
    moved = sum(o.size * o.dtype.itemsize for o in operands) + sum(o.size * o.dtype.itemsize for o in out_shape)
    return pl.pallas_call(
        kernel,
        out_shape=out_shape,
        in_specs=vmem(len(operands)),
        out_specs=vmem(len(out_shape)),
        scratch_shapes=scratch,
        compiler_params=pltpu.CompilerParams(vmem_limit_bytes=40 * 1024 * 1024),
        cost_estimate=pl.CostEstimate(flops=flops, bytes_accessed=moved, transcendentals=0),
    )(*operands)


def f32(*shape):
    return jax.ShapeDtypeStruct(shape, jnp.float32)


def b16(*shape):
    return jax.ShapeDtypeStruct(shape, jnp.bfloat16)


HEAD_ROWS = 16


def scan_prep(conv_in, small, *rest):
    rows, width = conv_in.shape
    outs = [
        f32(rows, width),
        b16(rows, width),
        f32(rows, width),
        f32(rows, 2 * LEN),
        f32(rows, 2 * LEN),
        f32(rows, LEN),
        f32(rows, LEN),
        f32(HEAD_ROWS, 1, rows),
        f32(HEAD_ROWS, 1, rows),
        f32(HEAD_ROWS, rows),
        f32(HEAD_ROWS, rows),
        b16(rows, 2 * LEN),
        b16(rows, LEN),
    ]
    scratch = [
        pltpu.VMEM((rows + 8, width), jnp.float32),
        pltpu.VMEM((rows + 8, 2 * LEN), jnp.float32),
        pltpu.VMEM((3, rows + 8, LEN), jnp.float32),
    ]
    return call(prep_kernel, outs, scratch, (conv_in, small, *rest), 10**9)


def scan_forward(chunks, heads, *operands):
    width = operands[0].shape[1]
    rows = LEN * len(chunks)
    count = sum(min(i, 2) + 1 for i in chunks)
    outs = [f32(rows, width), f32(rows, width), f32(1, rows)]
    scratch = [
        pltpu.VMEM((heads, rows, LEN), jnp.float32),
        pltpu.VMEM((count, LEN, LEN), jnp.float32),
        pltpu.VMEM((count, LEN, LEN), jnp.float32),
        pltpu.VMEM((2 * LEN, 3 * LEN), jnp.bfloat16),
        pltpu.VMEM((rows, LEN), jnp.float32),
    ]
    return call(functools.partial(scan_kernel, chunks, heads), outs, scratch, operands, 2 * 10**9)


def attention_forward(chunks, q, kv, seg_col, seg_row):
    rows = LEN * len(chunks)
    outs = [b16(rows, q.shape[1]), f32(8, rows)]
    return call(functools.partial(attention_kernel, chunks), outs, [], (q, kv, seg_col, seg_row), 10**9)


def attention_backward(chunks, final, *operands):
    q = operands[0]
    rows = q.shape[0]
    partial = [f32(rows, LEN), f32(rows, LEN)]
    sums = [pltpu.VMEM((rows, LEN), jnp.float32)] * 2
    outs = [b16(LEN * len(chunks), q.shape[1])] + ([b16(rows, LEN)] if final else partial)
    scratch = (sums if final else []) + [
        pltpu.VMEM((rows, LEN), jnp.bfloat16),
        pltpu.VMEM((HEAD_DIM, rows), jnp.bfloat16),
    ]
    return call(functools.partial(attention_back_kernel, chunks, final), outs, scratch, operands, 2 * 10**9)


def scan_backward(chunks, heads, *operands):
    rows, width = operands[0].shape
    sources = (chunks[-1] + 1) * LEN
    count = sum(min(i, 2) + 1 for i in chunks)
    outs = [
        b16(rows, width),
        f32(rows, width),
        f32(sources, width),
        f32(HEAD_ROWS, rows),
        f32(sources, LEN),
        f32(rows, LEN),
        f32(8, width),
    ]
    scratch = [
        pltpu.VMEM((rows, width), jnp.bfloat16),
        pltpu.VMEM((heads, sources, LEN), jnp.float32),
        pltpu.VMEM((count, LEN, LEN), jnp.float32),
        pltpu.VMEM((count, LEN, LEN), jnp.float32),
        pltpu.VMEM((count, LEN, LEN), jnp.float32),
        pltpu.VMEM((rows, width), jnp.bfloat16),
        pltpu.VMEM((rows, width), jnp.bfloat16),
        pltpu.VMEM((rows, LEN), jnp.float32),
        pltpu.VMEM((rows, LEN), jnp.float32),
        pltpu.VMEM((2 * LEN, 3 * LEN), jnp.float32),
        pltpu.VMEM((2 * LEN, 3 * LEN), jnp.bfloat16),
    ]
    return call(functools.partial(scan_back_kernel, chunks, heads), outs, scratch, operands, 4 * 10**9)


def scan_end(heads, *operands):
    gy = operands[0]
    rows, width = 2 * gy.shape[0], gy.shape[1]
    outs = [
        b16(rows, width),
        b16(rows, 2 * LEN),
        b16(rows, LEN),
        f32(8, width),
        f32(8, width),
        f32(8, 2 * LEN),
        f32(8, 2 * LEN),
        f32(2 * HEAD_ROWS, LEN),
    ]
    scratch = [
        pltpu.VMEM((rows + 8, width), jnp.float32),
        pltpu.VMEM((rows + 8, width), jnp.float32),
        pltpu.VMEM((rows + 8, 2 * LEN), jnp.float32),
        pltpu.VMEM((rows + 8, 2 * LEN), jnp.float32),
        pltpu.VMEM((3, rows + 8, LEN), jnp.float32),
        pltpu.VMEM((rows, width), jnp.bfloat16),
        pltpu.VMEM((rows, width), jnp.bfloat16),
        pltpu.VMEM((HEAD_ROWS, rows), jnp.float32),
    ]
    return call(functools.partial(scan_end_kernel, heads), outs, scratch, operands, 2 * 10**9)


def silu_slope(argument):
    logistic = jax.nn.sigmoid(argument)
    return logistic * (1.0 + argument * (1.0 - logistic))


def rope_tables(rows):
    half_size = HEAD_DIM // 2
    inverse = np.float32(rope_base) ** (-(2.0 * np.arange(half_size, dtype=np.float32)) / HEAD_DIM)
    angles = np.arange(rows, dtype=np.float32)[:, None] * inverse.astype(np.float32)[None, :]
    cosine, sine = np.cos(angles), np.sin(angles)
    return (
        np.concatenate([cosine] * 4, axis=1).astype(np.float32),
        np.concatenate([-sine, sine, -sine, sine], axis=1).astype(np.float32),
    )


def norm_backward(grad_unit, unit_rows, inv_rms):
    return inv_rms * (grad_unit - unit_rows * jnp.mean(grad_unit * unit_rows, axis=-1, keepdims=True))


def dot32(left, right):
    return jnp.dot(left, right, preferred_element_type=jnp.float32)


def swap(values, name):
    return lax.ppermute(values, name, PAIR)


def exchange(values, name):
    return values + swap(values, name)


def take(values, index, axis):
    return lax.dynamic_slice_in_dim(values, index, 1, axis)


def first_halving(values, name, axis, link):
    place = lax.axis_index(name)
    if link == "A":
        side = ((place + 1) // 2) % 2
        kept = jnp.concatenate([take(values, side, axis), take(values, 3 - side, axis)], axis)
        sent = jnp.concatenate([take(values, 1 - side, axis), take(values, 2 + side, axis)], axis)
    else:
        side = place // 2
        kept = lax.dynamic_slice_in_dim(values, 2 * side, 2, axis)
        sent = lax.dynamic_slice_in_dim(values, 2 - 2 * side, 2, axis)
    return kept + lax.ppermute(sent, name, LINKS[link])


def second_halving(values, name, axis, link):
    place = lax.axis_index(name)
    index = place // 2 if link == "B" else place % 2
    sent = take(values, 1 - index, axis)
    return take(values, index, axis) + lax.ppermute(sent, name, LINKS[link])


def either(chosen, first, second, axis):
    return jnp.where(chosen, jnp.concatenate([first, second], axis), jnp.concatenate([second, first], axis))


def second_doubling(values, name, axis, link):
    place = lax.axis_index(name)
    index = place // 2 if link == "B" else place % 2
    return either(index == 0, values, lax.ppermute(values, name, LINKS[link]), axis)


def first_doubling(values, name, axis, link):
    place = lax.axis_index(name)
    other = lax.ppermute(values, name, LINKS[link])
    if link == "B":
        return either(place // 2 == 0, values, other, axis)
    side = ((place + 1) // 2) % 2 == 0
    own = [lax.slice_in_dim(values, k, k + 1, axis=axis) for k in range(2)]
    far = [lax.slice_in_dim(other, k, k + 1, axis=axis) for k in range(2)]
    return jnp.where(
        side,
        jnp.concatenate([own[0], far[0], far[1], own[1]], axis),
        jnp.concatenate([far[0], own[0], own[1], far[1]], axis),
    )


def part_sizes(columns):
    tiles = columns // LEN
    return [LEN * (tiles // 4 + (1 if k < tiles % 4 else 0)) for k in range(4)]


def split_columns(values):
    parts, start = [], 0
    for size in part_sizes(values.shape[-1]):
        parts.append(values[..., start : start + size])
        start += size
    return parts


def reduce_blocks(values):
    count, rows, columns = values.shape
    parts = split_columns(values.reshape(count, 4, 2, 4, rows // 32, columns))
    for step in range(4):
        for k in range(4):
            name, link = ORDERS[k][step]
            seen = [n for n, _ in ORDERS[k][:step]]
            halving = second_halving if name in seen else first_halving
            parts[k] = halving(parts[k], name, AXIS[name], link)
    merged = jnp.concatenate(parts, axis=-1)
    place = lax.axis_index("zh")
    own = take(merged, place, 2) + swap(take(merged, 1 - place, 2), "zh")
    return own.reshape(count, rows // 32, columns)


def gather_rows(values):
    rows, columns = values.shape
    merged = values.reshape(1, 1, 1, 1, rows, columns)
    merged = either(lax.axis_index("zh") == 0, merged, swap(merged, "zh"), 2)
    parts = split_columns(merged)
    for step in reversed(range(4)):
        for k in range(4):
            name, link = ORDERS[k][step]
            seen = [n for n, _ in ORDERS[k][:step]]
            doubling = second_doubling if name in seen else first_doubling
            parts[k] = doubling(parts[k], name, AXIS[name], link)
    merged = jnp.concatenate(parts, axis=-1).reshape(32 * rows, columns)
    return either(lax.axis_index("core") == 0, merged, swap(merged, "core"), 0)


def core_rows(values, index):
    half = values.shape[1] // 2
    return lax.dynamic_slice_in_dim(values, index * half, half, 1)


def core_dot(left, right):
    place = lax.axis_index("core")

    def rows_of(index):
        return lax.dot_general(
            core_rows(left, index), right, (((0,), (0,)), ((), ())), preferred_element_type=jnp.float32
        )

    return rows_of(place) + swap(rows_of(1 - place), "core")


def on_device(
    layer_input,
    segments,
    input_gain,
    mixer_proj,
    state_proj,
    step_proj,
    step_bias,
    decay_log,
    skip_gain,
    conv_kernel,
    conv_bias,
    state_kernel,
    state_bias,
    gated_gain,
    mixer_out,
    query_proj,
    key_value_weight,
    attn_out,
    ffn_gain,
    ffn_gate,
    ffn_up,
    ffn_down,
    cotangent,
):
    segment = segments.reshape(-1)
    rows, model_width = layer_input.shape
    width = mixer_proj.shape[2]
    heads = step_proj.shape[1]
    state_size = state_proj.shape[1] // 2
    query_width = query_proj.shape[1]
    pair_width = key_value_weight.shape[2]
    cosine, sine = rope_tables(rows)
    select = np.arange(HEAD_ROWS)[:, None] == np.arange(width)[None, :] // HEAD_DIM
    select = jnp.asarray(select.astype(np.float32)).astype(jnp.bfloat16)
    seg_col, seg_row = segment[:, None], segment[None, :]
    keep = [jnp.ones((rows,), jnp.float32)]
    for lag in (1, 2, 3):
        previous = jnp.concatenate([jnp.full((lag,), -1, jnp.int32), segment[:-lag]])
        keep.append((previous == segment).astype(jnp.float32))
    keep = jnp.pad(jnp.stack(keep, axis=1), ((0, 8), (0, 4)))
    pad_heads = ((0, 0), (0, LEN - heads))
    rate_row = jnp.pad(-jnp.exp(decay_log)[None, :], pad_heads)
    step_bias_row = jnp.pad(step_bias[None, :], pad_heads)
    skip_row = jnp.repeat(skip_gain, HEAD_DIM)[None, :]
    gain_row = gated_gain[None, :]
    gate_proj, channel_proj = mixer_proj[:, 0, :], mixer_proj[:, 1, :]
    small_proj = jnp.concatenate(
        [
            state_proj,
            query_proj,
            key_value_weight.reshape(model_width, pair_width),
            step_proj,
            jnp.zeros((model_width, LEN - heads), jnp.bfloat16),
        ],
        axis=1,
    )

    tokens = layer_input.astype(jnp.float32)
    inv_rms_in = lax.rsqrt(jnp.mean(tokens * tokens, axis=-1, keepdims=True) + norm_eps)
    unit_in = tokens * inv_rms_in
    normed_input = (unit_in * input_gain).astype(jnp.bfloat16)
    small_in = dot32(normed_input, small_proj)
    conv_in = dot32(normed_input, channel_proj)
    gate_branch = dot32(normed_input, gate_proj)
    x, xb, slope, state, state_slope, cum, lag, cum_row, lag_row, step_row, sig_row, queries, pairs = scan_prep(
        conv_in,
        small_in,
        cosine,
        sine,
        keep,
        conv_kernel,
        conv_bias[None, :],
        state_kernel,
        state_bias[None, :],
        step_bias_row,
        rate_row,
    )

    blocks = rows // LEN
    late = tuple(range(blocks // 2, blocks))
    early = tuple(range(blocks // 2))
    half = {}
    for chunks in (late, early):
        span = slice(chunks[0] * LEN, (chunks[-1] + 1) * LEN)
        h = {"span": span}
        h["y"], h["gated"], squares = scan_forward(
            chunks, heads, gate_branch, x, xb, state, cum, lag_row, seg_col, seg_row, skip_row
        )
        h["attended"], h["lse"] = attention_forward(chunks, queries, pairs, seg_col, seg_row)
        squares = exchange(squares, "tensor")
        h["inv_gated"] = lax.rsqrt(squares.reshape(-1, 1) / DSSM + norm_eps)
        h["mixer_rows"] = (h["gated"] * h["inv_gated"] * gated_gain).astype(jnp.bfloat16)
        h["branch"] = exchange(dot32(h["mixer_rows"], mixer_out) + dot32(h["attended"], attn_out), "tensor")
        half[chunks] = h

    for chunks in (late, early):
        h = half[chunks]
        span = h["span"]
        hidden = tokens[span] + h["branch"]
        inv_rms_ffn = lax.rsqrt(jnp.mean(hidden * hidden, axis=-1, keepdims=True) + norm_eps)
        unit_ffn = hidden * inv_rms_ffn
        normed_ffn = (unit_ffn * ffn_gain).astype(jnp.bfloat16)
        gate_rows = dot32(normed_ffn, ffn_gate)
        up_rows = dot32(normed_ffn, ffn_up)
        gate_silu = jax.nn.silu(gate_rows)
        activated = (gate_silu * up_rows).astype(jnp.bfloat16)
        grad_activated = dot32(cotangent[span], ffn_down.T)
        grad_gate_rows = (grad_activated * up_rows * silu_slope(gate_rows)).astype(jnp.bfloat16)
        grad_up_rows = (grad_activated * gate_silu).astype(jnp.bfloat16)
        partial_ffn = dot32(grad_gate_rows, ffn_gate.T) + dot32(grad_up_rows, ffn_up.T)
        h["grad_normed_ffn"] = exchange(partial_ffn, "tensor")
        h["down"] = dot32(activated, ffn_down)
        h.update(
            hidden=hidden,
            unit_ffn=unit_ffn,
            inv_rms_ffn=inv_rms_ffn,
            normed_ffn=normed_ffn,
            activated=activated,
            grad_gate_rows=grad_gate_rows,
            grad_up_rows=grad_up_rows,
        )

    def whole(name):
        return jnp.concatenate([half[early][name], half[late][name]], axis=0)

    normed_ffn = whole("normed_ffn")
    first = reduce_blocks(
        jnp.stack(
            [
                core_dot(normed_ffn, whole("grad_gate_rows")),
                core_dot(normed_ffn, whole("grad_up_rows")),
                core_dot(whole("activated"), cotangent),
            ]
        )
    )
    first = lax.all_gather(first, ("core", "y", "zh", "x"), axis=1, tiled=True)

    grad_ffn_gain = 0.0
    for chunks in (late, early):
        h = half[chunks]
        span = h["span"]
        grad_ffn_gain = grad_ffn_gain + jnp.sum(h["grad_normed_ffn"] * h["unit_ffn"], axis=0)
        h["grad_hidden"] = cotangent[span].astype(jnp.float32) + norm_backward(
            h["grad_normed_ffn"] * ffn_gain, h["unit_ffn"], h["inv_rms_ffn"]
        )
        grad_branch = h["grad_hidden"].astype(jnp.bfloat16)
        h["grad_branch"] = grad_branch
        grad_mixer_rows = dot32(grad_branch, mixer_out.T)
        unit_gated = h["gated"] * h["inv_gated"]
        gated_dot = exchange(jnp.sum(grad_mixer_rows * gated_gain * unit_gated, axis=-1)[None, :], "tensor")
        grad_attended = dot32(grad_branch, attn_out.T).astype(jnp.bfloat16)
        operands = (queries, pairs, grad_attended, h["lse"], seg_col, seg_row, cosine, sine)
        if chunks == late:
            h["grad_queries"], grad_keys, grad_values = attention_backward(chunks, False, *operands)
        else:
            h["grad_queries"], grad_pairs = attention_backward(chunks, True, *operands, grad_keys, grad_values)
        h["grad_gate"], h["gy"], h["dx"], h["p"], h["grad_in"], h["grad_out"], h["sums"] = scan_backward(
            chunks,
            heads,
            grad_mixer_rows,
            h["gated"],
            h["inv_gated"],
            gated_dot.reshape(-1, 1) / DSSM,
            gain_row,
            gate_branch,
            h["y"],
            x,
            xb,
            state,
            lag,
            cum_row,
            skip_row,
            seg_col,
            seg_row,
            select,
        )
    ends = []
    for name in ("gy", "dx", "p", "grad_in", "grad_out"):
        ends += [half[early][name], half[late][name]]
    grad_conv, grad_state, grad_step, conv_kernel_sum, conv_bias_sum, state_kernel_sum, state_bias_sum, step_sum = scan_end(
        heads,
        *ends,
        xb,
        slope,
        state_slope,
        conv_in,
        small_in,
        step_row,
        sig_row,
        rate_row,
        skip_row,
        keep,
        seg_col,
        seg_row,
        select,
        conv_kernel,
        state_kernel,
    )

    left = jnp.concatenate([whole("mixer_rows"), whole("attended")], axis=1)
    right = jnp.concatenate([whole("grad_gate"), whole("grad_queries"), grad_pairs], axis=1)
    second = jnp.concatenate([core_dot(left, whole("grad_branch")), core_dot(normed_input, right)], axis=1)
    second = gather_rows(reduce_blocks(second[None])[0])

    grad_small = jnp.concatenate([grad_state, whole("grad_queries"), grad_pairs, grad_step], axis=1)
    partial_normed = (
        dot32(whole("grad_gate"), gate_proj.T) + dot32(grad_small, small_proj.T) + dot32(grad_conv, channel_proj.T)
    )
    sums = half[early]["sums"] + half[late]["sums"]
    over_tensor = [jnp.sum(partial_normed * unit_in, axis=0), state_kernel_sum[:4], state_bias_sum[0]]
    alone = [
        step_sum[:heads, 0],
        step_sum[HEAD_ROWS : HEAD_ROWS + heads, 0],
        jnp.sum(sums[0].reshape(heads, HEAD_DIM), axis=1),
        conv_kernel_sum[:4],
        conv_bias_sum[0],
        sums[1],
        grad_ffn_gain,
    ]

    def packed(values):
        flat = jnp.concatenate([v.reshape(-1) for v in values])
        count = -(-flat.shape[0] // model_width)
        return jnp.pad(flat, (0, count * model_width - flat.shape[0])).reshape(count, model_width)

    def unpacked(table, values):
        flat, result, start = table.T.reshape(-1), [], 0
        for v in values:
            result.append(flat[start : start + v.size].reshape(v.shape))
            start += v.size
        return result

    tables = [packed(over_tensor), packed(alone)]
    shared_end = heads + tables[0].shape[0]
    table = jnp.concatenate(tables, axis=0)
    table_end = heads + table.shape[0]
    place = lax.axis_index("core")
    table = (core_rows(table, place) + swap(core_rows(table, 1 - place), "core")).T
    third = core_dot(normed_input, jnp.concatenate([grad_conv, grad_state, grad_step], axis=1))
    at_state, at_step = width, width + 2 * state_size
    third = third + jnp.pad(table, ((0, 0), (at_step + heads, LEN - table_end)))
    third = reduce_blocks(third[None])[0]
    both = third[:, at_state:]
    summed = exchange(both, "tensor")
    lane = np.arange(both.shape[1]) - 2 * state_size
    is_shared = (lane < 0) | ((lane >= heads) & (lane < shared_end))
    third = jnp.concatenate([third[:, :at_state], jnp.where(is_shared[None, :], summed, both)], axis=1)
    third = gather_rows(third)

    grad_normed = exchange(partial_normed, "tensor")
    grad_hidden = whole("grad_hidden")
    input_grad = grad_hidden + norm_backward(grad_normed * input_gain, unit_in, inv_rms_in)
    layer_output = (whole("hidden") + exchange(whole("down"), "tensor")).astype(jnp.bfloat16)

    small_shared = unpacked(third[:, at_step + heads : at_step + shared_end], over_tensor)
    small_alone = unpacked(third[:, at_step + shared_end : at_step + table_end], alone)
    at_gate = model_width
    at_query = at_gate + width
    at_pair = at_query + query_width
    return (
        layer_output,
        input_grad,
        small_shared[0],
        jnp.stack([second[:, at_gate:at_query], third[:, :width]], axis=1),
        third[:, at_state:at_step],
        third[:, at_step : at_step + heads],
        small_alone[0],
        small_alone[1],
        small_alone[2],
        small_alone[3],
        small_alone[4],
        small_shared[1],
        small_shared[2],
        small_alone[5],
        second[:width, :model_width],
        second[:, at_query:at_pair],
        second[:, at_pair:].reshape(key_value_weight.shape),
        second[width:, :model_width],
        small_alone[6],
        first[0],
        first[1],
        first[2],
    )


def solution(mesh):
    dp, whole_spec, columns = P(DP, None), P(), P(None, "tensor")
    per_channel, middle = P("tensor"), P(None, "tensor", None)
    last, by_rows = P(None, None, "tensor"), P("tensor", None)
    weights = (
        whole_spec,
        last,
        whole_spec,
        columns,
        per_channel,
        per_channel,
        per_channel,
        columns,
        per_channel,
        whole_spec,
        whole_spec,
        per_channel,
        by_rows,
        columns,
        middle,
        by_rows,
        whole_spec,
        columns,
        columns,
        by_rows,
    )
    mesh = jax.sharding.Mesh(mesh.devices.reshape(4, 2, 4, 2, 2), (*DP, "tensor"))
    return jax.shard_map(
        on_device, mesh=mesh, in_specs=(dp, dp, *weights, dp), out_specs=(dp, dp, *weights), check_vma=False
    )
```

time: 692 us -> 748 us (1.081)
  waiting for transfers between devices: 360 us -> 256 us
  starting transfers between devices: 54.9 us -> 150 us
  local copies, waits for them, and re-layouts: 86.5 us -> 145 us
  matrix products: 109 us -> 61 us
  Pallas kernels: 0 us -> 33.1 us
  other arithmetic: 59.9 us -> 74.6 us
    all_gather x2 -> x1, waiting for transfers between devices: 81.2 us -> 0.01 us  [on_device(): first = lax.all_gather(first, ('core', 'y', 'zh', 'x'), axis=1, tiled=True)]
    ppermute x12 -> x57, starting transfers between devices: 29 us -> 103 us  [the longest x25 75.6 us: swap(): return lax.ppermute(values, name, PAIR)]
    unnamed x303 -> x453, local copies, waits for them, and re-layouts: 12.7 us -> 72.3 us
    ppermute x12 -> x57, waiting for transfers between devices: 192 us -> 143 us  [the longest x25 104 us: swap(): return lax.ppermute(values, name, PAIR)]
    dot_general x36 -> x38, matrix products: 109 us -> 61 us  [the longest x26 31.9 us: dot32(): return jnp.dot(left, right, preferred_element_type=jnp.float32)]
    ppermute x16 -> x24, waiting for transfers between devices: 27.6 us -> 65.1 us  [second_halving(): return take(values, index, axis) + lax.ppermute(sent, name, LINKS[link])]
    pallas_call x0 -> x10, Pallas kernels: none -> 33.1 us  [call(): pl.pallas_call(kernel, out_shape=out_shape, in_specs=vmem(len(operands)),...]
    select_n x1 -> x41, other arithmetic: 0.63 us -> 26 us  [the longest x28 25 us: either(): jnp.where(chosen, jnp.concatenate([first, second], axis), jnp.concatenate...]
  transfers between devices with their start and end apart: 46 -> 106, of which waited for: 29 -> 48; matrix products, arithmetic and copies ran while one was open for 12% -> 24% of each run, Pallas kernels for 0% -> 4%
where the time goes in v2:
time: 748 us; the launch traced here: 738 us
  waiting for transfers between devices  256 us (34%)
  starting transfers between devices  150 us (20%)
  local copies, waits for them, and re-layouts  145 us (19%)
  other arithmetic  74.6 us (10%)
  matrix products  61 us (8%)
  Pallas kernels  33.1 us (4%)
  between operations  18.3 us (2%)
    ppermute x25, waiting for transfers between devices, swap(): return lax.ppermute(values, name, PAIR)  104 us
    ppermute x25, starting transfers between devices, swap(): return lax.ppermute(values, name, PAIR)  75.6 us
    unnamed x453, local copies, waits for them, and re-layouts  72.3 us
    ppermute x24, waiting for transfers between devices, second_halving(): return take(values, index, axis) + lax.ppermute(sent, name, LINKS[link])  65.1 us
    ppermute x24, waiting for transfers between devices, first_halving(): return kept + lax.ppermute(sent, name, LINKS[link])  48.6 us
    pallas_call x10, Pallas kernels, call(): pl.pallas_call(kernel, out_shape=out_shape, in_specs=vmem(len(operands)),...  33.1 us
    dot_general x26, matrix products, dot32(): return jnp.dot(left, right, preferred_element_type=jnp.float32)  31.9 us
    dot_general x12, matrix products, rows_of(): lax.dot_general(core_rows(left, index), right, (((0,), (0,)), ((), ())),...  29 us
  transfers between devices with their start and end apart: 106, of which 48 were waited for; matrix products, arithmetic and copies ran while one was open for 24% of the time, Pallas kernels for 4%

profile of v2, /device:TPU:1, one launch (start us, length us, event | category | flops | bytes accessed | tf_op | source)
XLA Modules:
  0.0 737.8 jit_solution(6931817693855817688)
XLA Ops:
  8.9 7.6 %fusion.91 = (bf16[1024,1,768]{2,1,0:T(2,128)(2,1)S(1)}, bf16[1024,1,768]{2,1,0:T(2,128)(2,1)S(1)}) fusion(bf16[1024,2,768]{2,1,0:T(2,128)(2,1)} %param.30), kind=kLoop, calls=%fused_computation.465 | loop fusion | bytes 6291456 | tf_op jit(solution)/shard_map/slice | solution.py:958
  22.8 3.6 concatenate.1518
  26.5 3.9 fusion.111.small_ref
  34.1 3.7 shard_map.426
  61.0 18.6 %collective-permute-done.1 = f32[256,1024]{1,0:T(8,128)S(1)} collective-permute-done((f32[256,1024]{1,0:T(8,128)S(1)}, f32[256,1024]{1,0:T(8,128)S(1)}, u32[]{:S(2)}, u32[]{:S(2)}) %collective-permute-start.1) | collective-permute-done | bytes 1048608 | tf_op jit(solution)/shard_map/ppermute | solution.py:797
  79.6 22.5 %collective-permute-done.3 = f32[256,1024]{1,0:T(8,128)S(1)} collective-permute-done((f32[256,1024]{1,0:T(8,128)S(1)}, f32[256,1024]{1,0:T(8,128)S(1)}, u32[]{:S(2)}, u32[]{:S(2)}) %collective-permute-start.3) | collective-permute-done | bytes 1048608 | tf_op jit(solution)/shard_map/ppermute | solution.py:797
  111.5 3.5 fusion.28
  122.2 10.7 %collective-permute-done.5 = f32[256,1024]{1,0:T(8,128)} collective-permute-done((f32[256,1024]{1,0:T(8,128)}, f32[256,1024]{1,0:T(8,128)}, u32[]{:S(2)}, u32[]{:S(2)}) %collective-permute-start.5) | collective-permute-done | bytes 1048608 | tf_op jit(solution)/shard_map/ppermute | solution.py:797
  153.6 7.6 %collective-permute-done.6 = f32[256,1024]{1,0:T(8,128)S(1)} collective-permute-done((f32[256,1024]{1,0:T(8,128)S(1)}, f32[256,1024]{1,0:T(8,128)S(1)}, u32[]{:S(2)}, u32[]{:S(2)}) %collective-permute-start.6) | collective-permute-done | bytes 1048608 | tf_op jit(solution)/shard_map/ppermute | solution.py:797
  161.7 3.7 fusion.88
  178.1 28.2 %collective-permute-done.7 = f32[1,256]{1,0:T(1,128)S(1)} collective-permute-done((f32[1,256]{1,0:T(1,128)S(1)}, f32[1,256]{1,0:T(1,128)S(1)}, u32[]{:S(2)}, u32[]{:S(2)}) %collective-permute-start.7) | collective-permute-done | bytes 1056 | tf_op jit(solution)/shard_map/ppermute | solution.py:797
  209.4 4.4 collective-permute-start.48
  224.3 4.0 shard_map.431
  233.8 5.5 shard_map.432
  265.4 4.9 shard_map.433
  305.8 14.5 %collective-permute-done.100 = f32[3,2,2,4,16,256]{5,4,3,2,1,0:T(8,128)S(1)} collective-permute-done((f32[3,2,2,4,16,256]{5,4,3,2,1,0:T(8,128)S(1)}, f32[3,2,2,4,16,256]{5,4,3,2,1,0:T(8,128)S(1)}, u32[]{:S(2)}, u32[]{:S(2)}) %collective-permute-start.100) | collective-permute-done | bytes 786464 | tf_op jit(solution)/shard_map/ppermute | solution.py:818
  325.8 13.8 %collective-permute-done.92 = f32[3,4,2,2,16,256]{5,4,3,2,1,0:T(8,128)S(1)} collective-permute-done((f32[3,4,2,2,16,256]{5,4,3,2,1,0:T(8,128)S(1)}, f32[3,4,2,2,16,256]{5,4,3,2,1,0:T(8,128)S(1)}, u32[]{:S(2)}, u32[]{:S(2)}) %collective-permute-start.92) | collective-permute-done | bytes 786464 | tf_op jit(solution)/shard_map/ppermute | solution.py:818
  347.8 3.8 convolution_add_fusion.5
  358.3 7.2 collective-permute-done.97
  371.3 5.2 collective-permute-done.89
  398.3 4.9 collective-permute-done.99
  426.9 3.7 collective-permute-done.25
  433.1 3.5 collective-permute-done.17
  438.3 3.5 collective-permute-done.21
  446.8 6.3 collective-permute-done.26
  453.4 3.6 collective-permute-done.22
  457.0 4.7 collective-permute-done.18
  478.3 6.1 collective-permute-done.50
  488.5 3.6 collective-permute-done.15
  507.9 3.7 collective-permute-done.30
  512.6 5.2 collective-permute-done.56
  535.9 5.0 collective-permute-done.41
  546.9 5.0 collective-permute-done.53
  552.0 3.5 collective-permute-start.66
  575.7 32.9 %collective-permute-start.47 = (f32[512,1152]{1,0:T(8,128)}, f32[512,1152]{1,0:T(8,128)}, u32[]{:S(2)}, u32[]{:S(2)}) collective-permute-start(f32[512,1152]{1,0:T(8,128)} %pad_maximum_fusion.4), channel_id=1, source_target_pairs={{0,2},{2,0},{1,3},{3,1},{4,6},{6,4},{5,7},{7,5},{8,10},{10,8},{9,1... | collective-permute-start | bytes 7077896 | tf_op jit(solution)/shard_map/ppermute | solution.py:797
  613.6 6.5 collective-permute-done.78
  623.9 4.7 collective-permute-done.70
  628.7 4.6 collective-permute-done.83
  634.1 6.3 collective-permute-done.75
  640.6 5.7 collective-permute-done.71
  649.3 4.4 collective-permute-start.84
  653.7 3.9 fusion.1
  660.1 8.0 %maximum_select_fusion.1 = f32[1024,1152]{1,0:T(8,128)} fusion(f32[512,1152]{1,0:T(8,128)} %collective-permute-done.47, f32[512,256]{1,0:T(8,128)S(1)} %bitcast.321, f32[512,256]{1,0:T(8,128)S(1)} %bitcast.323, f32[512,256]{1,0:T(8,128)} %bitcast.325, f32[512,384]{1,0:T(8,128)S(1)} %bitcast.319, pred[]{:T(512)S(6)} %eq.112), kind=kLoop, calls=%fused_computation.3 | loop fusion | flops 10616832 | bytes 9437185 | tf_op jit(solution)/shard_map/jit(_where)/select_n | solution.py:829
  679.1 3.9 slice_bitcast_fusion.3
  683.0 16.3 %maximum_select_fusion = f32[1024,2176]{1,0:T(8,128)} fusion(f32[512,2176]{1,0:T(8,128)} %collective-permute-done.84, f32[512,512]{1,0:T(8,128)S(1)} %bitcast.310, f32[512,512]{1,0:T(8,128)S(1)} %bitcast.312, f32[512,512]{1,0:T(8,128)S(1)} %bitcast.308, f32[512,640]{1,0:T(8,128)S(1)} %bitcast.306, pred[]{:T(512)S(6)} %eq.112), kind=kLoop, calls=%fused_computation | loop fusion | flops 20054016 | bytes 17825792 | tf_op jit(solution)/shard_map/jit(_where)/select_n | solution.py:829
  699.3 4.0 slice.568
  712.9 7.6 %copy.249 = f32[1024,2,768]{2,1,0:T(2,128)} copy(f32[1024,2,768]{2,0,1:T(8,128)S(1)} %pad_maximum_fusion) | data formatting | bytes 12582912
  720.5 10.3 %slice_bitcast_fusion = (f32[1024,1024]{1,0:T(8,128)}, f32[1024,1024]{1,0:T(8,128)}, f32[1024,1024]{1,0:T(8,128)}) fusion(f32[3,1,1,1,1024,1024]{5,4,3,2,1,0:T(8,128)} %all-gather.3.cloned.1.call-done), kind=kLoop, calls=%fused_computation.6 | loop fusion | bytes 25165824 | tf_op jit(solution)/shard_map/squeeze | solution.py:1194
  (983 shorter events, 361.7 us)
Async XLA Ops:
  7.2 713.3 %all-gather.3.cloned.1.call-start = ((), (), s32[]{:S(2)}) async-start(), calls=%async_computation | async-start | bytes 12779520 | tf_op jit(solution)/shard_map/all_gather | solution.py:1048
  55.8 23.8 %collective-permute-start.1 = (f32[256,1024]{1,0:T(8,128)S(1)}, f32[256,1024]{1,0:T(8,128)S(1)}, u32[]{:S(2)}, u32[]{:S(2)}) collective-permute-start(f32[256,1024]{1,0:T(8,128)S(1)} %convolution_add_fusion.7), channel_id=1, source_target_pairs={{0,1},{1,0},{2,3},{3,2},{4,5},{5,4},{6,7},{7,6},{8,9},{9,8},{10,11... | collective-permute-start | bytes 3145736 | tf_op jit(solution)/shard_map/ppermute | solution.py:797
  58.3 43.8 %collective-permute-start.3 = (f32[256,1024]{1,0:T(8,128)S(1)}, f32[256,1024]{1,0:T(8,128)S(1)}, u32[]{:S(2)}, u32[]{:S(2)}) collective-permute-start(f32[256,1024]{1,0:T(8,128)S(1)} %convolution_add_fusion.6), channel_id=1, source_target_pairs={{0,1},{1,0},{2,3},{3,2},{4,5},{5,4},{6,7},{7,6},{8,9},{9,8},{10,11... | collective-permute-start | bytes 3145736 | tf_op jit(solution)/shard_map/ppermute | solution.py:797
  109.3 23.5 %collective-permute-start.5 = (f32[256,1024]{1,0:T(8,128)}, f32[256,1024]{1,0:T(8,128)}, u32[]{:S(2)}, u32[]{:S(2)}) collective-permute-start(f32[256,1024]{1,0:T(8,128)} %convolution_add_fusion.9), channel_id=1, source_target_pairs={{0,1},{1,0},{2,3},{3,2},{4,5},{5,4},{6,7},{7,6},{8,9},{9,8},{10,11... | collective-permute-start | bytes 3145736 | tf_op jit(solution)/shard_map/ppermute | solution.py:797
  139.2 21.9 %collective-permute-start.6 = (f32[256,1024]{1,0:T(8,128)S(1)}, f32[256,1024]{1,0:T(8,128)S(1)}, u32[]{:S(2)}, u32[]{:S(2)}) collective-permute-start(f32[256,1024]{1,0:T(8,128)S(1)} %convolution_add_fusion.8), channel_id=1, source_target_pairs={{0,1},{1,0},{2,3},{3,2},{4,5},{5,4},{6,7},{7,6},{8,9},{9,8},{10,11... | collective-permute-start | bytes 3145736 | tf_op jit(solution)/shard_map/ppermute | solution.py:797
  142.6 511.1 %collective-permute-start.4 = (f32[512,1024]{1,0:T(8,128)}, f32[512,1024]{1,0:T(8,128)}, u32[]{:S(2)}, u32[]{:S(2)}) collective-permute-start(f32[512,1024]{1,0:T(8,128)} %pad_maximum_fusion.5), channel_id=1, source_target_pairs={{0,1},{1,0},{2,3},{3,2},{4,5},{5,4},{6,7},{7,6},{8,9},{9,8},{10,11... | collective-permute-start | bytes 6291464 | tf_op jit(solution)/shard_map/ppermute | solution.py:797
  145.5 147.5 %collective-permute-start.87 = (f32[512,1024]{1,0:T(8,128)}, f32[512,1024]{1,0:T(8,128)}, u32[]{:S(2)}, u32[]{:S(2)}) collective-permute-start(f32[512,1024]{1,0:T(8,128)} %fusion.19), channel_id=1, source_target_pairs={{0,2},{2,0},{1,3},{3,1},{4,6},{6,4},{5,7},{7,5},{8,10},{10,8},{9,1... | collective-permute-start | bytes 6291464 | tf_op jit(solution)/shard_map/ppermute | solution.py:797
  151.0 138.3 %collective-permute-start.86 = (f32[512,1024]{1,0:T(8,128)}, f32[512,1024]{1,0:T(8,128)}, u32[]{:S(2)}, u32[]{:S(2)}) collective-permute-start(f32[512,1024]{1,0:T(8,128)} %fusion.12), channel_id=1, source_target_pairs={{0,2},{2,0},{1,3},{3,1},{4,6},{6,4},{5,7},{7,5},{8,10},{10,8},{9,1... | collective-permute-start | bytes 6291464 | tf_op jit(solution)/shard_map/ppermute | solution.py:797
  153.1 142.4 %collective-permute-start.85 = (f32[512,1024]{1,0:T(8,128)}, f32[512,1024]{1,0:T(8,128)}, u32[]{:S(2)}, u32[]{:S(2)}) collective-permute-start(f32[512,1024]{1,0:T(8,128)} %fusion.13), channel_id=1, source_target_pairs={{0,2},{2,0},{1,3},{3,1},{4,6},{6,4},{5,7},{7,5},{8,10},{10,8},{9,1... | collective-permute-start | bytes 6291464 | tf_op jit(solution)/shard_map/ppermute | solution.py:797
  169.7 36.5 %collective-permute-start.7 = (f32[1,256]{1,0:T(1,128)S(1)}, f32[1,256]{1,0:T(1,128)S(1)}, u32[]{:S(2)}, u32[]{:S(2)}) collective-permute-start(f32[1,256]{1,0:T(1,128)S(1)} %bitcast.363), channel_id=1, source_target_pairs={{0,1},{1,0},{2,3},{3,2},{4,5},{5,4},{6,7},{7,6},{8,9},{9,8},{10,11... | collective-permute-start | bytes 3080 | tf_op jit(solution)/shard_map/ppermute | solution.py:797
  209.4 137.9 %collective-permute-start.48 = (f32[512,1024]{1,0:T(8,128)}, f32[512,1024]{1,0:T(8,128)}, u32[]{:S(2)}, u32[]{:S(2)}) collective-permute-start(f32[512,1024]{1,0:T(8,128)} %fusion.14), channel_id=1, source_target_pairs={{0,2},{2,0},{1,3},{3,1},{4,6},{6,4},{5,7},{7,5},{8,10},{10,8},{9,1... | collective-permute-start | bytes 6291464 | tf_op jit(solution)/shard_map/ppermute | solution.py:797
  289.3 55.1 %collective-permute-start.9 = (f32[512,1024]{1,0:T(8,128)S(1)}, f32[512,1024]{1,0:T(8,128)S(1)}, u32[]{:S(2)}, u32[]{:S(2)}) collective-permute-start(f32[512,1024]{1,0:T(8,128)S(1)} %add_add_fusion), channel_id=1, source_target_pairs={{0,1},{1,0},{2,3},{3,2},{4,5},{5,4},{6,7},{7,6},{8,9},{9,8},{10,11... | collective-permute-start | bytes 6291464 | tf_op jit(solution)/shard_map/ppermute | solution.py:797
  300.1 20.3 %collective-permute-start.100 = (f32[3,2,2,4,16,256]{5,4,3,2,1,0:T(8,128)S(1)}, f32[3,2,2,4,16,256]{5,4,3,2,1,0:T(8,128)S(1)}, u32[]{:S(2)}, u32[]{:S(2)}) collective-permute-start(f32[3,2,2,4,16,256]{5,4,3,2,1,0:T(8,128)S(1)} %constant_dynamic-slice_fusion.7), channel_id=1, source_target_pairs={{32,64},{64,32},{96,0},{0,96},{33,65},{65,33},{97,1},{1,97},{34,66... | collective-permute-start | bytes 2359304 | tf_op jit(solution)/shard_map/ppermute | solution.py:818
  303.1 19.9 %collective-permute-start.96 = (f32[3,2,2,4,16,256]{5,4,3,2,1,0:T(8,128)S(1)}, f32[3,2,2,4,16,256]{5,4,3,2,1,0:T(8,128)S(1)}, u32[]{:S(2)}, u32[]{:S(2)}) collective-permute-start(f32[3,2,2,4,16,256]{5,4,3,2,1,0:T(8,128)S(1)} %pad_maximum_fusion.11), channel_id=1, source_target_pairs={{0,32},{32,0},{64,96},{96,64},{1,33},{33,1},{65,97},{97,65},{2,34}... | collective-permute-start | bytes 2359304 | tf_op jit(solution)/shard_map/ppermute | solution.py:818
  320.3 19.2 %collective-permute-start.92 = (f32[3,4,2,2,16,256]{5,4,3,2,1,0:T(8,128)S(1)}, f32[3,4,2,2,16,256]{5,4,3,2,1,0:T(8,128)S(1)}, u32[]{:S(2)}, u32[]{:S(2)}) collective-permute-start(f32[3,4,2,2,16,256]{5,4,3,2,1,0:T(8,128)S(1)} %constant_dynamic-slice_fusion.24), channel_id=1, source_target_pairs={{4,8},{8,4},{12,0},{0,12},{5,9},{9,5},{13,1},{1,13},{6,10},{10,6},... | collective-permute-start | bytes 2359304 | tf_op jit(solution)/shard_map/ppermute | solution.py:818
  323.0 20.3 %collective-permute-start.88 = (f32[3,4,2,2,16,256]{5,4,3,2,1,0:T(8,128)S(1)}, f32[3,4,2,2,16,256]{5,4,3,2,1,0:T(8,128)S(1)}, u32[]{:S(2)}, u32[]{:S(2)}) collective-permute-start(f32[3,4,2,2,16,256]{5,4,3,2,1,0:T(8,128)S(1)} %pad_maximum_fusion.10), channel_id=1, source_target_pairs={{0,4},{4,0},{8,12},{12,8},{1,5},{5,1},{9,13},{13,9},{2,6},{6,2},{1... | collective-permute-start | bytes 2359304 | tf_op jit(solution)/shard_map/ppermute | solution.py:818
  339.6 38.0 %collective-permute-start.10 = (f32[512,1152]{1,0:T(8,128)}, f32[512,1152]{1,0:T(8,128)}, u32[]{:S(2)}, u32[]{:S(2)}) collective-permute-start(f32[512,1152]{1,0:T(8,128)} %fusion.33), channel_id=1, source_target_pairs={{0,2},{2,0},{1,3},{3,1},{4,6},{6,4},{5,7},{7,5},{8,10},{10,8},{9,1... | collective-permute-start | bytes 7077896 | tf_op jit(solution)/shard_map/ppermute | solution.py:797
  343.3 39.8 %collective-permute-start.49 = (f32[512,1152]{1,0:T(8,128)}, f32[512,1152]{1,0:T(8,128)}, u32[]{:S(2)}, u32[]{:S(2)}) collective-permute-start(f32[512,1152]{1,0:T(8,128)} %fusion.27), channel_id=1, source_target_pairs={{0,2},{2,0},{1,3},{3,1},{4,6},{6,4},{5,7},{7,5},{8,10},{10,8},{9,1... | collective-permute-start | bytes 7077896 | tf_op jit(solution)/shard_map/ppermute | solution.py:797
  344.4 12.5 %collective-permute-start.101 = (f32[3,2,2,2,16,256]{5,4,3,2,1,0:T(8,128)}, f32[3,2,2,2,16,256]{5,4,3,2,1,0:T(8,128)}, u32[]{:S(2)}, u32[]{:S(2)}) collective-permute-start(f32[3,2,2,2,16,256]{5,4,3,2,1,0:T(8,128)} %pad_maximum_fusion.24), channel_id=1, source_target_pairs={{0,4},{4,0},{8,12},{12,8},{1,5},{5,1},{9,13},{13,9},{2,6},{6,2},{1... | collective-permute-start | bytes 1179656 | tf_op jit(solution)/shard_map/ppermute | solution.py:818
  353.3 12.2 %collective-permute-start.97 = (f32[3,1,2,4,16,256]{5,4,3,2,1,0:T(8,128)}, f32[3,1,2,4,16,256]{5,4,3,2,1,0:T(8,128)S(1)}, u32[]{:S(2)}, u32[]{:S(2)}) collective-permute-start(f32[3,1,2,4,16,256]{5,4,3,2,1,0:T(8,128)} %constant_dynamic-slice_fusion.13), channel_id=1, source_target_pairs={{32,64},{64,32},{96,0},{0,96},{33,65},{65,33},{97,1},{1,97},{34,66... | collective-permute-start | bytes 1179656 | tf_op jit(solution)/shard_map/ppermute | solution.py:825
  368.1 26.3 %collective-permute-start.102 = (f32[3,2,2,1,16,256]{5,4,3,2,1,0:T(8,128)S(1)}, f32[3,2,2,1,16,256]{5,4,3,2,1,0:T(8,128)S(1)}, u32[]{:S(2)}, u32[]{:S(2)}) collective-permute-start(f32[3,2,2,1,16,256]{5,4,3,2,1,0:T(8,128)S(1)} %constant_dynamic-slice_fusion.2), channel_id=1, source_target_pairs={{4,8},{8,4},{12,0},{0,12},{5,9},{9,5},{13,1},{1,13},{6,10},{10,6},... | collective-permute-start | bytes 589832 | tf_op jit(solution)/shard_map/ppermute | solution.py:825
  376.5 17.7 %collective-permute-start.98 = (f32[3,1,2,2,16,256]{5,4,3,2,1,0:T(8,128)S(1)}, f32[3,1,2,2,16,256]{5,4,3,2,1,0:T(8,128)S(1)}, u32[]{:S(2)}, u32[]{:S(2)}) collective-permute-start(f32[3,1,2,2,16,256]{5,4,3,2,1,0:T(8,128)S(1)} %pad_maximum_fusion.31), channel_id=1, source_target_pairs={{0,4},{4,0},{8,12},{12,8},{1,5},{5,1},{9,13},{13,9},{2,6},{6,2},{1... | collective-permute-start | bytes 589832 | tf_op jit(solution)/shard_map/ppermute | solution.py:818
  377.6 19.6 %collective-permute-start.94 = (f32[3,1,2,2,16,256]{5,4,3,2,1,0:T(8,128)S(1)}, f32[3,1,2,2,16,256]{5,4,3,2,1,0:T(8,128)S(1)}, u32[]{:S(2)}, u32[]{:S(2)}) collective-permute-start(f32[3,1,2,2,16,256]{5,4,3,2,1,0:T(8,128)S(1)} %constant_dynamic-slice_fusion.19), channel_id=1, source_target_pairs={{32,64},{64,32},{96,0},{0,96},{33,65},{65,33},{97,1},{1,97},{34,66... | collective-permute-start | bytes 589832 | tf_op jit(solution)/shard_map/ppermute | solution.py:825
  383.2 12.1 %collective-permute-start.90 = (f32[3,2,2,1,16,256]{5,4,3,2,1,0:T(8,128)S(1)}, f32[3,2,2,1,16,256]{5,4,3,2,1,0:T(8,128)S(1)}, u32[]{:S(2)}, u32[]{:S(2)}) collective-permute-start(f32[3,2,2,1,16,256]{5,4,3,2,1,0:T(8,128)S(1)} %pad_maximum_fusion.30), channel_id=1, source_target_pairs={{0,32},{32,0},{64,96},{96,64},{1,33},{33,1},{65,97},{97,65},{2,34}... | collective-permute-start | bytes 589832 | tf_op jit(solution)/shard_map/ppermute | solution.py:818
  394.2 20.6 %collective-permute-start.24 = (f32[1,2,2,4,16,256]{5,4,3,2,1,0:T(8,128)S(1)}, f32[1,2,2,4,16,256]{5,4,3,2,1,0:T(8,128)S(1)}, u32[]{:S(2)}, u32[]{:S(2)}) collective-permute-start(f32[1,2,2,4,16,256]{5,4,3,2,1,0:T(8,128)S(1)} %constant_dynamic-slice_fusion.78), channel_id=1, source_target_pairs={{32,64},{64,32},{96,0},{0,96},{33,65},{65,33},{97,1},{1,97},{34,66... | collective-permute-start | bytes 786440 | tf_op jit(solution)/shard_map/ppermute | solution.py:818
  394.4 22.4 %collective-permute-start.20 = (f32[1,2,2,4,16,256]{5,4,3,2,1,0:T(8,128)S(1)}, f32[1,2,2,4,16,256]{5,4,3,2,1,0:T(8,128)S(1)}, u32[]{:S(2)}, u32[]{:S(2)}) collective-permute-start(f32[1,2,2,4,16,256]{5,4,3,2,1,0:T(8,128)S(1)} %pad_maximum_fusion.27), channel_id=1, source_target_pairs={{0,32},{32,0},{64,96},{96,64},{1,33},{33,1},{65,97},{97,65},{2,34}... | collective-permute-start | bytes 786440 | tf_op jit(solution)/shard_map/ppermute | solution.py:818
  395.3 23.1 %collective-permute-start.16 = (f32[1,4,2,2,16,256]{5,4,3,2,1,0:T(8,128)S(1)}, f32[1,4,2,2,16,256]{5,4,3,2,1,0:T(8,128)S(1)}, u32[]{:S(2)}, u32[]{:S(2)}) collective-permute-start(f32[1,4,2,2,16,256]{5,4,3,2,1,0:T(8,128)S(1)} %constant_dynamic-slice_fusion.97), channel_id=1, source_target_pairs={{4,8},{8,4},{12,0},{0,12},{5,9},{9,5},{13,1},{1,13},{6,10},{10,6},... | collective-permute-start | bytes 786440 | tf_op jit(solution)/shard_map/ppermute | solution.py:818
  414.8 30.1 %collective-permute-start.12 = (f32[1,4,2,2,16,384]{5,4,3,2,1,0:T(8,128)}, f32[1,4,2,2,16,384]{5,4,3,2,1,0:T(8,128)}, u32[]{:S(2)}, u32[]{:S(2)}) collective-permute-start(f32[1,4,2,2,16,384]{5,4,3,2,1,0:T(8,128)} %pad_maximum_fusion.22), channel_id=1, source_target_pairs={{0,4},{4,0},{8,12},{12,8},{1,5},{5,1},{9,13},{13,9},{2,6},{6,2},{1... | collective-permute-start | bytes 1179656 | tf_op jit(solution)/shard_map/ppermute | solution.py:818
  414.9 57.1 %collective-permute-start.62 = (f32[1,2,2,4,16,512]{5,4,3,2,1,0:T(8,128)}, f32[1,2,2,4,16,512]{5,4,3,2,1,0:T(8,128)}, u32[]{:S(2)}, u32[]{:S(2)}) collective-permute-start(f32[1,2,2,4,16,512]{5,4,3,2,1,0:T(8,128)} %constant_dynamic-slice_fusion.42), channel_id=1, source_target_pairs={{32,64},{64,32},{96,0},{0,96},{33,65},{65,33},{97,1},{1,97},{34,66... | collective-permute-start | bytes 1572872 | tf_op jit(solution)/shard_map/ppermute | solution.py:818
  416.9 58.8 %collective-permute-start.58 = (f32[1,2,2,4,16,512]{5,4,3,2,1,0:T(8,128)}, f32[1,2,2,4,16,512]{5,4,3,2,1,0:T(8,128)}, u32[]{:S(2)}, u32[]{:S(2)}) collective-permute-start(f32[1,2,2,4,16,512]{5,4,3,2,1,0:T(8,128)} %pad_maximum_fusion.19), channel_id=1, source_target_pairs={{0,32},{32,0},{64,96},{96,64},{1,33},{33,1},{65,97},{97,65},{2,34}... | collective-permute-start | bytes 1572872 | tf_op jit(solution)/shard_map/ppermute | solution.py:818
  441.8 35.5 %collective-permute-start.54 = (f32[1,4,2,2,16,512]{5,4,3,2,1,0:T(8,128)}, f32[1,4,2,2,16,512]{5,4,3,2,1,0:T(8,128)S(1)}, u32[]{:S(2)}, u32[]{:S(2)}) collective-permute-start(f32[1,4,2,2,16,512]{5,4,3,2,1,0:T(8,128)} %constant_dynamic-slice_fusion.59), channel_id=1, source_target_pairs={{4,8},{8,4},{12,0},{0,12},{5,9},{9,5},{13,1},{1,13},{6,10},{10,6},... | collective-permute-start | bytes 1572872 | tf_op jit(solution)/shard_map/ppermute | solution.py:818
  471.9 12.4 %collective-permute-start.50 = (f32[1,4,2,2,16,640]{5,4,3,2,1,0:T(8,128)S(1)}, f32[1,4,2,2,16,640]{5,4,3,2,1,0:T(8,128)S(1)}, u32[]{:S(2)}, u32[]{:S(2)}) collective-permute-start(f32[1,4,2,2,16,640]{5,4,3,2,1,0:T(8,128)S(1)} %copy-done.196), channel_id=1, source_target_pairs={{0,4},{4,0},{8,12},{12,8},{1,5},{5,1},{9,13},{13,9},{2,6},{6,2},{1... | collective-permute-start | bytes 1966088 | tf_op jit(solution)/shard_map/ppermute | solution.py:818
  475.6 18.4 %collective-permute-start.63 = (f32[1,2,2,2,16,512]{5,4,3,2,1,0:T(8,128)S(1)}, f32[1,2,2,2,16,512]{5,4,3,2,1,0:T(8,128)S(1)}, u32[]{:S(2)}, u32[]{:S(2)}) collective-permute-start(f32[1,2,2,2,16,512]{5,4,3,2,1,0:T(8,128)S(1)} %pad_maximum_fusion.29), channel_id=1, source_target_pairs={{0,4},{4,0},{8,12},{12,8},{1,5},{5,1},{9,13},{13,9},{2,6},{6,2},{1... | collective-permute-start | bytes 786440 | tf_op jit(solution)/shard_map/ppermute | solution.py:818
  477.3 20.2 %collective-permute-start.59 = (f32[1,1,2,4,16,512]{5,4,3,2,1,0:T(8,128)S(1)}, f32[1,1,2,4,16,512]{5,4,3,2,1,0:T(8,128)S(1)}, u32[]{:S(2)}, u32[]{:S(2)}) collective-permute-start(f32[1,1,2,4,16,512]{5,4,3,2,1,0:T(8,128)S(1)} %constant_dynamic-slice_fusion.48), channel_id=1, source_target_pairs={{32,64},{64,32},{96,0},{0,96},{33,65},{65,33},{97,1},{1,97},{34,66... | collective-permute-start | bytes 786440 | tf_op jit(solution)/shard_map/ppermute | solution.py:825
  478.0 23.3 %collective-permute-start.55 = (f32[1,2,2,2,16,512]{5,4,3,2,1,0:T(8,128)S(1)}, f32[1,2,2,2,16,512]{5,4,3,2,1,0:T(8,128)S(1)}, u32[]{:S(2)}, u32[]{:S(2)}) collective-permute-start(f32[1,2,2,2,16,512]{5,4,3,2,1,0:T(8,128)S(1)} %pad_maximum_fusion.28), channel_id=1, source_target_pairs={{0,32},{32,0},{64,96},{96,64},{1,33},{33,1},{65,97},{97,65},{2,34}... | collective-permute-start | bytes 786440 | tf_op jit(solution)/shard_map/ppermute | solution.py:818
  492.1 36.9 %collective-permute-start.51 = (f32[1,4,2,1,16,640]{5,4,3,2,1,0:T(8,128)S(1)}, f32[1,4,2,1,16,640]{5,4,3,2,1,0:T(8,128)S(1)}, u32[]{:S(2)}, u32[]{:S(2)}) collective-permute-start(f32[1,4,2,1,16,640]{5,4,3,2,1,0:T(8,128)S(1)} %constant_dynamic-slice_fusion.65), channel_id=1, source_target_pairs={{4,8},{8,4},{12,0},{0,12},{5,9},{9,5},{13,1},{1,13},{6,10},{10,6},... | collective-permute-start | bytes 983048 | tf_op jit(solution)/shard_map/ppermute | solution.py:825
  497.6 14.7 %collective-permute-start.64 = (f32[1,2,2,1,16,512]{5,4,3,2,1,0:T(8,128)S(1)}, f32[1,2,2,1,16,512]{5,4,3,2,1,0:T(8,128)S(1)}, u32[]{:S(2)}, u32[]{:S(2)}) collective-permute-start(f32[1,2,2,1,16,512]{5,4,3,2,1,0:T(8,128)S(1)} %constant_dynamic-slice_fusion.37), channel_id=1, source_target_pairs={{4,8},{8,4},{12,0},{0,12},{5,9},{9,5},{13,1},{1,13},{6,10},{10,6},... | collective-permute-start | bytes 393224 | tf_op jit(solution)/shard_map/ppermute | solution.py:825
  543.8 14.2 %collective-permute-start.42 = (f32[1,2,2,4,16,256]{5,4,2,3,1,0:T(8,128)S(1)}, f32[1,2,2,4,16,256]{5,4,2,3,1,0:T(8,128)S(1)}, u32[]{:S(2)}, u32[]{:S(2)}) collective-permute-start(f32[1,2,2,4,16,256]{5,4,2,3,1,0:T(8,128)S(1)} %maximum_select_fusion.18), channel_id=1, source_target_pairs={{0,32},{32,0},{64,96},{96,64},{1,33},{33,1},{65,97},{97,65},{2,34}... | collective-permute-start | bytes 786440 | tf_op jit(solution)/shard_map/ppermute | solution.py:840
  544.0 17.4 %collective-permute-start.46 = (f32[1,2,2,4,16,256]{5,4,2,1,3,0:T(8,128)S(1)}, f32[1,2,2,4,16,256]{5,4,2,1,3,0:T(8,128)S(1)}, u32[]{:S(2)}, u32[]{:S(2)}) collective-permute-start(f32[1,2,2,4,16,256]{5,4,2,1,3,0:T(8,128)S(1)} %maximum_select_fusion.19), channel_id=1, source_target_pairs={{32,64},{64,32},{96,0},{0,96},{33,65},{65,33},{97,1},{1,97},{34,66... | collective-permute-start | bytes 786440 | tf_op jit(solution)/shard_map/ppermute | solution.py:840
  557.9 15.8 %collective-permute-start.34 = (f32[1,4,2,2,16,384]{5,4,2,1,3,0:T(8,128)S(1)}, f32[1,4,2,2,16,384]{5,4,2,1,3,0:T(8,128)S(1)}, u32[]{:S(2)}, u32[]{:S(2)}) collective-permute-start(f32[1,4,2,2,16,384]{5,4,2,1,3,0:T(8,128)S(1)} %maximum_select_fusion.14), channel_id=1, source_target_pairs={{0,4},{4,0},{8,12},{12,8},{1,5},{5,1},{9,13},{13,9},{2,6},{6,2},{1... | collective-permute-start | bytes 1179656 | tf_op jit(solution)/shard_map/ppermute | solution.py:840
  570.3 39.7 %collective-permute-start.77 = (f32[1,1,2,2,16,512]{5,4,2,3,1,0:T(8,128)S(1)}, f32[1,1,2,2,16,512]{5,4,2,3,1,0:T(8,128)S(1)}, u32[]{:S(2)}, u32[]{:S(2)}) collective-permute-start(f32[1,1,2,2,16,512]{5,4,2,3,1,0:T(8,128)S(1)} %maximum_select_fusion.38), channel_id=1, source_target_pairs={{0,4},{4,0},{8,12},{12,8},{1,5},{5,1},{9,13},{13,9},{2,6},{6,2},{1... | collective-permute-start | bytes 393224 | tf_op jit(solution)/shard_map/ppermute | solution.py:840
  571.8 36.8 %collective-permute-start.73 = (f32[1,1,2,2,16,512]{5,4,3,2,1,0:T(8,128)S(1)}, f32[1,1,2,2,16,512]{5,4,3,2,1,0:T(8,128)S(1)}, u32[]{:S(2)}, u32[]{:S(2)}) collective-permute-start(f32[1,1,2,2,16,512]{5,4,3,2,1,0:T(8,128)S(1)} %maximum_select_fusion.37), channel_id=1, source_target_pairs={{32,64},{64,32},{96,0},{0,96},{33,65},{65,33},{97,1},{1,97},{34,66... | collective-permute-start | bytes 393224 | tf_op jit(solution)/shard_map/ppermute | solution.py:835
  573.7 38.3 %collective-permute-start.69 = (f32[1,2,2,1,16,640]{5,4,2,3,1,0:T(8,128)S(1)}, f32[1,2,2,1,16,640]{5,4,2,3,1,0:T(8,128)S(1)}, u32[]{:S(2)}, u32[]{:S(2)}) collective-permute-start(f32[1,2,2,1,16,640]{5,4,2,3,1,0:T(8,128)S(1)} %maximum_select_fusion.27), channel_id=1, source_target_pairs={{0,32},{32,0},{64,96},{96,64},{1,33},{33,1},{65,97},{97,65},{2,34}... | collective-permute-start | bytes 491528 | tf_op jit(solution)/shard_map/ppermute | solution.py:840
  575.7 84.4 %collective-permute-start.47 = (f32[512,1152]{1,0:T(8,128)}, f32[512,1152]{1,0:T(8,128)}, u32[]{:S(2)}, u32[]{:S(2)}) collective-permute-start(f32[512,1152]{1,0:T(8,128)} %pad_maximum_fusion.4), channel_id=1, source_target_pairs={{0,2},{2,0},{1,3},{3,1},{4,6},{6,4},{5,7},{7,5},{8,10},{10,8},{9,1... | collective-permute-start | bytes 7077896 | tf_op jit(solution)/shard_map/ppermute | solution.py:797
  620.2 13.3 %collective-permute-start.79 = (f32[1,2,2,4,16,512]{5,4,2,3,1,0:T(8,128)S(1)}, f32[1,2,2,4,16,512]{5,4,2,3,1,0:T(8,128)S(1)}, u32[]{:S(2)}, u32[]{:S(2)}) collective-permute-start(f32[1,2,2,4,16,512]{5,4,2,3,1,0:T(8,128)S(1)} %maximum_select_fusion.12), channel_id=1, source_target_pairs={{0,32},{32,0},{64,96},{96,64},{1,33},{33,1},{65,97},{97,65},{2,34}... | collective-permute-start | bytes 1572872 | tf_op jit(solution)/shard_map/ppermute | solution.py:840
  620.5 12.8 %collective-permute-start.83 = (f32[1,2,2,4,16,512]{5,4,2,1,3,0:T(8,128)S(1)}, f32[1,2,2,4,16,512]{5,4,2,1,3,0:T(8,128)S(1)}, u32[]{:S(2)}, u32[]{:S(2)}) collective-permute-start(f32[1,2,2,4,16,512]{5,4,2,1,3,0:T(8,128)S(1)} %maximum_select_fusion.13), channel_id=1, source_target_pairs={{32,64},{64,32},{96,0},{0,96},{33,65},{65,33},{97,1},{1,97},{34,66... | collective-permute-start | bytes 1572872 | tf_op jit(solution)/shard_map/ppermute | solution.py:840
  633.4 12.9 %collective-permute-start.71 = (f32[1,4,2,2,16,640]{5,4,2,1,3,0:T(8,128)S(1)}, f32[1,4,2,2,16,640]{5,4,2,1,3,0:T(8,128)S(1)}, u32[]{:S(2)}, u32[]{:S(2)}) collective-permute-start(f32[1,4,2,2,16,640]{5,4,2,1,3,0:T(8,128)S(1)} %maximum_select_fusion.7), channel_id=1, source_target_pairs={{0,4},{4,0},{8,12},{12,8},{1,5},{5,1},{9,13},{13,9},{2,6},{6,2},{1... | collective-permute-start | bytes 1966088 | tf_op jit(solution)/shard_map/ppermute | solution.py:840
  649.3 33.6 %collective-permute-start.84 = (f32[512,2176]{1,0:T(8,128)}, f32[512,2176]{1,0:T(8,128)}, u32[]{:S(2)}, u32[]{:S(2)}) collective-permute-start(f32[512,2176]{1,0:T(8,128)} %pad_maximum_fusion.3), channel_id=1, source_target_pairs={{0,2},{2,0},{1,3},{3,1},{4,6},{6,4},{5,7},{7,5},{8,10},{10,8},{9,1... | collective-permute-start | bytes 13369352 | tf_op jit(solution)/shard_map/ppermute | solution.py:797
  (280 other events, 2094.2 us)
Sparse Core Ops, SparseCore 0:
  427.0 109.5 all-gather.2

commit v3 on v2

v3 whole, which is shorter than its diff:
```python
import functools

import jax
import jax.numpy as jnp
import numpy as np
from jax import lax
from jax.experimental import pallas as pl
from jax.experimental.pallas import tpu as pltpu
from jax.sharding import PartitionSpec as P

HEAD_DIM = 64
DSSM = 1536
DP = ("y", "zh", "x", "core")
PAIR = [(0, 1), (1, 0)]
LOG2E = 1.4426950408889634
hidden_bias = -1e30
norm_eps = 1e-05
rope_base = 10000.0
LEN = 128


def dot_nn(left, right):
    return lax.dot_general(
        left, right, (((1,), (0,)), ((), ())), preferred_element_type=jnp.float32
    )


def dot_nt(left, right):
    return lax.dot_general(
        left, right, (((1,), (1,)), ((), ())), preferred_element_type=jnp.float32
    )


def dot_tn(left, right):
    return lax.dot_general(
        left, right, (((0,), (0,)), ((), ())), preferred_element_type=jnp.float32
    )


def two_terms(v):
    high = v.astype(jnp.bfloat16)
    return high, (v - high.astype(jnp.float32)).astype(jnp.bfloat16)


def three_dots(dot, left, right):
    left_high, left_low = two_terms(left)
    right_high, right_low = two_terms(right)
    return dot(left_high, right_high) + dot(left_high, right_low) + dot(left_low, right_high)


def sigmoid(v):
    return 1.0 / (1.0 + jnp.exp(-v))


def block(index):
    return slice(index * LEN, (index + 1) * LEN)


def lane_iota(rows=LEN):
    return lax.broadcasted_iota(jnp.int32, (rows, LEN), 1)


def mask_ts(seg_col, seg_row, i, j):
    same = seg_col[block(i), :] == seg_row[:, block(j)]
    if i != j:
        return same
    down = lax.broadcasted_iota(jnp.int32, (LEN, LEN), 0)
    return same & (down >= lane_iota())


def mask_st(seg_col, seg_row, j, i):
    same = seg_col[block(j), :] == seg_row[:, block(i)]
    if i != j:
        return same
    down = lax.broadcasted_iota(jnp.int32, (LEN, LEN), 0)
    return same & (down <= lane_iota())


def conv_rows(pad_ref, keep_ref, kernel, bias, start, lanes):
    summed = bias + kernel[3:4] * pad_ref[8 + start : 8 + start + LEN, lanes]
    for lag in (1, 2, 3):
        moved = pad_ref[8 + start - lag : 8 + start - lag + LEN, lanes]
        summed = summed + kernel[3 - lag : 4 - lag] * (moved * keep_ref[lag - 1, start : start + LEN, :])
    return summed


def widen(keep_ref, wide_ref):
    rows = keep_ref.shape[0]
    for lag in (1, 2, 3):
        wide_ref[lag - 1, :, :] = jnp.broadcast_to(keep_ref[:, lag : lag + 1], (rows, LEN))


def prep_kernel(
    conv_ref,
    small_ref,
    cos_ref,
    sin_ref,
    keep_ref,
    conv_kernel_ref,
    conv_bias_ref,
    state_kernel_ref,
    state_bias_ref,
    step_bias_ref,
    rate_ref,
    x_ref,
    xb_ref,
    slope_ref,
    state_ref,
    state_slope_ref,
    cum_ref,
    lag_ref,
    cum_row_ref,
    lag_row_ref,
    step_row_ref,
    sig_row_ref,
    q_ref,
    kv_ref,
    pad_ref,
    wide_ref,
):
    rows = conv_ref.shape[0]
    blocks = rows // LEN

    @pl.when(pl.program_id(0) == 0)
    def _():
        pad_ref[0:8, :] = jnp.zeros((8, LEN), jnp.float32)
        widen(keep_ref, wide_ref)
        for c in range(2):
            pad_ref[8 : rows + 8, :] = small_ref[:, block(c)]
            for i in range(blocks):
                pre = conv_rows(
                    pad_ref, wide_ref, state_kernel_ref[:, block(c)], state_bias_ref[:, block(c)], i * LEN, slice(0, LEN)
                )
                sig = sigmoid(pre)
                state_ref[block(i), block(c)] = pre * sig
                state_slope_ref[block(i), block(c)] = sig * (1.0 + pre * (1.0 - sig))

    @pl.when(pl.program_id(0) == 1)
    def _():
        down = lax.broadcasted_iota(jnp.int32, (LEN, LEN), 0)
        lower = jnp.where(down >= lane_iota(), 1.0, 0.0).astype(jnp.bfloat16)
        left_half = lane_iota() < HEAD_DIM
        carry = jnp.zeros((1, LEN), jnp.float32)
        heads = cum_row_ref.shape[0]
        for i in range(blocks):
            argument = small_ref[block(i), block(5)] + step_bias_ref[...]
            tail = jnp.exp(-jnp.abs(argument))
            grown = jnp.where(tail < 1e-3, tail - 0.5 * tail * tail, jnp.log(1.0 + tail))
            step = jnp.maximum(argument, 0.0) + grown
            scaled = step * rate_ref[...] * LOG2E
            first, rest = two_terms(scaled)
            last = scaled - first.astype(jnp.float32) - rest.astype(jnp.float32)
            cum = dot_nn(lower, first) + dot_nn(lower, rest) + dot_nn(lower, last.astype(jnp.bfloat16)) + carry
            carry = cum[LEN - 1 : LEN, :]
            lag = cum - jnp.log(step) * LOG2E
            cum_ref[block(i), :] = cum
            lag_ref[block(i), :] = lag
            cum_t, lag_t = cum.T, lag.T
            step_row_ref[:, block(i)] = step.T[:heads]
            sig_row_ref[:, block(i)] = sigmoid(argument).T[:heads]
            for h in range(heads):
                cum_row_ref[h, :, block(i)] = cum_t[h : h + 1]
                lag_row_ref[h, :, block(i)] = lag_t[h : h + 1]
            cosine, sine = cos_ref[block(i), :], sin_ref[block(i), :]
            kv = small_ref[block(i), block(4)]
            kv_ref[block(i), :] = jnp.where(left_half, rotate_tile(kv, cosine, sine), kv).astype(jnp.bfloat16)
            for p in range(q_ref.shape[1] // LEN):
                q_ref[block(i), block(p)] = rotate_tile(small_ref[block(i), block(2 + p)], cosine, sine).astype(
                    jnp.bfloat16
                )

    for sub in range(GROUP):
        lanes = block(sub)
        pad_ref[8 : rows + 8, :] = conv_ref[:, lanes]
        for i in range(blocks):
            pre = conv_rows(pad_ref, wide_ref, conv_kernel_ref[:, lanes], conv_bias_ref[:, lanes], i * LEN, slice(0, LEN))
            sig = sigmoid(pre)
            x = pre * sig
            x_ref[block(i), lanes] = x
            xb_ref[block(i), lanes] = x.astype(jnp.bfloat16)
            slope_ref[block(i), lanes] = sig * (1.0 + pre * (1.0 - sig))


def rotate_tile(v, cosine, sine):
    first = lax.rem(lane_iota(v.shape[0]), HEAD_DIM) < HEAD_DIM // 2
    swapped = jnp.where(first, pltpu.roll(v, LEN - HEAD_DIM // 2, 1), pltpu.roll(v, HEAD_DIM // 2, 1))
    return v * cosine + swapped * sine


def scan_kernel(
    chunks,
    heads,
    gate_ref,
    x_ref,
    xb_ref,
    state_ref,
    cum_ref,
    lag_row_ref,
    seg_col_ref,
    seg_row_ref,
    skip_ref,
    y_ref,
    gated_ref,
    row_ref,
    wide_ref,
    cross_ref,
    bias_ref,
    mix_ref,
    square_ref,
):
    step = pl.program_id(0)
    first = chunks[0]
    pairs = [(i, j) for i in chunks for j in range(max(0, i - 2), i + 1)]
    left_half = lane_iota() < HEAD_DIM

    @pl.when(step == 0)
    def _():
        for h in range(heads):
            for i in chunks:
                wide_ref[h, block(i - first), :] = jnp.broadcast_to(cum_ref[block(i), h : h + 1], (LEN, LEN))
        for i in chunks:
            low = max(0, i - 2)
            cross = three_dots(dot_nt, state_ref[block(i), LEN:], state_ref[low * LEN : (i + 1) * LEN, :LEN])
            for n, (i2, j) in enumerate(pairs):
                if i2 == i:
                    cross_ref[n] = cross[:, block(j - low)]
                    allowed = mask_ts(seg_col_ref, seg_row_ref, i, j)
                    bias_ref[n] = jnp.where(allowed, 0.0, hidden_bias)
        square_ref[...] = jnp.zeros(square_ref.shape, jnp.float32)

    tiles = (gate_ref, x_ref, xb_ref, skip_ref, y_ref, gated_ref)

    def head_pair(hp, gate_ref, x_ref, xb_ref, skip_ref, y_ref, gated_ref):
        for i in chunks:
            at = block(i - first)
            low = max(0, i - 2)
            for n, (i2, j) in enumerate(pairs):
                if i2 != i:
                    continue
                for e in range(2):
                    spread = wide_ref[2 * hp + e, at, :] - lag_row_ref[2 * hp + e, :, block(j)]
                    decay = jnp.exp2(spread + bias_ref[n])
                    mix_ref[i - first, block(e), block(j - low)] = (decay * cross_ref[n]).astype(jnp.bfloat16)
            both = dot_nn(mix_ref[i - first, :, : (i + 1 - low) * LEN], xb_ref[low * LEN : (i + 1) * LEN, :])
            y = jnp.where(left_half, both[:LEN], both[LEN:])
            y_ref[at, :] = y
            gate = gate_ref[at, :]
            gated = (y + skip_ref[...] * x_ref[at, :]) * (gate * sigmoid(gate))
            gated_ref[at, :] = gated
            square_ref[at, :] = square_ref[at, :] + gated * gated

    for sub in range(GROUP):
        head_pair(GROUP * step + sub, *[t.at[:, block(sub)] for t in tiles])

    @pl.when(step == pl.num_programs(0) - 1)
    def _():
        for i in chunks:
            at = block(i - first)
            total = jnp.sum(square_ref[at, :], axis=1, keepdims=True)
            row_ref[0:1, at] = jnp.broadcast_to(total, (LEN, LEN)).T[0:1]


def attention_kernel(chunks, q_ref, kv_ref, seg_col_ref, seg_row_ref, out_ref, lse_ref):
    scale = HEAD_DIM ** (-0.5) * LOG2E
    first = chunks[0]
    left_half = lane_iota() < HEAD_DIM
    zero = jnp.zeros((LEN, LEN), jnp.bfloat16)
    lse_ref[...] = jnp.zeros(lse_ref.shape, jnp.float32)
    for i in chunks:
        at = block(i - first)
        low = max(0, i - 2) * LEN
        span = (i + 1) * LEN - low
        allowed = jnp.concatenate([mask_ts(seg_col_ref, seg_row_ref, i, j) for j in range(low // LEN, i + 1)], axis=1)
        keys = kv_ref[low : low + span, :]
        turned = pltpu.roll(keys.astype(jnp.float32), HEAD_DIM, 1).astype(jnp.bfloat16)
        for p in range(q_ref.shape[1] // LEN):
            queries = q_ref[block(i), block(p)]
            result = []
            for e in range(2):
                masked = jnp.where(left_half == (e == 0), queries, zero)
                scores = dot_nt(masked, keys if e == 0 else turned) * scale
                scores = jnp.where(allowed, scores, hidden_bias)
                top = jnp.max(scores, axis=1, keepdims=True)
                weights = jnp.exp2(scores - top)
                total = jnp.sum(weights, axis=1, keepdims=True)
                probs = (weights * (1.0 / total)).astype(jnp.bfloat16)
                result.append(dot_nn(probs, turned if e == 0 else keys))
                lse = jnp.broadcast_to(top + jnp.log(total) * LOG2E, (LEN, LEN))
                lse_ref[2 * p + e : 2 * p + e + 1, at] = lse.T[0:1]
            out_ref[at, block(p)] = jnp.where(left_half, result[0], result[1]).astype(jnp.bfloat16)


def attention_back_kernel(chunks, final, *refs):
    q_ref, kv_ref, do_ref, lse_ref, seg_col_ref, seg_row_ref, cos_ref, sin_ref = refs[:8]
    if final:
        dk_in_ref, dv_in_ref, dq_ref, dkv_ref, dk_ref, dv_ref, turned_ref, key_t_ref = refs[8:]
    else:
        dq_ref, dk_ref, dv_ref, turned_ref, key_t_ref = refs[8:]
    scale = HEAD_DIM ** (-0.5)
    blocks = q_ref.shape[0] // LEN
    first = chunks[0]
    left_half = lane_iota() < HEAD_DIM
    zero = jnp.zeros((LEN, LEN), jnp.bfloat16)
    for i in range(chunks[-1] + 1):
        kv = kv_ref[block(i), :].astype(jnp.float32)
        turned_ref[block(i), :] = pltpu.roll(kv, HEAD_DIM, 1).astype(jnp.bfloat16)
        key_t_ref[:, block(i)] = kv.T[:HEAD_DIM].astype(jnp.bfloat16)
    if final:
        dk_ref[...] = dk_in_ref[...]
        dv_ref[...] = dv_in_ref[...]
    else:
        dk_ref[...] = jnp.zeros(dk_ref.shape, jnp.float32)
        dv_ref[...] = jnp.zeros(dv_ref.shape, jnp.float32)
    for i in chunks:
        at = block(i - first)
        low = max(0, i - 2) * LEN
        span = (i + 1) * LEN - low
        window = slice(low, low + span)
        allowed = jnp.concatenate([mask_st(seg_col_ref, seg_row_ref, j, i) for j in range(low // LEN, i + 1)], axis=0)
        keys, turned = kv_ref[window, :], turned_ref[window, :]
        for p in range(q_ref.shape[1] // LEN):
            queries, douts = q_ref[block(i), block(p)], do_ref[at, block(p)]
            back = []
            for e in range(2):
                side = left_half == (e == 0)
                q_half = jnp.where(side, queries, zero)
                do_half = jnp.where(side, douts, zero)
                h = 2 * p + e
                scores = dot_nt(keys if e == 0 else turned, q_half) * (scale * LOG2E)
                probs = jnp.exp2(jnp.where(allowed, scores, hidden_bias) - lse_ref[h : h + 1, at])
                dprobs = dot_nt(turned if e == 0 else keys, do_half)
                inner = jnp.sum(probs * dprobs, axis=0, keepdims=True)
                dscores = (probs * (dprobs - inner)).astype(jnp.bfloat16)
                dv_ref[window, :] = dv_ref[window, :] + dot_nn(probs.astype(jnp.bfloat16), do_half)
                dk_ref[window, :] = dk_ref[window, :] + dot_nn(dscores, q_half)
                back.append(dot_nn(key_t_ref[:, window], dscores))
            dq = jnp.concatenate(back, axis=0).T * scale
            dq_ref[at, block(p)] = rotate_tile(dq, cos_ref[block(i), :], -sin_ref[block(i), :]).astype(jnp.bfloat16)
    if not final:
        return
    for i in range(blocks):
        dk = dk_ref[block(i), :]
        dk = (dk + pltpu.roll(dk, HEAD_DIM, 1)) * scale
        dk = rotate_tile(dk, cos_ref[block(i), :], -sin_ref[block(i), :])
        dv = dv_ref[block(i), :]
        dv = dv + pltpu.roll(dv, HEAD_DIM, 1)
        dkv_ref[block(i), :] = jnp.where(left_half, dk, dv).astype(jnp.bfloat16)


def scan_back_kernel(
    chunks,
    heads,
    gmr_ref,
    gated_ref,
    square_a_ref,
    square_b_ref,
    dot_a_ref,
    dot_b_ref,
    gain_ref,
    gate_ref,
    y_ref,
    x_ref,
    xb_ref,
    state_ref,
    lag_ref,
    cum_row_ref,
    skip_ref,
    seg_col_ref,
    seg_row_ref,
    select_ref,
    dgate_ref,
    gy_ref,
    dx_ref,
    p_ref,
    grad_in_ref,
    grad_out_ref,
    sums_ref,
    gyb_ref,
    wide_ref,
    cross_ref,
    bias_ref,
    dcross_ref,
    inv_wide_ref,
    dot_wide_ref,
    inner_ref,
    mix_ref,
):
    step = pl.program_id(0)
    first = chunks[0]
    sources = chunks[-1] + 1
    left_half = lane_iota() < HEAD_DIM
    zero = jnp.zeros((LEN, LEN), jnp.bfloat16)
    spans = [(j, max(j, first), min(j + 3, sources)) for j in range(sources)]
    pairs = [(j, i) for j, start, stop in spans for i in range(start, stop)]

    @pl.when(step == 0)
    def _():
        for i in chunks:
            at = block(i - first)
            square = (square_a_ref[:, at] + square_b_ref[:, at]) / DSSM
            inv = lax.rsqrt(square + norm_eps)
            inv_wide_ref[at, :] = jnp.broadcast_to(inv, (LEN, LEN)).T
            dot = (dot_a_ref[:, at] + dot_b_ref[:, at]) / DSSM
            dot_wide_ref[at, :] = jnp.broadcast_to(dot, (LEN, LEN)).T
        p_ref[...] = jnp.zeros(p_ref.shape, jnp.float32)
        for h in range(heads):
            wide_ref[h] = jnp.broadcast_to(lag_ref[: sources * LEN, h : h + 1], (sources * LEN, LEN))
        for j, start, stop in spans:
            cross = three_dots(dot_nt, state_ref[block(j), :LEN], state_ref[start * LEN : stop * LEN, LEN:])
            for n, (j2, i) in enumerate(pairs):
                if j2 == j:
                    cross_ref[n] = cross[:, block(i - start)]
                    allowed = mask_st(seg_col_ref, seg_row_ref, j, i)
                    bias_ref[n] = jnp.where(allowed, 0.0, hidden_bias)
                    dcross_ref[n] = jnp.zeros((LEN, LEN), jnp.float32)

    tiles = (
        gmr_ref, gated_ref, gain_ref, gate_ref, y_ref, x_ref, xb_ref, skip_ref, dgate_ref, gy_ref, dx_ref, sums_ref
    )

    def head_pair(
        hp,
        select,
        gmr_ref,
        gated_ref,
        gain_ref,
        gate_ref,
        y_ref,
        x_ref,
        xb_ref,
        skip_ref,
        dgate_ref,
        gy_ref,
        dx_ref,
        sums_ref,
    ):
        skip = skip_ref[...]
        gain = gain_ref[...]
        skip_sum = jnp.zeros((1, LEN), jnp.float32)
        gain_sum = jnp.zeros((1, LEN), jnp.float32)
        for i in chunks:
            at = block(i - first)
            inv = inv_wide_ref[at, :]
            unit = gated_ref[at, :] * inv
            rows_grad = gmr_ref[at, :]
            grad = inv * (rows_grad * gain - unit * dot_wide_ref[at, :])
            gate = gate_ref[at, :]
            sig = sigmoid(gate)
            y = y_ref[at, :]
            x = x_ref[at, :]
            gy = grad * (gate * sig)
            dgate_ref[at, :] = (grad * (y + skip * x) * (sig * (1.0 + gate * (1.0 - sig)))).astype(jnp.bfloat16)
            gyb = gy.astype(jnp.bfloat16)
            gy_ref[at, :] = gy
            gyb_ref[at, :] = gyb
            high, rest = two_terms(gyb.astype(jnp.float32) * y)
            p_ref[:, at] = p_ref[:, at] + dot_nt(select, high) + dot_nt(select, rest)
            skip_sum = skip_sum + jnp.sum(gy * x, axis=0, keepdims=True)
            gain_sum = gain_sum + jnp.sum(rows_grad * unit, axis=0, keepdims=True)
        sums_ref[0:1, :] = skip_sum
        sums_ref[1:2, :] = gain_sum

        for j, start, stop in spans:
            x_pair = xb_ref[block(j), :]
            x_both = jnp.concatenate([jnp.where(left_half, x_pair, zero), jnp.where(left_half, zero, x_pair)], axis=0)
            wide = (stop - start) * LEN
            gy_rows = gyb_ref[(start - first) * LEN : (stop - first) * LEN, :]
            inner_ref[:, :wide] = dot_nt(x_both, gy_rows)
            for n, (j2, i) in enumerate(pairs):
                if j2 != j:
                    continue
                grown = dcross_ref[n]
                for e in range(2):
                    spread = cum_row_ref[2 * hp + e, :, block(i)] - wide_ref[2 * hp + e, block(j), :]
                    decay = jnp.exp2(spread + bias_ref[n])
                    grown = grown + inner_ref[block(e), block(i - start)] * decay
                    mix_ref[block(e), block(i - start)] = (decay * cross_ref[n]).astype(jnp.bfloat16)
                dcross_ref[n] = grown
            both = dot_nn(mix_ref[:, :wide], gy_rows)
            dx_ref[block(j), :] = jnp.where(left_half, both[:LEN], both[LEN:])

    for sub in range(GROUP):
        head_pair(GROUP * step + sub, select_ref[:, block(sub)], *[t.at[:, block(sub)] for t in tiles])

    @pl.when(step == pl.num_programs(0) - 1)
    def _():
        grad_out = {i: jnp.zeros((LEN, LEN), jnp.float32) for i in chunks}
        for j in range(sources):
            grad_in = jnp.zeros((LEN, LEN), jnp.float32)
            for n, (j2, i) in enumerate(pairs):
                if j2 != j:
                    continue
                high, rest = two_terms(dcross_ref[n])
                out_high, out_rest = two_terms(state_ref[block(i), LEN:])
                in_high, in_rest = two_terms(state_ref[block(j), :LEN])
                grad_in = grad_in + dot_nn(high, out_high) + dot_nn(high, out_rest) + dot_nn(rest, out_high)
                grad_out[i] = grad_out[i] + dot_tn(high, in_high) + dot_tn(high, in_rest) + dot_tn(rest, in_high)
            grad_in_ref[block(j), :] = grad_in
        for i in chunks:
            grad_out_ref[block(i - first), :] = grad_out[i]


def conv_back(grad_ref, value_ref, keep_ref, kernel_ref, out_ref, sum_ref, lanes, blocks):
    taps = kernel_ref[:, lanes]
    totals = [jnp.zeros((1, LEN), jnp.float32) for _ in range(5)]
    for i in range(blocks):
        here = grad_ref[i * LEN : (i + 1) * LEN, :]
        grad = taps[3:4] * here
        totals[4] = totals[4] + jnp.sum(here, axis=0, keepdims=True)
        totals[3] = totals[3] + jnp.sum(here * value_ref[8 + i * LEN : 8 + (i + 1) * LEN, :], axis=0, keepdims=True)
        for lag in (1, 2, 3):
            ahead = grad_ref[i * LEN + lag : (i + 1) * LEN + lag, :]
            grad = grad + taps[3 - lag : 4 - lag] * (ahead * keep_ref[lag - 1, i * LEN + lag : (i + 1) * LEN + lag, :])
            moved = value_ref[8 + i * LEN - lag : 8 + (i + 1) * LEN - lag, :]
            masked = here * keep_ref[lag - 1, i * LEN : (i + 1) * LEN, :]
            totals[3 - lag] = totals[3 - lag] + jnp.sum(masked * moved, axis=0, keepdims=True)
        out_ref[block(i), lanes] = grad.astype(jnp.bfloat16)
    for tap in range(5):
        sum_ref[tap : tap + 1, lanes] = totals[tap]


def scan_end_kernel(
    heads,
    gy_a_ref,
    gy_b_ref,
    dx_a_ref,
    dx_b_ref,
    p_a_ref,
    p_b_ref,
    in_a_ref,
    in_b_ref,
    out_a_ref,
    out_b_ref,
    xb_ref,
    slope_ref,
    state_slope_ref,
    conv_ref,
    small_ref,
    step_row_ref,
    sig_row_ref,
    rate_ref,
    skip_ref,
    keep_ref,
    seg_col_ref,
    seg_row_ref,
    select_ref,
    conv_kernel_ref,
    state_kernel_ref,
    dconv_ref,
    dstate_ref,
    dstep_ref,
    conv_sum_ref,
    state_sum_ref,
    step_sum_ref,
    grad_pad_ref,
    value_pad_ref,
    wide_ref,
    q_ref,
    flow_ref,
):
    step = pl.program_id(0)
    rows = conv_ref.shape[0]
    blocks = rows // LEN
    half = rows // 2
    count = flow_ref.shape[0]

    @pl.when(step == 0)
    def _():
        value_pad_ref[0:8, :] = jnp.zeros((8, LEN), jnp.float32)
        grad_pad_ref[rows : rows + 8, :] = jnp.zeros((8, LEN), jnp.float32)
        widen(keep_ref, wide_ref)
        q_ref[...] = jnp.zeros(q_ref.shape, jnp.float32)
        for c in range(2):
            if c == 0:
                grad_pad_ref[0:half, :] = (in_a_ref[...] + in_b_ref[0:half, :]) * state_slope_ref[0:half, block(c)]
                grad_pad_ref[half:rows, :] = in_b_ref[half:rows, :] * state_slope_ref[half:rows, block(c)]
            else:
                grad_pad_ref[0:half, :] = out_a_ref[...] * state_slope_ref[0:half, block(c)]
                grad_pad_ref[half:rows, :] = out_b_ref[...] * state_slope_ref[half:rows, block(c)]
            value_pad_ref[8 : rows + 8, :] = small_ref[:, block(c)]
            conv_back(grad_pad_ref, value_pad_ref, wide_ref, state_kernel_ref, dstate_ref, state_sum_ref, block(c), blocks)

    tiles = (
        gy_a_ref, gy_b_ref, dx_a_ref, dx_b_ref, xb_ref, slope_ref, conv_ref, skip_ref, conv_kernel_ref, dconv_ref, conv_sum_ref
    )

    def head_pair(
        select,
        gy_a_ref,
        gy_b_ref,
        dx_a_ref,
        dx_b_ref,
        xb_ref,
        slope_ref,
        conv_ref,
        skip_ref,
        conv_kernel_ref,
        dconv_ref,
        conv_sum_ref,
    ):
        for j in range(blocks):
            dx = dx_b_ref[block(j), :]
            if j < blocks // 2:
                dx = dx + dx_a_ref[block(j), :]
                gy = gy_a_ref[block(j), :]
            else:
                gy = gy_b_ref[block(j - blocks // 2), :]
            high, rest = two_terms(dx * xb_ref[block(j), :].astype(jnp.float32))
            q_ref[:, block(j)] = q_ref[:, block(j)] + dot_nt(select, high) + dot_nt(select, rest)
            grad_pad_ref[block(j), :] = (dx + gy * skip_ref[...]) * slope_ref[block(j), :]
        value_pad_ref[8 : rows + 8, :] = conv_ref[...]
        conv_back(
            grad_pad_ref, value_pad_ref, wide_ref, conv_kernel_ref, dconv_ref, conv_sum_ref, slice(0, LEN), blocks
        )

    for sub in range(GROUP):
        head_pair(select_ref[:, block(sub)], *[t.at[:, block(sub)] for t in tiles])

    @pl.when(step == pl.num_programs(0) - 1)
    def _():
        q = q_ref[...]
        flow_ref[:, 0:half] = p_a_ref[...] - q[:, 0:half]
        flow_ref[:, half:rows] = p_b_ref[...] - q[:, half:rows]
        rate = jnp.broadcast_to(rate_ref[...], (LEN, LEN)).T[:count]
        bias_total = jnp.zeros((count, LEN), jnp.float32)
        decay_total = jnp.zeros((count, LEN), jnp.float32)
        for j in range(blocks):
            log_grad = jnp.zeros((count, LEN), jnp.float32)
            for i in range(j, min(j + 3, blocks)):
                chosen = jnp.where(mask_st(seg_col_ref, seg_row_ref, j, i), 1.0, 0.0).astype(jnp.bfloat16)
                high, rest = two_terms(flow_ref[:, block(i)])
                log_grad = log_grad + dot_nt(high, chosen) + dot_nt(rest, chosen)
            step = step_row_ref[:, block(j)]
            grad_step = jnp.where(step > 1e-30, q[:, block(j)] / step, 0.0) + log_grad * rate
            grad_arg = grad_step * sig_row_ref[:, block(j)]
            bias_total = bias_total + grad_arg
            decay_total = decay_total + log_grad * step
            tall = jnp.concatenate([grad_arg, jnp.zeros((LEN - count, LEN), jnp.float32)], axis=0)
            dstep_ref[block(j), :] = tall.T.astype(jnp.bfloat16)
        step_sum_ref[0:count, :] = jnp.broadcast_to(jnp.sum(bias_total, axis=1, keepdims=True), (count, LEN))
        step_sum_ref[count : 2 * count, :] = jnp.broadcast_to(
            jnp.sum(decay_total * rate, axis=1, keepdims=True), (count, LEN)
        )


def whole_block(shape):
    return pl.BlockSpec(shape, lambda step: (0,) * len(shape), pipeline_mode=pl.Buffered(1))


def tile(rows, row_block=0, first=0):
    return pl.BlockSpec((rows, GROUP * LEN), lambda step: (row_block, first + step))


def call(kernel, steps, out_shape, out_specs, scratch, operands, specs, flops):
    moved = sum(o.size * o.dtype.itemsize for o in operands) + sum(o.size * o.dtype.itemsize for o in out_shape)
    return pl.pallas_call(
        kernel,
        grid=(steps,),
        out_shape=out_shape,
        in_specs=[s or whole_block(o.shape) for o, s in zip(operands, specs)],
        out_specs=[s or whole_block(o.shape) for o, s in zip(out_shape, out_specs)],
        scratch_shapes=scratch,
        compiler_params=pltpu.CompilerParams(vmem_limit_bytes=VMEM_BYTES),
        cost_estimate=pl.CostEstimate(flops=flops, bytes_accessed=moved, transcendentals=0),
    )(*operands)


def f32(*shape):
    return jax.ShapeDtypeStruct(shape, jnp.float32)


def b16(*shape):
    return jax.ShapeDtypeStruct(shape, jnp.bfloat16)


HEAD_ROWS = 16
GROUP = 3
VMEM_BYTES = 60 * 1024 * 1024


def scan_prep(width, wide_in, small, cosine, sine, keep, conv_kernel, conv_bias, *rest):
    rows = wide_in.shape[0]
    steps = width // LEN // GROUP
    outs = [
        f32(rows, width),
        b16(rows, width),
        f32(rows, width),
        f32(rows, 2 * LEN),
        f32(rows, 2 * LEN),
        f32(rows, LEN),
        f32(rows, LEN),
        f32(HEAD_ROWS, 1, rows),
        f32(HEAD_ROWS, 1, rows),
        f32(HEAD_ROWS, rows),
        f32(HEAD_ROWS, rows),
        b16(rows, 2 * LEN),
        b16(rows, LEN),
    ]
    scratch = [pltpu.VMEM((rows + 8, LEN), jnp.float32), pltpu.VMEM((3, rows + 8, LEN), jnp.float32)]
    operands = (wide_in, small, cosine, sine, keep, conv_kernel, conv_bias, *rest)
    specs = [tile(rows, 0, steps), None, None, None, None, tile(4), tile(1)] + [None] * len(rest)
    return call(prep_kernel, steps, outs, [tile(rows)] * 3 + [None] * 10, scratch, operands, specs, 10**9)


def scan_forward(chunks, heads, wide_in, x, xb, *rest):
    width = x.shape[1]
    rows = LEN * len(chunks)
    at = chunks[0] // len(chunks)
    count = sum(min(i, 2) + 1 for i in chunks)
    outs = [f32(rows, width), f32(rows, width), f32(1, rows)]
    scratch = [
        pltpu.VMEM((heads, rows, LEN), jnp.float32),
        pltpu.VMEM((count, LEN, LEN), jnp.float32),
        pltpu.VMEM((count, LEN, LEN), jnp.float32),
        pltpu.VMEM((len(chunks), 2 * LEN, 3 * LEN), jnp.bfloat16),
        pltpu.VMEM((rows, LEN), jnp.float32),
    ]
    specs = [tile(rows, at), tile(rows, at), tile((chunks[-1] + 1) * LEN)] + [None] * (len(rest) - 1) + [tile(1)]
    kernel = functools.partial(scan_kernel, chunks, heads)
    operands = (wide_in, x, xb, *rest)
    return call(kernel, heads // 2 // GROUP, outs, [tile(rows), tile(rows), None], scratch, operands, specs, 2 * 10**9)


def attention_forward(chunks, q, kv, seg_col, seg_row):
    rows = LEN * len(chunks)
    outs = [b16(rows, q.shape[1]), f32(8, rows)]
    kernel = functools.partial(attention_kernel, chunks)
    return call(kernel, 1, outs, [None] * 2, [], (q, kv, seg_col, seg_row), [None] * 4, 10**9)


def attention_backward(chunks, final, *operands):
    q = operands[0]
    rows = q.shape[0]
    partial = [f32(rows, LEN), f32(rows, LEN)]
    sums = [pltpu.VMEM((rows, LEN), jnp.float32)] * 2
    outs = [b16(LEN * len(chunks), q.shape[1])] + ([b16(rows, LEN)] if final else partial)
    scratch = (sums if final else []) + [
        pltpu.VMEM((rows, LEN), jnp.bfloat16),
        pltpu.VMEM((HEAD_DIM, rows), jnp.bfloat16),
    ]
    kernel = functools.partial(attention_back_kernel, chunks, final)
    return call(kernel, 1, outs, [None] * len(outs), scratch, operands, [None] * len(operands), 2 * 10**9)


def scan_backward(chunks, heads, *operands):
    rows, width = operands[0].shape
    at = chunks[0] // len(chunks)
    sources = (chunks[-1] + 1) * LEN
    count = sum(min(i, 2) + 1 for i in chunks)
    outs = [
        b16(rows, width),
        f32(rows, width),
        f32(sources, width),
        f32(HEAD_ROWS, rows),
        f32(sources, LEN),
        f32(rows, LEN),
        f32(8, width),
    ]
    scratch = [
        pltpu.VMEM((rows, LEN), jnp.bfloat16),
        pltpu.VMEM((heads, sources, LEN), jnp.float32),
        pltpu.VMEM((count, LEN, LEN), jnp.float32),
        pltpu.VMEM((count, LEN, LEN), jnp.float32),
        pltpu.VMEM((count, LEN, LEN), jnp.float32),
        pltpu.VMEM((rows, LEN), jnp.float32),
        pltpu.VMEM((rows, LEN), jnp.float32),
        pltpu.VMEM((2 * LEN, 3 * LEN), jnp.float32),
        pltpu.VMEM((2 * LEN, 3 * LEN), jnp.bfloat16),
    ]
    specs = [tile(rows), tile(rows), None, None, None, None, tile(1), tile(rows, at), tile(rows), tile(rows, at), tile(sources)]
    specs += [None, None, None, tile(1), None, None, tile(HEAD_ROWS)]
    out_specs = [tile(rows), tile(rows), tile(sources), None, None, None, tile(8)]
    kernel = functools.partial(scan_back_kernel, chunks, heads)
    return call(kernel, heads // 2 // GROUP, outs, out_specs, scratch, operands, specs, 4 * 10**9)


def scan_end(heads, *operands):
    rows, width = 2 * operands[0].shape[0], operands[0].shape[1]
    steps = heads // 2 // GROUP
    outs = [
        b16(rows, width),
        b16(rows, 2 * LEN),
        b16(rows, LEN),
        f32(8, width),
        f32(8, 2 * LEN),
        f32(2 * HEAD_ROWS, LEN),
    ]
    scratch = [
        pltpu.VMEM((rows + 8, LEN), jnp.float32),
        pltpu.VMEM((rows + 8, LEN), jnp.float32),
        pltpu.VMEM((3, rows + 8, LEN), jnp.float32),
        pltpu.VMEM((HEAD_ROWS, rows), jnp.float32),
        pltpu.VMEM((HEAD_ROWS, rows), jnp.float32),
    ]
    half = rows // 2
    specs = [tile(half), tile(half), tile(half), tile(rows)] + [None] * 6 + [tile(rows), tile(rows), None]
    specs += [tile(rows, 0, steps)] + [None] * 4 + [tile(1), None, None, None, tile(HEAD_ROWS), tile(4), None]
    out_specs = [tile(rows), None, None, tile(8), None, None]
    kernel = functools.partial(scan_end_kernel, heads)
    return call(kernel, steps, outs, out_specs, scratch, operands, specs, 2 * 10**9)


def assemble_kernel(
    core_ref, own_ref, far_ref, mixer_out_ref, attn_out_ref, mixer_proj_ref, query_ref, pair_ref, state_ref, step_ref
):
    at = pl.program_id(0)
    count = pl.num_programs(0)
    width = mixer_proj_ref.shape[2]
    model_width = mixer_out_ref.shape[1]
    split = mixer_out_count(width)

    def write(source):
        @pl.when(at < split)
        def _():
            mixer_out_ref[...] = source[:, :model_width]

        @pl.when(at >= split)
        def _():
            attn_out_ref[...] = source[:, :model_width]

        start = model_width
        mixer_proj_ref[:, 0, :] = source[:, start : start + width]
        start += width
        query_ref[...] = source[:, start : start + query_ref.shape[1]]
        start += query_ref.shape[1]
        pair_ref[:, 0, :] = source[:, start : start + LEN]
        start += LEN
        mixer_proj_ref[:, 1, :] = source[:, start : start + width]
        start += width
        state_ref[...] = source[:, start : start + 2 * LEN]
        step_ref[...] = source[:, start + 2 * LEN :]

    mine = at // (count // 2) == core_ref[0]

    @pl.when(mine)
    def _():
        write(own_ref)

    @pl.when(jnp.logical_not(mine))
    def _():
        write(far_ref)


def mixer_out_count(width):
    return width // LEN


def assemble(own, far, width, query_width):
    half, columns = own.shape
    rows = 2 * half
    blocks = rows // LEN
    split = mixer_out_count(width)
    core = lax.axis_index("core").astype(jnp.int32).reshape(1)

    def source(flip):
        def index(at, core_ref):
            first = (blocks // 2) * jnp.where(flip, 1 - core_ref[0], core_ref[0])
            return (jnp.clip(at - first, 0, blocks // 2 - 1), 0)

        return pl.BlockSpec((LEN, columns), index)

    def plain(count):
        return pl.BlockSpec((LEN, count), lambda at, core_ref: (at, 0))

    out_specs = [
        pl.BlockSpec((LEN, rows), lambda at, core_ref: (jnp.minimum(at, split - 1), 0)),
        pl.BlockSpec((LEN, rows), lambda at, core_ref: (jnp.maximum(at - split, 0), 0)),
        pl.BlockSpec((LEN, 2, width), lambda at, core_ref: (at, 0, 0)),
        plain(query_width),
        pl.BlockSpec((LEN, 1, LEN), lambda at, core_ref: (at, 0, 0)),
        plain(2 * LEN),
        plain(LEN),
    ]
    out_shape = [
        f32(width, rows),
        f32(rows - width, rows),
        f32(rows, 2, width),
        f32(rows, query_width),
        f32(rows, 1, LEN),
        f32(rows, 2 * LEN),
        f32(rows, LEN),
    ]
    return pl.pallas_call(
        assemble_kernel,
        grid_spec=pltpu.PrefetchScalarGridSpec(
            num_scalar_prefetch=1, grid=(blocks,), in_specs=[source(False), source(True)], out_specs=out_specs
        ),
        out_shape=out_shape,
        compiler_params=pltpu.CompilerParams(vmem_limit_bytes=VMEM_BYTES),
        cost_estimate=pl.CostEstimate(flops=0, bytes_accessed=16 * own.size, transcendentals=0),
    )(core, own, far)


def silu_slope(argument):
    logistic = jax.nn.sigmoid(argument)
    return logistic * (1.0 + argument * (1.0 - logistic))


def rope_tables(rows):
    half_size = HEAD_DIM // 2
    inverse = np.float32(rope_base) ** (-(2.0 * np.arange(half_size, dtype=np.float32)) / HEAD_DIM)
    angles = np.arange(rows, dtype=np.float32)[:, None] * inverse.astype(np.float32)[None, :]
    cosine, sine = np.cos(angles), np.sin(angles)
    return (
        np.concatenate([cosine] * 4, axis=1).astype(np.float32),
        np.concatenate([-sine, sine, -sine, sine], axis=1).astype(np.float32),
    )


def norm_backward(grad_unit, unit_rows, inv_rms):
    return inv_rms * (grad_unit - unit_rows * jnp.mean(grad_unit * unit_rows, axis=-1, keepdims=True))


def dot32(left, right):
    return jnp.dot(left, right, preferred_element_type=jnp.float32)


def after(value, *others):
    return lax.optimization_barrier((value, *others))[0]


def swap(values, name):
    return lax.ppermute(values, name, PAIR)


def exchange(values, name):
    return values + swap(values, name)


def core_rows(values, index):
    half = values.shape[1] // 2
    return lax.dynamic_slice_in_dim(values, index * half, half, 1)


def rows_dot(left, right, index):
    return lax.dot_general(core_rows(left, index), right, (((0,), (0,)), ((), ())), preferred_element_type=jnp.float32)


def on_device(
    layer_input,
    segments,
    input_gain,
    mixer_proj,
    state_proj,
    step_proj,
    step_bias,
    decay_log,
    skip_gain,
    conv_kernel,
    conv_bias,
    state_kernel,
    state_bias,
    gated_gain,
    mixer_out,
    query_proj,
    key_value_weight,
    attn_out,
    ffn_gain,
    ffn_gate,
    ffn_up,
    ffn_down,
    cotangent,
):
    segment = segments.reshape(-1)
    rows, model_width = layer_input.shape
    width = mixer_proj.shape[2]
    heads = step_proj.shape[1]
    state_size = state_proj.shape[1] // 2
    query_width = query_proj.shape[1]
    pair_width = key_value_weight.shape[2]
    place = lax.axis_index("core")
    cosine, sine = rope_tables(rows)
    select = np.arange(HEAD_ROWS)[:, None] == np.arange(width)[None, :] // HEAD_DIM
    select = jnp.asarray(select.astype(np.float32)).astype(jnp.bfloat16)
    seg_col, seg_row = segment[:, None], segment[None, :]
    keep = [jnp.ones((rows,), jnp.float32)]
    for lag in (1, 2, 3):
        previous = jnp.concatenate([jnp.full((lag,), -1, jnp.int32), segment[:-lag]])
        keep.append((previous == segment).astype(jnp.float32))
    keep = jnp.pad(jnp.stack(keep, axis=1), ((0, 8), (0, 4)))
    pad_heads = ((0, 0), (0, LEN - heads))
    rate_row = jnp.pad(-jnp.exp(decay_log)[None, :], pad_heads)
    step_bias_row = jnp.pad(step_bias[None, :], pad_heads)
    skip_row = jnp.repeat(skip_gain, HEAD_DIM)[None, :]
    gain_row = gated_gain[None, :]
    wide_proj = mixer_proj.reshape(model_width, 2 * width)
    small_proj = jnp.concatenate(
        [
            state_proj,
            query_proj,
            key_value_weight.reshape(model_width, pair_width),
            jnp.pad(step_proj, pad_heads),
        ],
        axis=1,
    )

    tokens = layer_input.astype(jnp.float32)
    inv_rms_in = lax.rsqrt(jnp.mean(tokens * tokens, axis=-1, keepdims=True) + norm_eps)
    unit_in = tokens * inv_rms_in
    normed_input = (unit_in * input_gain).astype(jnp.bfloat16)
    small_in = dot32(normed_input, small_proj)
    wide_in = dot32(normed_input, wide_proj)
    x, xb, slope, state, state_slope, cum, lag, cum_row, lag_row, step_row, sig_row, queries, pairs = scan_prep(
        width,
        wide_in,
        small_in,
        cosine,
        sine,
        keep,
        conv_kernel,
        conv_bias[None, :],
        state_kernel,
        state_bias[None, :],
        step_bias_row,
        rate_row,
    )

    blocks = rows // LEN
    late = tuple(range(blocks // 2, blocks))
    early = tuple(range(blocks // 2))
    half = {}
    ready = None
    for chunks in (late, early):
        span = slice(chunks[0] * LEN, (chunks[-1] + 1) * LEN)
        h = {"span": span}
        lag_now = lag_row if ready is None else after(lag_row, ready)
        h["y"], h["gated"], h["square"] = scan_forward(
            chunks, heads, wide_in, x, xb, state, cum, lag_now, seg_col, seg_row, skip_row
        )
        h["attended"], h["lse"] = attention_forward(chunks, after(queries, h["square"]), pairs, seg_col, seg_row)
        h["square_far"] = swap(h["square"], "tensor")
        squares = after(h["square"] + h["square_far"], h["lse"])
        h["inv_gated"] = lax.rsqrt(squares.reshape(-1, 1) / DSSM + norm_eps)
        h["mixer_rows"] = (h["gated"] * h["inv_gated"] * gated_gain).astype(jnp.bfloat16)
        h["part"] = dot32(h["mixer_rows"], mixer_out) + dot32(h["attended"], attn_out)
        h["branch_far"] = swap(h["part"], "tensor")
        ready = h["part"]
        half[chunks] = h

    ready = None
    for chunks in (late, early):
        h = half[chunks]
        span = h["span"]
        far = h["branch_far"] if ready is None else after(h["branch_far"], ready)
        hidden = tokens[span] + (h["part"] + far)
        inv_rms_ffn = lax.rsqrt(jnp.mean(hidden * hidden, axis=-1, keepdims=True) + norm_eps)
        unit_ffn = hidden * inv_rms_ffn
        normed_ffn = (unit_ffn * ffn_gain).astype(jnp.bfloat16)
        gate_rows = dot32(normed_ffn, ffn_gate)
        up_rows = dot32(normed_ffn, ffn_up)
        gate_silu = jax.nn.silu(gate_rows)
        activated = (gate_silu * up_rows).astype(jnp.bfloat16)
        grad_activated = dot32(cotangent[span], ffn_down.T)
        grad_gate_rows = (grad_activated * up_rows * silu_slope(gate_rows)).astype(jnp.bfloat16)
        grad_up_rows = (grad_activated * gate_silu).astype(jnp.bfloat16)
        partial_ffn = dot32(grad_gate_rows, ffn_gate.T) + dot32(grad_up_rows, ffn_up.T)
        h["part_ffn"] = partial_ffn
        h["ffn_far"] = swap(partial_ffn, "tensor")
        ready = partial_ffn
        h.update(
            hidden=hidden,
            unit_ffn=unit_ffn,
            inv_rms_ffn=inv_rms_ffn,
            normed_ffn=normed_ffn,
            activated=activated,
            grad_gate_rows=grad_gate_rows,
            grad_up_rows=grad_up_rows,
        )

    def whole(name):
        return jnp.concatenate([half[early][name], half[late][name]], axis=0)

    normed_ffn = whole("normed_ffn")
    sides = [
        (normed_ffn, whole("grad_gate_rows")),
        (normed_ffn, whole("grad_up_rows")),
        (whole("activated"), cotangent),
    ]
    sent = [swap(rows_dot(left, right, 1 - place), "core") for left, right in sides]
    kept = [rows_dot(left, right, place) for left, right in sides]
    first = jnp.concatenate([a + b for a, b in zip(kept, sent)], axis=1)
    first_sum = lax.psum_scatter(first, ("y", "x"), scatter_dimension=0, tiled=True)
    depth = first_sum.shape[0] // 2
    zh = lax.axis_index("zh")
    first_own = lax.dynamic_slice_in_dim(first_sum, zh * depth, depth, 0) + swap(
        lax.dynamic_slice_in_dim(first_sum, (1 - zh) * depth, depth, 0), "zh"
    )
    first_all = lax.all_gather(first_own, ("core", "y", "x", "zh"), axis=0, tiled=True)

    grad_ffn_gain = 0.0
    ready = first
    for chunks in (late, early):
        h = half[chunks]
        span = h["span"]
        grad_normed_ffn = h["part_ffn"] + after(h["ffn_far"], ready)
        grad_ffn_gain = grad_ffn_gain + jnp.sum(grad_normed_ffn * h["unit_ffn"], axis=0)
        h["grad_hidden"] = cotangent[span].astype(jnp.float32) + norm_backward(
            grad_normed_ffn * ffn_gain, h["unit_ffn"], h["inv_rms_ffn"]
        )
        grad_branch = h["grad_hidden"].astype(jnp.bfloat16)
        h["grad_branch"] = grad_branch
        grad_mixer_rows = dot32(grad_branch, mixer_out.T)
        unit_gated = h["gated"] * h["inv_gated"]
        gated_dot = jnp.sum(grad_mixer_rows * gated_gain * unit_gated, axis=-1)[None, :]
        dot_far = swap(gated_dot, "tensor")
        grad_attended = dot32(after(grad_branch, gated_dot), attn_out.T).astype(jnp.bfloat16)
        operands = (queries, pairs, grad_attended, h["lse"], seg_col, seg_row, cosine, sine)
        if chunks == late:
            h["grad_queries"], grad_keys, grad_values = attention_backward(chunks, False, *operands)
        else:
            h["grad_queries"], grad_pairs = attention_backward(chunks, True, *operands, grad_keys, grad_values)
        h["grad_gate"], h["gy"], h["dx"], h["p"], h["grad_in"], h["grad_out"], h["sums"] = scan_backward(
            chunks,
            heads,
            grad_mixer_rows,
            h["gated"],
            h["square"],
            h["square_far"],
            gated_dot,
            after(dot_far, h["grad_queries"]),
            gain_row,
            wide_in,
            h["y"],
            x,
            xb,
            state,
            lag,
            cum_row,
            skip_row,
            seg_col,
            seg_row,
            select,
        )
        ready = h["p"]
    down = dot32(whole("activated"), ffn_down)
    down_far = swap(after(down, dot_far), "tensor")
    ends = []
    for name in ("gy", "dx", "p", "grad_in", "grad_out"):
        ends += [half[early][name], half[late][name]]
    grad_conv, grad_state, grad_step, conv_sum, state_sum, step_sum = scan_end(
        heads,
        *ends,
        xb,
        slope,
        state_slope,
        wide_in,
        small_in,
        step_row,
        sig_row,
        rate_row,
        skip_row,
        keep,
        seg_col,
        seg_row,
        select,
        conv_kernel,
        state_kernel,
    )

    grad_queries, grad_gate = whole("grad_queries"), whole("grad_gate")
    outer = jnp.concatenate([whole("mixer_rows"), whole("attended")], axis=1)
    grad_branch = whole("grad_branch")
    right = jnp.concatenate([grad_gate, grad_queries, grad_pairs, grad_conv, grad_state, grad_step], axis=1)
    far_outer = swap(rows_dot(outer, grad_branch, 1 - place), "core")
    far_inner = swap(rows_dot(normed_input, right, 1 - place), "core")

    wide_grad = jnp.concatenate([grad_gate, grad_conv], axis=1)
    small_grad = jnp.concatenate([grad_state, grad_queries, grad_pairs, grad_step], axis=1)
    partial_normed = dot32(wide_grad, wide_proj.T) + dot32(small_grad, small_proj.T)
    normed_far = swap(partial_normed, "tensor")
    sums = half[early]["sums"] + half[late]["sums"]
    over_tensor = [jnp.sum(partial_normed * unit_in, axis=0), state_sum[:4], state_sum[4]]
    alone = [
        step_sum[:heads, 0],
        step_sum[HEAD_ROWS : HEAD_ROWS + heads, 0],
        jnp.sum(sums[0].reshape(heads, HEAD_DIM), axis=1),
        conv_sum[:4],
        conv_sum[4],
        sums[1],
        grad_ffn_gain,
    ]

    def packed(values):
        flat = jnp.concatenate([v.reshape(-1) for v in values])
        count = -(-flat.shape[0] // model_width)
        return jnp.pad(flat, (0, count * model_width - flat.shape[0])).reshape(count, model_width)

    def unpacked(table, values):
        flat, result, start = table.T.reshape(-1), [], 0
        for v in values:
            result.append(flat[start : start + v.size].reshape(v.shape))
            start += v.size
        return result

    tables = [packed(over_tensor), packed(alone)]
    shared_end = heads + tables[0].shape[0]
    table = jnp.concatenate(tables, axis=0)
    table_end = heads + table.shape[0]
    table = (core_rows(table, place) + swap(core_rows(table, 1 - place), "core")).T
    table = jnp.pad(table, ((0, 0), (heads, LEN - table_end)))
    kept_outer, kept_inner = rows_dot(outer, grad_branch, place), rows_dot(normed_input, right, place)
    at_step = model_width + 2 * width + query_width + pair_width + 2 * state_size
    inner = kept_inner + far_inner
    inner_end = at_step - model_width
    second = jnp.concatenate([kept_outer + far_outer, inner[:, :inner_end], inner[:, inner_end:] + table], axis=1)
    devices = 32
    own_rows = second.shape[0] // devices
    columns = second.shape[1]
    second = after(second, first_own)
    second = lax.all_to_all(second.reshape(devices, own_rows, columns), ("y", "zh", "x"), 0, 0, tiled=True)
    second = jnp.sum(second, axis=0)
    at_state = at_step - 2 * state_size
    both = second[:, at_state:]
    summed = exchange(both, "tensor")
    lane = np.arange(both.shape[1]) - 2 * state_size
    is_shared = (lane < 0) | ((lane >= heads) & (lane < shared_end))
    second = jnp.concatenate([second[:, :at_state], jnp.where(is_shared[None, :], summed, both)], axis=1)
    second = jnp.broadcast_to(second[None], (devices, own_rows, columns))
    second = lax.all_to_all(second, ("y", "zh", "x"), 0, 0, tiled=True).reshape(devices * own_rows, columns)
    second_far = swap(second, "core")
    grad_mixer_out, grad_attn_out, grad_mixer_proj, grad_query_proj, grad_keyval, grad_state_proj, step_block = assemble(
        second, second_far, width, query_width
    )

    grad_hidden = whole("grad_hidden")
    grad_normed = partial_normed + normed_far
    input_grad = grad_hidden + norm_backward(grad_normed * input_gain, unit_in, inv_rms_in)
    layer_output = (whole("hidden") + (down + down_far)).astype(jnp.bfloat16)

    small_shared = unpacked(step_block[:, heads:shared_end], over_tensor)
    small_alone = unpacked(step_block[:, shared_end:table_end], alone)
    return (
        layer_output,
        input_grad,
        small_shared[0],
        grad_mixer_proj,
        grad_state_proj,
        step_block[:, :heads],
        small_alone[0],
        small_alone[1],
        small_alone[2],
        small_alone[3],
        small_alone[4],
        small_shared[1],
        small_shared[2],
        small_alone[5],
        grad_mixer_out,
        grad_query_proj,
        grad_keyval,
        grad_attn_out,
        small_alone[6],
        first_all[:, :model_width],
        first_all[:, model_width : 2 * model_width],
        first_all[:, 2 * model_width :],
    )


def solution(mesh):
    dp, whole_spec, columns = P(DP, None), P(), P(None, "tensor")
    per_channel, middle = P("tensor"), P(None, "tensor", None)
    last, by_rows = P(None, None, "tensor"), P("tensor", None)
    weights = (
        whole_spec,
        last,
        whole_spec,
        columns,
        per_channel,
        per_channel,
        per_channel,
        columns,
        per_channel,
        whole_spec,
        whole_spec,
        per_channel,
        by_rows,
        columns,
        middle,
        by_rows,
        whole_spec,
        columns,
        columns,
        by_rows,
    )
    mesh = jax.sharding.Mesh(mesh.devices.reshape(4, 2, 4, 2, 2), (*DP, "tensor"))
    return jax.shard_map(
        on_device, mesh=mesh, in_specs=(dp, dp, *weights, dp), out_specs=(dp, dp, *weights), check_vma=False
    )
```

time: 748 us -> 617 us (0.82)
  blocking collectives: 0 us -> 183 us
  starting transfers between devices: 150 us -> 22.6 us
  waiting for transfers between devices: 256 us -> 156 us
  local copies, waits for them, and re-layouts: 145 us -> 54.8 us
  other arithmetic: 74.6 us -> 36.2 us
  Pallas kernels: 33.1 us -> 70.2 us
  matrix products: 61 us -> 69 us
    all_to_all x0 -> x2, blocking collectives: none -> 183 us  [the longest x1 91.6 us: on_device(): lax.all_to_all(second.reshape(devices, own_rows, columns), ('y', 'zh', 'x...]
    ppermute x80 -> x0, waiting for transfers between devices: 152 us -> none  [the longest x24 65.1 us: second_halving(): return take(values, index, axis) + lax.ppermute(sent, name, LINKS[link])]
    ppermute x80 -> x0, starting transfers between devices: 74 us -> none  [the longest x24 27.6 us: second_halving(): return take(values, index, axis) + lax.ppermute(sent, name, LINKS[link])]
    ppermute x25 -> x19, starting transfers between devices: 75.6 us -> 22.5 us  [swap(): return lax.ppermute(values, name, PAIR)]
    ppermute x25 -> x19, waiting for transfers between devices: 104 us -> 156 us  [swap(): return lax.ppermute(values, name, PAIR)]
    unnamed x453 -> x226, local copies, waits for them, and re-layouts: 72.3 us -> 26.5 us
    pallas_call x10 -> x11, Pallas kernels: 33.1 us -> 70.2 us  [the longest x10 57.4 us: call(): pl.pallas_call(kernel, grid=(steps,), out_shape=out_shape, in_specs=[s or...]
    select_n x40 -> x0, other arithmetic: 26 us -> none  [the longest x28 25 us: either(): jnp.where(chosen, jnp.concatenate([first, second], axis), jnp.concatenate...]
  transfers between devices with their start and end apart: 106 -> 21, of which waited for: 48 -> 7; matrix products, arithmetic and copies ran while one was open for 24% -> 17% of each run, Pallas kernels for 4% -> 10%
where the time goes in v3:
time: 617 us; the launch traced here: 607 us
  blocking collectives  183 us (30%)
  waiting for transfers between devices  156 us (25%)
  Pallas kernels  70.2 us (11%)
  matrix products  69 us (11%)
  local copies, waits for them, and re-layouts  54.8 us (9%)
  other arithmetic  36.2 us (6%)
  starting transfers between devices  22.6 us (4%)
  between operations  15.6 us (3%)
    ppermute x19, waiting for transfers between devices, swap(): return lax.ppermute(values, name, PAIR)  156 us
    all_to_all x1, blocking collectives, on_device(): lax.all_to_all(second.reshape(devices, own_rows, columns), ('y', 'zh', 'x...  91.6 us
    all_to_all x1, blocking collectives, on_device(): lax.all_to_all(second, ('y', 'zh', 'x'), 0, 0, tiled=True)  91.2 us
    pallas_call x10, Pallas kernels, call(): pl.pallas_call(kernel, grid=(steps,), out_shape=out_shape, in_specs=[s or...  57.4 us
    dot_general x23, matrix products, dot32(): return jnp.dot(left, right, preferred_element_type=jnp.float32)  37 us
    dot_general x10, matrix products, rows_dot(): lax.dot_general(core_rows(left, index), right, (((0,), (0,)), ((), ())),...  32 us
    unnamed x226, local copies, waits for them, and re-layouts  26.5 us
    ppermute x19, starting transfers between devices, swap(): return lax.ppermute(values, name, PAIR)  22.5 us
  transfers between devices with their start and end apart: 21, of which 7 were waited for; matrix products, arithmetic and copies ran while one was open for 17% of the time, Pallas kernels for 10%

profile of v3, /device:TPU:1, one launch (start us, length us, event | category | flops | bytes accessed | tf_op | source)
XLA Modules:
  0.0 607.2 jit_solution(14423948837419977089)
XLA Ops:
  9.0 4.2 copy.88
  18.8 5.8 fusion.73.conv_ref.gate_ref
  24.6 2.2 fusion.62.small_ref
  26.8 6.6 %shard_map.426 = (f32[512,768]{1,0:T(8,128)}, bf16[512,768]{1,0:T(8,128)(2,1)}, f32[512,768]{1,0:T(8,128)}, f32[512,256]{1,0:T(8,128)}, f32[512,256]{1,0:T(8,128...) custom-call(f32[512,1536]{1,0:T(8,128)} %fusion.73.conv_ref.gate_ref, ...), custom_call_target="tpu_custom_call" | custom-call | flops 1000000000 | bytes 11310336 | tf_op jit(solution)/shard_map/pallas_call | solution.py:656
  33.4 5.3 shard_map.427
  38.7 2.5 collective-permute-start
  41.1 3.5 fusion.38
  44.6 4.7 shard_map.428
  56.6 4.4 shard_map.429
  62.5 4.0 shard_map.430
  66.5 14.1 %collective-permute-done.1.square_b_ref = f32[1,256]{1,0:T(1,128)S(1)} collective-permute-done((f32[1,256]{1,0:T(1,128)}, f32[1,256]{1,0:T(1,128)S(1)}, u32[]{:S(2)}, u32[]{:S(2)}) %collective-permute-start.1) | collective-permute-done | bytes 1056 | tf_op jit(solution)/shard_map/ppermute | solution.py:923
  91.2 14.7 %collective-permute-done.2 = f32[256,1024]{1,0:T(8,128)S(1)} collective-permute-done((f32[256,1024]{1,0:T(8,128)S(1)}, f32[256,1024]{1,0:T(8,128)S(1)}, u32[]{:S(2)}, u32[]{:S(2)}) %collective-permute-start.2) | collective-permute-done | bytes 1048608 | tf_op jit(solution)/shard_map/ppermute | solution.py:923
  112.2 2.8 collective-permute-start.7
  115.0 2.1 fusion.29
  117.2 2.1 fusion.23
  119.9 2.9 convolution_add_fusion.3
  122.9 2.5 convolution_add_fusion.2
  125.5 2.3 convolution_add_fusion.4
  127.8 3.1 pad_maximum_fusion.1
  132.0 2.5 fusion.80
  137.5 18.6 %collective-permute-done.5 = f32[256,1024]{1,0:T(8,128)S(1)} collective-permute-done((f32[256,1024]{1,0:T(8,128)}, f32[256,1024]{1,0:T(8,128)S(1)}, u32[]{:S(2)}, u32[]{:S(2)}) %collective-permute-start.5) | collective-permute-done | bytes 1048608 | tf_op jit(solution)/shard_map/ppermute | solution.py:923
  161.5 4.6 shard_map.431
  166.1 12.5 %collective-permute-done.9.dot_b_ref = f32[1,256]{1,0:T(1,128)S(1)} collective-permute-done((f32[1,256]{1,0:T(1,128)S(1)}, f32[1,256]{1,0:T(1,128)S(1)}, u32[]{:S(2)}, u32[]{:S(2)}) %collective-permute-start.9) | collective-permute-done | bytes 1056 | tf_op jit(solution)/shard_map/ppermute | solution.py:923
  179.2 8.4 %shard_map.432 = (bf16[256,768]{1,0:T(8,128)(2,1)}, f32[256,768]{1,0:T(8,128)}, f32[512,768]{1,0:T(8,128)}, f32[16,256]{1,0:T(8,128)}, f32[512,128]{1,0:T(8,128)}, /*index=5*/f32[256,128]{1,0:T(8,128)}, f32[8,768]{1,0:T(8,128)}) custom-call(f32[256,768]{1,0:T(8,128)} %get-tuple-element.265.gmr_ref, f32[256,768]{1,0:T(8,128)} %get-tuple-element.96.gated_ref, ...), custom_call_target="tpu_custom_call" | custom-call | flops 4000000000 | bytes 11909120 | tf_op jit(solution)/shard_map/pallas_call | solution.py:656
  187.7 2.6 multiply_reduce_fusion.3
  190.3 3.0 fusion.68
  196.4 4.4 shard_map.433
  201.4 6.6 %shard_map.434 = (bf16[256,768]{1,0:T(8,128)(2,1)}, f32[256,768]{1,0:T(8,128)}, f32[256,768]{1,0:T(8,128)}, f32[16,256]{1,0:T(8,128)}, f32[256,128]{1,0:T(8,128)}, /*index=5*/f32[256,128]{1,0:T(8,128)}, f32[8,768]{1,0:T(8,128)}) custom-call(f32[256,768]{1,0:T(8,128)} %get-tuple-element.267.gmr_ref, f32[256,768]{1,0:T(8,128)} %get-tuple-element.105.gated_ref, ...), custom_call_target="tpu_custom_call" | custom-call | flops 4000000000 | bytes 10991616 | tf_op jit(solution)/shard_map/pallas_call | solution.py:656
  212.6 8.5 %shard_map.435 = (bf16[512,768]{1,0:T(8,128)(2,1)}, bf16[512,256]{1,0:T(8,128)(2,1)}, bf16[512,128]{1,0:T(8,128)(2,1)}, f32[8,768]{1,0:T(8,128)}, f32[8,256]{1,0:T(8,128)}, /*index=5*/f32[32,128]{1,0:T(8,128)}) custom-call(f32[256,768]{1,0:T(8,128)} %get-tuple-element.130.gy_a_ref, f32[256,768]{1,0:T(8,128)} %get-tuple-element.131.gy_b_ref, ...), custom_call_target="tpu_custom_call" | custom-call | flops 2000000000 | bytes 13582080 | tf_op jit(solution)/shard_map/pallas_call | solution.py:656
  221.1 2.2 constant_dynamic-update-slice_fusion.2
  225.6 5.4 fusion.31
  234.4 2.3 convolution_add_fusion.5
  238.1 3.7 fusion.21
  243.0 3.5 collective-permute-start.16
  247.9 43.3 %collective-permute-done.16 = f32[16,3072]{1,0:T(8,128)S(1)} collective-permute-done((f32[16,3072]{1,0:T(8,128)S(1)}, f32[16,3072]{1,0:T(8,128)S(1)}, u32[]{:S(2)}, u32[]{:S(2)}) %collective-permute-start.16) | collective-permute-done | bytes 196640 | tf_op jit(solution)/shard_map/ppermute | solution.py:923
  297.7 3.0 multiply_reduce_fusion
  302.4 4.2 convolution_add_fusion.1
  307.8 4.7 convolution_add_fusion
  314.6 91.6 %all_to_all.10 = f32[32,16,3328]{2,1,0:T(8,128)} all-to-all(f32[32,16,3328]{2,1,0:T(8,128)S(1)} %bitcast.82), channel_id=1, replica_groups=mesh['y'=4,'zh'=2,'x'=4,'core'=2,'tensor'=2] {'y','zh','x'}, dimensions={0} | all-to-all | bytes 13631488 | tf_op jit(solution)/shard_map/all_to_all | solution.py:1210
  406.2 3.3 reduce_sum.129
  409.6 2.6 collective-permute-done.17
  413.1 91.2 %all_to_all.11 = f32[32,16,3328]{2,1,0:T(8,128)S(1)} all-to-all(f32[32,16,3328]{2,1,0:T(8,128)S(1)} %broadcast_in_dim.63), channel_id=1, replica_groups=mesh['y'=4,'zh'=2,'x'=4,'core'=2,'tensor'=2] {'y','zh','x'}, dimensions={0} | all-to-all | bytes 13631488 | tf_op jit(solution)/shard_map/all_to_all | solution.py:1219
  504.3 3.7 collective-permute-start.18
  510.0 50.0 %collective-permute-done.11 = f32[512,1024]{1,0:T(8,128)S(1)} collective-permute-done((f32[512,1024]{1,0:T(8,128)S(1)}, f32[512,1024]{1,0:T(8,128)S(1)}, u32[]{:S(2)}, u32[]{:S(2)}) %collective-permute-start.11) | collective-permute-done | bytes 2097184 | tf_op jit(solution)/shard_map/ppermute | solution.py:923
  561.5 4.2 maximum_add_fusion.1
  565.7 2.8 copy-done.27
  568.5 12.8 %shard_map.436 = (f32[768,1024]{1,0:T(8,128)}, f32[256,1024]{1,0:T(8,128)}, f32[1024,2,768]{2,1,0:T(2,128)}, f32[1024,256]{1,0:T(8,128)}, f32[1024,1,128]{2,1,0:...) custom-call(s32[1]{0:T(128)} %bitcast.15.core_ref, f32[512,3328]{1,0:T(8,128)} %bitcast.81, f32[512,3328]{1,0:T(8,128)} %copy-done.27), custom_call_target="tpu_custom_call" | custom-call | bytes 27262976 | tf_op jit(solution)/shard_map/pallas_call | solution.py:883
  590.0 10.3 %fusion.70 = (f32[1024,1024]{1,0:T(8,128)}, f32[1024,1024]{1,0:T(8,128)}, f32[1024,1024]{1,0:T(8,128)}) fusion(f32[1024,3072]{1,0:T(8,128)} %all-gather.2.cloned.1.call-done), kind=kLoop, calls=%fused_computation.166 | loop fusion | bytes 25165824 | tf_op jit(solution)/shard_map/slice | solution.py:1254
  (355 shorter events, 85.4 us)
Async XLA Ops:
  7.2 79.7 %copy-start = (bf16[1024,1024]{1,0:T(8,128)(2,1)S(1)}, bf16[1024,1024]{1,0:T(8,128)(2,1)}, u32[]{:S(2)}) copy-start(bf16[1024,1024]{1,0:T(8,128)(2,1)} %param.47) | copy-start | bytes 6291460
  7.2 234.9 %reduce-scatter.2.cloned.1.call-start = ((), (), s32[]{:S(2)}) async-start(), calls=%async_computation.3 | async-start | bytes 6684672 | tf_op jit(solution)/shard_map/reduce_scatter | solution.py:1082
  8.9 9.5 %copy-start.76 = (f32[512]{0:T(512)}, f32[512]{0:T(512)S(1)}, u32[]{:S(2)}) copy-start(f32[512]{0:T(512)S(1)} %add_rsqrt_fusion) | copy-start | bytes 6148
  9.0 8.7 %copy-start.95 = (f32[12]{0:T(128)S(1)}, f32[12]{0:T(128)}, u32[]{:S(2)}) copy-start(f32[12]{0:T(128)} %param.35) | copy-start | bytes 148
  9.0 9.4 %copy-start.74 = (f32[1024]{0:T(1024)S(1)}, f32[1024]{0:T(1024)}, u32[]{:S(2)}) copy-start(f32[1024]{0:T(1024)} %param.29) | copy-start | bytes 12292
  38.7 12.2 %collective-permute-start = (f32[1,256]{1,0:T(1,128)}, f32[1,256]{1,0:T(1,128)S(1)}, u32[]{:S(2)}, u32[]{:S(2)}) collective-permute-start(f32[1,256]{1,0:T(1,128)} %get-tuple-element.97.square_a_ref), channel_id=1, source_target_pairs={{0,1},{1,0},{2,3},{3,2},{4,5},{5,4},{6,7},{7,6},{8,9},{9,8},{10,11... | collective-permute-start | bytes 3080 | tf_op jit(solution)/shard_map/ppermute | solution.py:923
  56.1 27.3 %collective-permute-start.3 = (f32[256,1024]{1,0:T(8,128)}, f32[256,1024]{1,0:T(8,128)}, u32[]{:S(2)}, u32[]{:S(2)}) collective-permute-start(f32[256,1024]{1,0:T(8,128)} %convolution_add_fusion.7), channel_id=1, source_target_pairs={{0,1},{1,0},{2,3},{3,2},{4,5},{5,4},{6,7},{7,6},{8,9},{9,8},{10,11... | collective-permute-start | bytes 3145736 | tf_op jit(solution)/shard_map/ppermute | solution.py:923
  61.0 19.6 %copy-start.88 = (f32[1,256]{1,0:T(1,128)S(1)}, f32[1,256]{1,0:T(1,128)}, u32[]{:S(2)}) copy-start(f32[1,256]{1,0:T(1,128)} %get-tuple-element.106.square_a_ref) | copy-start | bytes 3076
  61.0 21.0 %copy-start.8 = (bf16[768,1024]{1,0:T(8,128)(2,1)S(1)}, bf16[768,1024]{1,0:T(8,128)(2,1)}, u32[]{:S(2)}) copy-start(bf16[768,1024]{1,0:T(8,128)(2,1)} %param.41) | copy-start | bytes 4718596
  61.0 19.6 %collective-permute-start.1 = (f32[1,256]{1,0:T(1,128)}, f32[1,256]{1,0:T(1,128)S(1)}, u32[]{:S(2)}, u32[]{:S(2)}) collective-permute-start(f32[1,256]{1,0:T(1,128)} %get-tuple-element.106.square_a_ref), channel_id=1, source_target_pairs={{0,1},{1,0},{2,3},{3,2},{4,5},{5,4},{6,7},{7,6},{8,9},{9,8},{10,11... | collective-permute-start | bytes 3080 | tf_op jit(solution)/shard_map/ppermute | solution.py:923
  83.0 22.9 %collective-permute-start.2 = (f32[256,1024]{1,0:T(8,128)S(1)}, f32[256,1024]{1,0:T(8,128)S(1)}, u32[]{:S(2)}, u32[]{:S(2)}) collective-permute-start(f32[256,1024]{1,0:T(8,128)S(1)} %convolution_add_fusion.6), channel_id=1, source_target_pairs={{0,1},{1,0},{2,3},{3,2},{4,5},{5,4},{6,7},{7,6},{8,9},{9,8},{10,11... | collective-permute-start | bytes 3145736 | tf_op jit(solution)/shard_map/ppermute | solution.py:923
  86.2 30.9 %copy-start.22 = (bf16[256,1024]{1,0:T(8,128)(2,1)}, bf16[256,1024]{1,0:T(8,128)(2,1)S(1)}, u32[]{:S(2)}) copy-start(bf16[256,1024]{1,0:T(8,128)(2,1)S(1)} %multiply_convert_fusion.8) | copy-start | bytes 1572868
  88.7 21.5 %copy-start.45 = (bf16[256,1024]{1,0:T(8,128)(2,1)}, bf16[256,1024]{1,0:T(8,128)(2,1)S(1)}, u32[]{:S(2)}) copy-start(bf16[256,1024]{1,0:T(8,128)(2,1)S(1)} %get-tuple-element.254) | copy-start | bytes 1572868
  88.7 26.3 %copy-start.48 = (bf16[256,1024]{1,0:T(8,128)(2,1)}, bf16[256,1024]{1,0:T(8,128)(2,1)S(1)}, u32[]{:S(2)}) copy-start(bf16[256,1024]{1,0:T(8,128)(2,1)S(1)} %get-tuple-element.252) | copy-start | bytes 1572868
  88.7 28.4 %copy-start.41 = (bf16[256,1024]{1,0:T(8,128)(2,1)}, bf16[256,1024]{1,0:T(8,128)(2,1)S(1)}, u32[]{:S(2)}) copy-start(bf16[256,1024]{1,0:T(8,128)(2,1)S(1)} %get-tuple-element.253) | copy-start | bytes 1572868
  106.3 10.9 %copy-start.11 = (bf16[256,1024]{1,0:T(8,128)(2,1)}, bf16[256,1024]{1,0:T(8,128)(2,1)S(1)}, u32[]{:S(2)}) copy-start(bf16[256,1024]{1,0:T(8,128)(2,1)S(1)} %multiply_convert_fusion.5) | copy-start | bytes 1572868
  112.2 7.7 %collective-permute-start.7 = (f32[512,1024]{1,0:T(8,128)}, f32[512,1024]{1,0:T(8,128)}, u32[]{:S(2)}, u32[]{:S(2)}) collective-permute-start(f32[512,1024]{1,0:T(8,128)} %fusion.22), channel_id=1, source_target_pairs={{0,2},{2,0},{1,3},{3,1},{4,6},{6,4},{5,7},{7,5},{8,10},{10,8},{9,1... | collective-permute-start | bytes 6291464 | tf_op jit(solution)/shard_map/ppermute | solution.py:923
  117.1 5.8 collective-permute-start.8
  119.2 6.2 %collective-permute-start.6 = (f32[512,1024]{1,0:T(8,128)}, f32[512,1024]{1,0:T(8,128)}, u32[]{:S(2)}, u32[]{:S(2)}) collective-permute-start(f32[512,1024]{1,0:T(8,128)} %fusion.23), channel_id=1, source_target_pairs={{0,2},{2,0},{1,3},{3,1},{4,6},{6,4},{5,7},{7,5},{8,10},{10,8},{9,1... | collective-permute-start | bytes 6291464 | tf_op jit(solution)/shard_map/ppermute | solution.py:923
  131.0 459.0 %all-gather.2.cloned.1.call-start = ((), (), s32[]{:S(2)}) async-start(), calls=%async_computation.4 | async-start | bytes 12779520 | tf_op jit(solution)/shard_map/all_gather | solution.py:1088
  131.0 25.0 %collective-permute-start.5 = (f32[256,1024]{1,0:T(8,128)}, f32[256,1024]{1,0:T(8,128)S(1)}, u32[]{:S(2)}, u32[]{:S(2)}) collective-permute-start(f32[256,1024]{1,0:T(8,128)} %convolution_add_fusion.9), channel_id=1, source_target_pairs={{0,1},{1,0},{2,3},{3,2},{4,5},{5,4},{6,7},{7,6},{8,9},{9,8},{10,11... | collective-permute-start | bytes 3145736 | tf_op jit(solution)/shard_map/ppermute | solution.py:923
  134.6 21.5 %copy-start.20 = (f32[256,1024]{1,0:T(8,128)S(1)}, f32[256,1024]{1,0:T(8,128)}, u32[]{:S(2)}) copy-start(f32[256,1024]{1,0:T(8,128)} %convolution_add_fusion.9) | copy-start | bytes 3145732
  134.6 21.5 %copy-start.82 = (f32[256]{0:T(256)S(1)}, f32[256]{0:T(256)}, u32[]{:S(2)}) copy-start(f32[256]{0:T(256)} %copy-done.81) | copy-start | bytes 3076
  136.3 20.2 %copy-start.18 = (bf16[512,1024]{1,0:T(8,128)(2,1)S(1)}, bf16[512,1024]{1,0:T(8,128)(2,1)}, u32[]{:S(2)}) copy-start(bf16[512,1024]{1,0:T(8,128)(2,1)} %param.49) | copy-start | bytes 3145732
  136.3 51.3 %collective-permute-start.4 = (f32[256,1024]{1,0:T(8,128)}, f32[256,1024]{1,0:T(8,128)}, u32[]{:S(2)}, u32[]{:S(2)}) collective-permute-start(f32[256,1024]{1,0:T(8,128)} %convolution_add_fusion.8), channel_id=1, source_target_pairs={{0,1},{1,0},{2,3},{3,2},{4,5},{5,4},{6,7},{7,6},{8,9},{9,8},{10,11... | collective-permute-start | bytes 3145736 | tf_op jit(solution)/shard_map/ppermute | solution.py:923
  160.1 18.6 %collective-permute-start.9 = (f32[1,256]{1,0:T(1,128)S(1)}, f32[1,256]{1,0:T(1,128)S(1)}, u32[]{:S(2)}, u32[]{:S(2)}) collective-permute-start(f32[1,256]{1,0:T(1,128)S(1)} %bitcast.102), channel_id=1, source_target_pairs={{0,1},{1,0},{2,3},{3,2},{4,5},{5,4},{6,7},{7,6},{8,9},{9,8},{10,11... | collective-permute-start | bytes 3080 | tf_op jit(solution)/shard_map/ppermute | solution.py:923
  179.2 8.4 %copy-start.80 = (f32[256]{0:T(256)S(1)}, f32[256]{0:T(256)}, u32[]{:S(2)}) copy-start(f32[256]{0:T(256)} %copy-done.79) | copy-start | bytes 3076
  194.9 5.9 collective-permute-start.10
  201.4 8.5 %copy-start.60 = (bf16[256,768]{1,0:T(8,128)(2,1)S(1)}, bf16[256,768]{1,0:T(8,128)(2,1)}, u32[]{:S(2)}) copy-start(bf16[256,768]{1,0:T(8,128)(2,1)} %get-tuple-element.129) | copy-start | bytes 1179652
  201.4 9.3 %copy-start.67 = (bf16[256,256]{1,0:T(8,128)(2,1)S(1)}, bf16[256,256]{1,0:T(8,128)(2,1)}, u32[]{:S(2)}) copy-start(bf16[256,256]{1,0:T(8,128)(2,1)} %get-tuple-element.125) | copy-start | bytes 393220
  201.4 9.9 %copy-start.66 = (bf16[256,256]{1,0:T(8,128)(2,1)S(1)}, bf16[256,256]{1,0:T(8,128)(2,1)}, u32[]{:S(2)}) copy-start(bf16[256,256]{1,0:T(8,128)(2,1)} %get-tuple-element.114) | copy-start | bytes 393220
  231.0 76.8 %collective-permute-start.14 = (f32[512,2304]{1,0:T(8,128)}, f32[512,2304]{1,0:T(8,128)}, u32[]{:S(2)}, u32[]{:S(2)}) collective-permute-start(f32[512,2304]{1,0:T(8,128)} %fusion.31), channel_id=1, source_target_pairs={{0,2},{2,0},{1,3},{3,1},{4,6},{6,4},{5,7},{7,5},{8,10},{10,8},{9,1... | collective-permute-start | bytes 14155784 | tf_op jit(solution)/shard_map/ppermute | solution.py:923
  236.8 60.9 %collective-permute-start.12 = (f32[512,1024]{1,0:T(8,128)}, f32[512,1024]{1,0:T(8,128)}, u32[]{:S(2)}, u32[]{:S(2)}) collective-permute-start(f32[512,1024]{1,0:T(8,128)} %convolution_add_fusion.5), channel_id=1, source_target_pairs={{0,1},{1,0},{2,3},{3,2},{4,5},{5,4},{6,7},{7,6},{8,9},{9,8},{10,11... | collective-permute-start | bytes 6291464 | tf_op jit(solution)/shard_map/ppermute | solution.py:923
  238.0 8.5 %copy-start.78 = (f32[1024]{0:T(1024)S(1)}, f32[1024]{0:T(1024)}, u32[]{:S(2)}) copy-start(f32[1024]{0:T(1024)} %get-tuple-element.228) | copy-start | bytes 12292
  238.1 59.6 %copy-start.7 = (bf16[512,1024]{1,0:T(8,128)(2,1)S(1)}, bf16[512,1024]{1,0:T(8,128)(2,1)}, u32[]{:S(2)}) copy-start(bf16[512,1024]{1,0:T(8,128)(2,1)} %param.27) | copy-start | bytes 3145732
  238.1 59.6 %copy-start.77 = (f32[512]{0:T(512)S(1)}, f32[512]{0:T(512)}, u32[]{:S(2)}) copy-start(f32[512]{0:T(512)} %copy-done.76) | copy-start | bytes 6148
  241.8 60.7 %collective-permute-start.13 = (f32[512,1024]{1,0:T(8,128)}, f32[512,1024]{1,0:T(8,128)}, u32[]{:S(2)}, u32[]{:S(2)}) collective-permute-start(f32[512,1024]{1,0:T(8,128)} %fusion.21), channel_id=1, source_target_pairs={{0,2},{2,0},{1,3},{3,1},{4,6},{6,4},{5,7},{7,5},{8,10},{10,8},{9,1... | collective-permute-start | bytes 6291464 | tf_op jit(solution)/shard_map/ppermute | solution.py:923
  243.0 48.2 %collective-permute-start.16 = (f32[16,3072]{1,0:T(8,128)S(1)}, f32[16,3072]{1,0:T(8,128)S(1)}, u32[]{:S(2)}, u32[]{:S(2)}) collective-permute-start(f32[16,3072]{1,0:T(8,128)S(1)} %constant_dynamic-slice_fusion), channel_id=1, source_target_pairs={{0,16},{16,0},{1,17},{17,1},{2,18},{18,2},{3,19},{19,3},{4,20},{20... | collective-permute-start | bytes 589832 | tf_op jit(solution)/shard_map/ppermute | solution.py:923
  301.6 5.2 collective-permute-start.15
  409.5 2.8 collective-permute-start.17
  413.1 95.0 %copy-start.47 = (bf16[1024,1024]{1,0:T(8,128)(2,1)S(1)}, bf16[1024,1024]{1,0:T(8,128)(2,1)}, u32[]{:S(2)}) copy-start(bf16[1024,1024]{1,0:T(8,128)(2,1)} %param.48) | copy-start | bytes 6291460
  413.1 95.0 %copy-start.50 = (bf16[256,1024]{1,0:T(8,128)(2,1)S(1)}, bf16[256,1024]{1,0:T(8,128)(2,1)}, u32[]{:S(2)}) copy-start(bf16[256,1024]{1,0:T(8,128)(2,1)} %copy-done.48) | copy-start | bytes 1572868
  413.1 95.0 %copy-start.53 = (bf16[256,1024]{1,0:T(8,128)(2,1)S(1)}, bf16[256,1024]{1,0:T(8,128)(2,1)}, u32[]{:S(2)}) copy-start(bf16[256,1024]{1,0:T(8,128)(2,1)} %copy-done.51) | copy-start | bytes 1572868
  504.3 61.3 %collective-permute-start.18 = (f32[512,3328]{1,0:T(8,128)S(1)}, f32[512,3328]{1,0:T(8,128)S(1)}, u32[]{:S(2)}, u32[]{:S(2)}) collective-permute-start(f32[512,3328]{1,0:T(8,128)S(1)} %bitcast.80), channel_id=1, source_target_pairs={{0,2},{2,0},{1,3},{3,1},{4,6},{6,4},{5,7},{7,5},{8,10},{10,8},{9,1... | collective-permute-start | bytes 20447240 | tf_op jit(solution)/shard_map/ppermute | solution.py:923
  509.4 50.5 %collective-permute-start.11 = (f32[512,1024]{1,0:T(8,128)S(1)}, f32[512,1024]{1,0:T(8,128)S(1)}, u32[]{:S(2)}, u32[]{:S(2)}) collective-permute-start(f32[512,1024]{1,0:T(8,128)S(1)} %fusion.9), channel_id=1, source_target_pairs={{0,1},{1,0},{2,3},{3,2},{4,5},{5,4},{6,7},{7,6},{8,9},{9,8},{10,11... | collective-permute-start | bytes 6291464 | tf_op jit(solution)/shard_map/ppermute | solution.py:923
  509.9 51.6 %copy-start.32 = (f32[256,1024]{1,0:T(8,128)S(1)}, f32[256,1024]{1,0:T(8,128)}, u32[]{:S(2)}) copy-start(f32[256,1024]{1,0:T(8,128)} %get-tuple-element.241) | copy-start | bytes 3145732
  510.0 51.5 %copy-start.33 = (f32[256,1024]{1,0:T(8,128)S(1)}, f32[256,1024]{1,0:T(8,128)}, u32[]{:S(2)}) copy-start(f32[256,1024]{1,0:T(8,128)} %get-tuple-element.239) | copy-start | bytes 3145732
  590.0 10.3 %copy-start.1 = (bf16[1024,1024]{1,0:T(8,128)(2,1)S(1)}, bf16[1024,1024]{1,0:T(8,128)(2,1)}, u32[]{:S(2)}) copy-start(bf16[1024,1024]{1,0:T(8,128)(2,1)} %param.47) | copy-start | bytes 6291460
  (79 other events, 278.8 us)
Sparse Core Ops, SparseCore 0:
  131.1 81.6 reduce-scatter.1
  293.0 243.4 all-gather.1

commit v4 on v3

--- a/solution.py
+++ b/solution.py
@@ -1019,23 +1019,27 @@
     late = tuple(range(blocks // 2, blocks))
     early = tuple(range(blocks // 2))
     half = {}
-    ready = None
     for chunks in (late, early):
-        span = slice(chunks[0] * LEN, (chunks[-1] + 1) * LEN)
-        h = {"span": span}
-        lag_now = lag_row if ready is None else after(lag_row, ready)
+        h = {"span": slice(chunks[0] * LEN, (chunks[-1] + 1) * LEN)}
         h["y"], h["gated"], h["square"] = scan_forward(
-            chunks, heads, wide_in, x, xb, state, cum, lag_now, seg_col, seg_row, skip_row
+            chunks, heads, wide_in, x, xb, state, cum, lag_row, seg_col, seg_row, skip_row
         )
-        h["attended"], h["lse"] = attention_forward(chunks, after(queries, h["square"]), pairs, seg_col, seg_row)
-        h["square_far"] = swap(h["square"], "tensor")
-        squares = after(h["square"] + h["square_far"], h["lse"])
-        h["inv_gated"] = lax.rsqrt(squares.reshape(-1, 1) / DSSM + norm_eps)
+        half[chunks] = h
+    squares = jnp.concatenate([half[early]["square"], half[late]["square"]], axis=1)
+    squares_far = swap(squares, "tensor")
+    ready = squares
+    for chunks in (late, early):
+        h = half[chunks]
+        h["attended"], h["lse"] = attention_forward(chunks, after(queries, ready), pairs, seg_col, seg_row)
+        if chunks == late:
+            squares_far = after(squares_far, h["lse"])
+            squares_all = squares + squares_far
+        h["square"], h["square_far"] = squares[:, h["span"]], squares_far[:, h["span"]]
+        h["inv_gated"] = lax.rsqrt(squares_all[:, h["span"]].reshape(-1, 1) / DSSM + norm_eps)
         h["mixer_rows"] = (h["gated"] * h["inv_gated"] * gated_gain).astype(jnp.bfloat16)
         h["part"] = dot32(h["mixer_rows"], mixer_out) + dot32(h["attended"], attn_out)
         h["branch_far"] = swap(h["part"], "tensor")
         ready = h["part"]
-        half[chunks] = h
 
     ready = None
     for chunks in (late, early):
@@ -1070,25 +1074,8 @@
     def whole(name):
         return jnp.concatenate([half[early][name], half[late][name]], axis=0)
 
-    normed_ffn = whole("normed_ffn")
-    sides = [
-        (normed_ffn, whole("grad_gate_rows")),
-        (normed_ffn, whole("grad_up_rows")),
-        (whole("activated"), cotangent),
-    ]
-    sent = [swap(rows_dot(left, right, 1 - place), "core") for left, right in sides]
-    kept = [rows_dot(left, right, place) for left, right in sides]
-    first = jnp.concatenate([a + b for a, b in zip(kept, sent)], axis=1)
-    first_sum = lax.psum_scatter(first, ("y", "x"), scatter_dimension=0, tiled=True)
-    depth = first_sum.shape[0] // 2
-    zh = lax.axis_index("zh")
-    first_own = lax.dynamic_slice_in_dim(first_sum, zh * depth, depth, 0) + swap(
-        lax.dynamic_slice_in_dim(first_sum, (1 - zh) * depth, depth, 0), "zh"
-    )
-    first_all = lax.all_gather(first_own, ("core", "y", "x", "zh"), axis=0, tiled=True)
-
     grad_ffn_gain = 0.0
-    ready = first
+    ready = half[early]["part_ffn"]
     for chunks in (late, early):
         h = half[chunks]
         span = h["span"]
@@ -1107,6 +1094,23 @@
         operands = (queries, pairs, grad_attended, h["lse"], seg_col, seg_row, cosine, sine)
         if chunks == late:
             h["grad_queries"], grad_keys, grad_values = attention_backward(chunks, False, *operands)
+            normed_ffn = after(whole("normed_ffn"), grad_keys)
+            sides = [
+                (normed_ffn, whole("grad_gate_rows")),
+                (normed_ffn, whole("grad_up_rows")),
+                (after(whole("activated"), grad_keys), cotangent),
+            ]
+            sent = [swap(rows_dot(left, right, 1 - place), "core") for left, right in sides]
+            kept = [rows_dot(left, right, place) for left, right in sides]
+            first = jnp.concatenate([a + b for a, b in zip(kept, sent)], axis=1)
+            first_sum = lax.psum_scatter(first, ("y", "x"), scatter_dimension=0, tiled=True)
+            depth = first_sum.shape[0] // 2
+            zh = lax.axis_index("zh")
+            first_own = lax.dynamic_slice_in_dim(first_sum, zh * depth, depth, 0) + swap(
+                lax.dynamic_slice_in_dim(first_sum, (1 - zh) * depth, depth, 0), "zh"
+            )
+            first_all = lax.all_gather(first_own, ("core", "y", "x", "zh"), axis=0, tiled=True)
+            dot_far = after(dot_far, first)
         else:
             h["grad_queries"], grad_pairs = attention_backward(chunks, True, *operands, grad_keys, grad_values)
         h["grad_gate"], h["gy"], h["dx"], h["p"], h["grad_in"], h["grad_out"], h["sums"] = scan_backward(
@@ -1132,8 +1136,6 @@
             select,
         )
         ready = h["p"]
-    down = dot32(whole("activated"), ffn_down)
-    down_far = swap(after(down, dot_far), "tensor")
     ends = []
     for name in ("gy", "dx", "p", "grad_in", "grad_out"):
         ends += [half[early][name], half[late][name]]
@@ -1167,7 +1169,7 @@
     wide_grad = jnp.concatenate([grad_gate, grad_conv], axis=1)
     small_grad = jnp.concatenate([grad_state, grad_queries, grad_pairs, grad_step], axis=1)
     partial_normed = dot32(wide_grad, wide_proj.T) + dot32(small_grad, small_proj.T)
-    normed_far = swap(partial_normed, "tensor")
+    normed_far = swap(after(partial_normed, first_own), "tensor")
     sums = half[early]["sums"] + half[late]["sums"]
     over_tensor = [jnp.sum(partial_normed * unit_in, axis=0), state_sum[:4], state_sum[4]]
     alone = [
@@ -1203,20 +1205,32 @@
     inner = kept_inner + far_inner
     inner_end = at_step - model_width
     second = jnp.concatenate([kept_outer + far_outer, inner[:, :inner_end], inner[:, inner_end:] + table], axis=1)
-    devices = 32
-    own_rows = second.shape[0] // devices
+    peers = 16
+    peer_rows = second.shape[0] // peers
     columns = second.shape[1]
     second = after(second, first_own)
-    second = lax.all_to_all(second.reshape(devices, own_rows, columns), ("y", "zh", "x"), 0, 0, tiled=True)
+    second = lax.all_to_all(second.reshape(peers, peer_rows, columns), ("y", "x"), 0, 0, tiled=True)
+    second = after(second, normed_far)
     second = jnp.sum(second, axis=0)
+    depth = peer_rows // 2
+    second = lax.dynamic_slice_in_dim(second, zh * depth, depth, 0) + swap(
+        lax.dynamic_slice_in_dim(second, (1 - zh) * depth, depth, 0), "zh"
+    )
     at_state = at_step - 2 * state_size
     both = second[:, at_state:]
     summed = exchange(both, "tensor")
     lane = np.arange(both.shape[1]) - 2 * state_size
     is_shared = (lane < 0) | ((lane >= heads) & (lane < shared_end))
     second = jnp.concatenate([second[:, :at_state], jnp.where(is_shared[None, :], summed, both)], axis=1)
-    second = jnp.broadcast_to(second[None], (devices, own_rows, columns))
-    second = lax.all_to_all(second, ("y", "zh", "x"), 0, 0, tiled=True).reshape(devices * own_rows, columns)
+    other = swap(second, "zh")
+    second = jnp.where(
+        zh == 0, jnp.concatenate([second, other], axis=0), jnp.concatenate([other, second], axis=0)
+    )
+    down = dot32(whole("activated"), ffn_down)
+    down_far = swap(after(down, second), "tensor")
+    second = jnp.broadcast_to(after(second, first_all)[None], (peers, peer_rows, columns))
+    second = lax.all_to_all(second, ("y", "x"), 0, 0, tiled=True)
+    second = after(second, down_far).reshape(peers * peer_rows, columns)
     second_far = swap(second, "core")
     grad_mixer_out, grad_attn_out, grad_mixer_proj, grad_query_proj, grad_keyval, grad_state_proj, step_block = assemble(
         second, second_far, width, query_width

time: 617 us -> 679 us (1.10)
  waiting for transfers between devices: 156 us -> 288 us
  blocking collectives: 183 us -> 83.7 us
  starting transfers between devices: 22.6 us -> 38.2 us
  other arithmetic: 36.2 us -> 45.6 us
    all_to_all x2 -> x1, blocking collectives: 183 us -> 83.7 us  [on_device(): lax.all_to_all(second.reshape(peers, peer_rows, columns), ('y', 'x'), 0,...]
    reduce_scatter x1, waiting for transfers between devices: 0.01 us -> 82.1 us  [on_device(): lax.psum_scatter(first, ('y', 'x'), scatter_dimension=0, tiled=True)]
    all_to_all x0 -> x1, waiting for transfers between devices: none -> 43.6 us  [on_device(): second = lax.all_to_all(second, ('y', 'x'), 0, 0, tiled=True)]
    ppermute x19 -> x20, starting transfers between devices: 22.5 us -> 33.5 us  [swap(): return lax.ppermute(values, name, PAIR)]
    ppermute x19 -> x20, waiting for transfers between devices: 156 us -> 162 us  [swap(): return lax.ppermute(values, name, PAIR)]
    unnamed x226 -> x225, local copies, waits for them, and re-layouts: 26.5 us -> 23.3 us
  transfers between devices with their start and end apart: 21 -> 23, of which waited for: 7 -> 13; matrix products, arithmetic and copies ran while one was open for 17% -> 16% of each run, Pallas kernels for 10% -> 6%
where the time goes in v4:
time: 679 us; the launch traced here: 670 us
  waiting for transfers between devices  288 us (42%)
  blocking collectives  83.7 us (12%)
  Pallas kernels  71.3 us (11%)
  matrix products  68.2 us (10%)
  local copies, waits for them, and re-layouts  58.9 us (9%)
  other arithmetic  45.6 us (7%)
  starting transfers between devices  38.2 us (6%)
  between operations  15.8 us (2%)
    ppermute x20, waiting for transfers between devices, swap(): return lax.ppermute(values, name, PAIR)  162 us
    all_to_all x1, blocking collectives, on_device(): lax.all_to_all(second.reshape(peers, peer_rows, columns), ('y', 'x'), 0,...  83.7 us
    reduce_scatter x1, waiting for transfers between devices, on_device(): lax.psum_scatter(first, ('y', 'x'), scatter_dimension=0, tiled=True)  82.1 us
    pallas_call x10, Pallas kernels, call(): pl.pallas_call(kernel, grid=(steps,), out_shape=out_shape, in_specs=[s or...  58.5 us
    all_to_all x1, waiting for transfers between devices, on_device(): second = lax.all_to_all(second, ('y', 'x'), 0, 0, tiled=True)  43.6 us
    dot_general x23, matrix products, dot32(): return jnp.dot(left, right, preferred_element_type=jnp.float32)  36.8 us
    ppermute x20, starting transfers between devices, swap(): return lax.ppermute(values, name, PAIR)  33.5 us
    dot_general x10, matrix products, rows_dot(): lax.dot_general(core_rows(left, index), right, (((0,), (0,)), ((), ())),...  31.4 us
  transfers between devices with their start and end apart: 23, of which 13 were waited for; matrix products, arithmetic and copies ran while one was open for 16% of the time, Pallas kernels for 6%

profile of v4, /device:TPU:1, one launch (start us, length us, event | category | flops | bytes accessed | tf_op | source)
XLA Modules:
  0.0 669.8 jit_solution(7650973091335611667)
XLA Ops:
  9.0 4.2 copy.88
  18.8 5.8 fusion.73.conv_ref.gate_ref
  26.7 6.5 shard_map.426
  33.2 4.4 shard_map.427
  37.6 5.2 shard_map.428
  46.0 4.7 shard_map.429
  57.1 3.5 fusion.31
  60.6 4.1 shard_map.430
  67.6 12.0 %collective-permute-done.2 = f32[256,1024]{1,0:T(8,128)} collective-permute-done((f32[256,1024]{1,0:T(8,128)}, f32[256,1024]{1,0:T(8,128)}, u32[]{:S(2)}, u32[]{:S(2)}) %collective-permute-start.2) | collective-permute-done | bytes 1048608 | tf_op jit(solution)/shard_map/ppermute | solution.py:923
  86.2 15.8 %collective-permute-done.1 = f32[256,1024]{1,0:T(8,128)S(1)} collective-permute-done((f32[256,1024]{1,0:T(8,128)S(1)}, f32[256,1024]{1,0:T(8,128)S(1)}, u32[]{:S(2)}, u32[]{:S(2)}) %collective-permute-start.1) | collective-permute-done | bytes 1048608 | tf_op jit(solution)/shard_map/ppermute | solution.py:923
  110.2 17.0 %collective-permute-done.4 = f32[256,1024]{1,0:T(8,128)S(1)} collective-permute-done((f32[256,1024]{1,0:T(8,128)S(1)}, f32[256,1024]{1,0:T(8,128)S(1)}, u32[]{:S(2)}, u32[]{:S(2)}) %collective-permute-start.4) | collective-permute-done | bytes 1048608 | tf_op jit(solution)/shard_map/ppermute | solution.py:923
  133.2 4.7 shard_map.431
  137.9 3.2 fusion.19
  141.1 2.8 collective-permute-start.7
  149.4 2.9 convolution_add_fusion.3
  157.3 3.2 pad_maximum_fusion.1
  160.6 82.1 %reduce-scatter.2.cloned.1.call-done = f32[32,3072]{1,0:T(8,128)} async-done(((f32[512,3072]{1,0:T(8,128)}), f32[32,3072]{1,0:T(8,128)}) %reduce-scatter.2.cloned.1.call-update) | async-done | bytes 393232 | tf_op jit(solution)/shard_map/reduce_scatter | solution.py:1106
  243.7 3.0 collective-permute-start.13
  246.7 3.1 collective-permute-done.13
  254.3 20.5 %collective-permute-done.5.dot_b_ref = f32[1,256]{1,0:T(1,128)S(1)} collective-permute-done((f32[1,256]{1,0:T(1,128)S(1)}, f32[1,256]{1,0:T(1,128)S(1)}, u32[]{:S(2)}, u32[]{:S(2)}) %collective-permute-start.5) | collective-permute-done | bytes 1056 | tf_op jit(solution)/shard_map/ppermute | solution.py:923
  275.3 8.3 %shard_map.432 = (bf16[256,768]{1,0:T(8,128)(2,1)}, f32[256,768]{1,0:T(8,128)}, f32[512,768]{1,0:T(8,128)}, f32[16,256]{1,0:T(8,128)}, f32[512,128]{1,0:T(8,128)}, /*index=5*/f32[256,128]{1,0:T(8,128)}, f32[8,768]{1,0:T(8,128)}) custom-call(f32[256,768]{1,0:T(8,128)} %get-tuple-element.281.gmr_ref, f32[256,768]{1,0:T(8,128)} %get-tuple-element.109.gated_ref, ...), custom_call_target="tpu_custom_call" | custom-call | flops 4000000000 | bytes 11909120 | tf_op jit(solution)/shard_map/pallas_call | solution.py:656
  286.1 2.7 fusion.67
  292.7 4.4 shard_map.433
  297.7 6.7 shard_map.434
  308.9 9.5 %shard_map.435 = (bf16[512,768]{1,0:T(8,128)(2,1)}, bf16[512,256]{1,0:T(8,128)(2,1)}, bf16[512,128]{1,0:T(8,128)(2,1)}, f32[8,768]{1,0:T(8,128)}, f32[8,256]{1,0:T(8,128)}, /*index=5*/f32[32,128]{1,0:T(8,128)}) custom-call(f32[256,768]{1,0:T(8,128)} %get-tuple-element.136.gy_a_ref, f32[256,768]{1,0:T(8,128)} %get-tuple-element.137.gy_b_ref, ...), custom_call_target="tpu_custom_call" | custom-call | flops 2000000000 | bytes 13582080 | tf_op jit(solution)/shard_map/pallas_call | solution.py:656
  323.0 5.4 fusion.21
  328.4 3.0 collective-permute-start.11
  340.2 5.1 collective-permute-done.9
  345.3 4.2 convolution_add_fusion.1
  349.5 36.5 %collective-permute-done.14 = f32[512,1024]{1,0:T(8,128)} collective-permute-done((f32[512,1024]{1,0:T(8,128)}, f32[512,1024]{1,0:T(8,128)}, u32[]{:S(2)}, u32[]{:S(2)}) %collective-permute-start.14) | collective-permute-done | bytes 2097184 | tf_op jit(solution)/shard_map/ppermute | solution.py:923
  386.0 2.9 multiply_reduce_fusion
  391.7 4.6 convolution_add_fusion
  403.1 3.5 pad_maximum_fusion
  406.5 83.7 %all_to_all.10 = f32[16,32,3328]{2,1,0:T(8,128)} all-to-all(f32[16,32,3328]{2,1,0:T(8,128)S(1)} %bitcast.80), channel_id=1, replica_groups=mesh['y'=4,'zh'=2,'x'=4,'core'=2,'tensor'=2] {'y','x'}, dimensions={0} | all-to-all | bytes 13631488 | tf_op jit(solution)/shard_map/all_to_all | solution.py:1212
  490.2 4.0 reduce_sum.128
  495.2 2.5 collective-permute-start.15
  497.8 4.4 collective-permute-done.15
  509.0 4.1 collective-permute-done.17
  514.9 4.5 broadcast_in_dim.63
  519.5 4.7 all-to-all-start.1
  524.1 3.2 fusion.66
  529.3 41.9 %collective-permute-done.18 = f32[512,1024]{1,0:T(8,128)} collective-permute-done((f32[512,1024]{1,0:T(8,128)S(1)}, f32[512,1024]{1,0:T(8,128)}, u32[]{:S(2)}, u32[]{:S(2)}) %collective-permute-start.18) | collective-permute-done | bytes 2097184 | tf_op jit(solution)/shard_map/ppermute | solution.py:923
  571.2 43.6 %all-to-all-done.1 = f32[16,32,3328]{2,1,0:T(8,128)} async-done(((f32[16,32,3328]{2,1,0:T(8,128)}), f32[16,32,3328]{2,1,0:T(8,128)}, u32[]{:S(2)}, u32[]{:S(2)}) %all-to-all-start.1) | async-done | bytes 6815776 | tf_op jit(solution)/shard_map/all_to_all | solution.py:1232
  614.8 6.0 collective-permute-start.19
  620.9 4.9 maximum_add_fusion.1
  625.8 3.2 fusion.1
  629.0 10.1 %fusion.69 = (f32[1024,1024]{1,0:T(8,128)}, f32[1024,1024]{1,0:T(8,128)}, f32[1024,1024]{1,0:T(8,128)}) fusion(f32[1024,3072]{1,0:T(8,128)} %all-gather.2.cloned.1.call-done), kind=kLoop, calls=%fused_computation.169 | loop fusion | bytes 25165824 | tf_op jit(solution)/shard_map/slice | solution.py:1268
  639.1 12.8 %shard_map.436 = (f32[768,1024]{1,0:T(8,128)}, f32[256,1024]{1,0:T(8,128)}, f32[1024,2,768]{2,1,0:T(2,128)}, f32[1024,256]{1,0:T(8,128)}, f32[1024,1,128]{2,1,0:...) custom-call(s32[1]{0:T(128)} %bitcast.18.core_ref, f32[512,3328]{1,0:T(8,128)} %bitcast.19.own_ref, ...), custom_call_target="tpu_custom_call" | custom-call | bytes 27262976 | tf_op jit(solution)/shard_map/pallas_call | solution.py:883
  (361 shorter events, 114.9 us)
Async XLA Ops:
  7.2 75.1 %copy-start = (bf16[1024,1024]{1,0:T(8,128)(2,1)S(1)}, bf16[1024,1024]{1,0:T(8,128)(2,1)}, u32[]{:S(2)}) copy-start(bf16[1024,1024]{1,0:T(8,128)(2,1)} %param.47) | copy-start | bytes 6291460
  7.2 235.5 %reduce-scatter.2.cloned.1.call-start = ((), (), s32[]{:S(2)}) async-start(), calls=%async_computation.3 | async-start | bytes 6684672 | tf_op jit(solution)/shard_map/reduce_scatter | solution.py:1106
  9.0 7.3 %copy-start.104 = (f32[12]{0:T(128)S(1)}, f32[12]{0:T(128)}, u32[]{:S(2)}) copy-start(f32[12]{0:T(128)} %param.34) | copy-start | bytes 148
  9.0 8.7 %copy-start.94 = (f32[12]{0:T(128)S(1)}, f32[12]{0:T(128)}, u32[]{:S(2)}) copy-start(f32[12]{0:T(128)} %param.35) | copy-start | bytes 148
  9.0 9.4 %copy-start.72 = (f32[1024]{0:T(1024)S(1)}, f32[1024]{0:T(1024)}, u32[]{:S(2)}) copy-start(f32[1024]{0:T(1024)} %param.29) | copy-start | bytes 12292
  42.8 8.5 %copy-start.71 = (f32[768]{0:T(1024)S(1)}, f32[768]{0:T(1024)}, u32[]{:S(2)}) copy-start(f32[768]{0:T(1024)} %param.40) | copy-start | bytes 9220
  43.5 7.1 %collective-permute-start = (f32[1,512]{1,0:T(1,128)S(1)}, f32[1,512]{1,0:T(1,128)S(1)}, u32[]{:S(2)}, u32[]{:S(2)}) collective-permute-start(f32[1,512]{1,0:T(1,128)S(1)} %constant_dynamic-update-slice_fusion), channel_id=1, source_target_pairs={{0,1},{1,0},{2,3},{3,2},{4,5},{5,4},{6,7},{7,6},{8,9},{9,8},{10,11... | collective-permute-start | bytes 6152 | tf_op jit(solution)/shard_map/ppermute | solution.py:923
  55.4 24.2 %collective-permute-start.2 = (f32[256,1024]{1,0:T(8,128)}, f32[256,1024]{1,0:T(8,128)}, u32[]{:S(2)}, u32[]{:S(2)}) collective-permute-start(f32[256,1024]{1,0:T(8,128)} %convolution_add_fusion.7), channel_id=1, source_target_pairs={{0,1},{1,0},{2,3},{3,2},{4,5},{5,4},{6,7},{7,6},{8,9},{9,8},{10,11... | collective-permute-start | bytes 3145736 | tf_op jit(solution)/shard_map/ppermute | solution.py:923
  65.3 14.3 %copy-start.24 = (f32[512,1024]{1,0:T(8,128)S(1)}, f32[512,1024]{1,0:T(8,128)}, u32[]{:S(2)}) copy-start(f32[512,1024]{1,0:T(8,128)} %convert_element_type.85) | copy-start | bytes 6291460
  66.1 15.3 %copy-start.63 = (f32[1024]{0:T(1024)S(1)}, f32[1024]{0:T(1024)}, u32[]{:S(2)}) copy-start(f32[1024]{0:T(1024)} %param.45) | copy-start | bytes 12292
  66.1 15.5 %copy-start.2 = (bf16[1024,1024]{1,0:T(8,128)(2,1)S(1)}, bf16[1024,1024]{1,0:T(8,128)(2,1)}, u32[]{:S(2)}) copy-start(bf16[1024,1024]{1,0:T(8,128)(2,1)} %param.46) | copy-start | bytes 6291460
  66.1 35.9 %collective-permute-start.1 = (f32[256,1024]{1,0:T(8,128)S(1)}, f32[256,1024]{1,0:T(8,128)S(1)}, u32[]{:S(2)}, u32[]{:S(2)}) collective-permute-start(f32[256,1024]{1,0:T(8,128)S(1)} %convolution_add_fusion.6), channel_id=1, source_target_pairs={{0,1},{1,0},{2,3},{3,2},{4,5},{5,4},{6,7},{7,6},{8,9},{9,8},{10,11... | collective-permute-start | bytes 3145736 | tf_op jit(solution)/shard_map/ppermute | solution.py:923
  84.6 62.6 %copy-start.28 = (bf16[256,1024]{1,0:T(8,128)(2,1)}, bf16[256,1024]{1,0:T(8,128)(2,1)S(1)}, u32[]{:S(2)}) copy-start(bf16[256,1024]{1,0:T(8,128)(2,1)S(1)} %get-tuple-element.263) | copy-start | bytes 1572868
  103.9 23.3 %collective-permute-start.4 = (f32[256,1024]{1,0:T(8,128)S(1)}, f32[256,1024]{1,0:T(8,128)S(1)}, u32[]{:S(2)}, u32[]{:S(2)}) collective-permute-start(f32[256,1024]{1,0:T(8,128)S(1)} %convolution_add_fusion.9), channel_id=1, source_target_pairs={{0,1},{1,0},{2,3},{3,2},{4,5},{5,4},{6,7},{7,6},{8,9},{9,8},{10,11... | collective-permute-start | bytes 3145736 | tf_op jit(solution)/shard_map/ppermute | solution.py:923
  141.1 8.2 %collective-permute-start.7 = (f32[512,1024]{1,0:T(8,128)}, f32[512,1024]{1,0:T(8,128)}, u32[]{:S(2)}, u32[]{:S(2)}) collective-permute-start(f32[512,1024]{1,0:T(8,128)} %fusion.19), channel_id=1, source_target_pairs={{0,2},{2,0},{1,3},{3,1},{4,6},{6,4},{5,7},{7,5},{8,10},{10,8},{9,1... | collective-permute-start | bytes 6291464 | tf_op jit(solution)/shard_map/ppermute | solution.py:923
  146.1 6.2 collective-permute-start.8
  149.3 5.6 collective-permute-start.6
  160.5 90.9 %copy-start.22 = (f32[256,1024]{1,0:T(8,128)S(1)}, f32[256,1024]{1,0:T(8,128)}, u32[]{:S(2)}) copy-start(f32[256,1024]{1,0:T(8,128)} %convolution_add_fusion.8) | copy-start | bytes 3145732
  160.5 92.9 %copy-start.91 = (f32[256]{0:T(256)S(1)}, f32[256]{0:T(256)}, u32[]{:S(2)}) copy-start(f32[256]{0:T(256)} %get-tuple-element.280) | copy-start | bytes 3076
  160.5 93.2 %copy-start.87 = (f32[1,512]{1,0:T(1,128)S(1)}, f32[1,512]{1,0:T(1,128)}, u32[]{:S(2)}) copy-start(f32[1,512]{1,0:T(1,128)} %copy-done.86) | copy-start | bytes 6148
  160.5 354.4 %all-gather.2.cloned.1.call-start = ((), (), s32[]{:S(2)}) async-start(), calls=%async_computation.4 | async-start | bytes 12779520 | tf_op jit(solution)/shard_map/all_gather | solution.py:1112
  243.7 6.1 collective-permute-start.13
  251.4 32.3 %collective-permute-start.3 = (f32[256,1024]{1,0:T(8,128)S(1)}, f32[256,1024]{1,0:T(8,128)}, u32[]{:S(2)}, u32[]{:S(2)}) collective-permute-start(f32[256,1024]{1,0:T(8,128)S(1)} %copy-done.22), channel_id=1, source_target_pairs={{0,1},{1,0},{2,3},{3,2},{4,5},{5,4},{6,7},{7,6},{8,9},{9,8},{10,11... | collective-permute-start | bytes 3145736 | tf_op jit(solution)/shard_map/ppermute | solution.py:923
  253.4 21.4 %collective-permute-start.5 = (f32[1,256]{1,0:T(1,128)S(1)}, f32[1,256]{1,0:T(1,128)S(1)}, u32[]{:S(2)}, u32[]{:S(2)}) collective-permute-start(f32[1,256]{1,0:T(1,128)S(1)} %bitcast.99), channel_id=1, source_target_pairs={{0,1},{1,0},{2,3},{3,2},{4,5},{5,4},{6,7},{7,6},{8,9},{9,8},{10,11... | collective-permute-start | bytes 3080 | tf_op jit(solution)/shard_map/ppermute | solution.py:923
  275.3 8.4 %copy-start.4 = (f32[256,1024]{1,0:T(8,128)S(1)}, f32[256,1024]{1,0:T(8,128)}, u32[]{:S(2)}) copy-start(f32[256,1024]{1,0:T(8,128)} %copy-done.3) | copy-start | bytes 3145732
  275.3 8.4 %copy-start.80 = (f32[256]{0:T(256)S(1)}, f32[256]{0:T(256)}, u32[]{:S(2)}) copy-start(f32[256]{0:T(256)} %copy-done.79) | copy-start | bytes 3076
  288.9 42.7 %copy-start.14 = (bf16[256,1024]{1,0:T(8,128)(2,1)}, bf16[256,1024]{1,0:T(8,128)(2,1)S(1)}, u32[]{:S(2)}) copy-start(bf16[256,1024]{1,0:T(8,128)(2,1)S(1)} %get-tuple-element.127) | copy-start | bytes 1572868
  290.4 6.7 collective-permute-start.10
  297.7 8.5 %copy-start.58 = (bf16[256,768]{1,0:T(8,128)(2,1)S(1)}, bf16[256,768]{1,0:T(8,128)(2,1)}, u32[]{:S(2)}) copy-start(bf16[256,768]{1,0:T(8,128)(2,1)} %get-tuple-element.134) | copy-start | bytes 1179652
  297.7 9.3 %copy-start.65 = (bf16[256,256]{1,0:T(8,128)(2,1)S(1)}, bf16[256,256]{1,0:T(8,128)(2,1)}, u32[]{:S(2)}) copy-start(bf16[256,256]{1,0:T(8,128)(2,1)} %get-tuple-element.130) | copy-start | bytes 393220
  297.7 9.9 %copy-start.64 = (bf16[256,256]{1,0:T(8,128)(2,1)S(1)}, bf16[256,256]{1,0:T(8,128)(2,1)}, u32[]{:S(2)}) copy-start(bf16[256,256]{1,0:T(8,128)(2,1)} %get-tuple-element.120) | copy-start | bytes 393220
  323.0 8.4 %copy-start.43 = (bf16[256,768]{1,0:T(8,128)(2,1)S(1)}, bf16[256,768]{1,0:T(8,128)(2,1)}, u32[]{:S(2)}) copy-start(bf16[256,768]{1,0:T(8,128)(2,1)} %copy-done.42) | copy-start | bytes 1179652
  323.0 8.4 %copy-start.55 = (bf16[256,256]{1,0:T(8,128)(2,1)S(1)}, bf16[256,256]{1,0:T(8,128)(2,1)}, u32[]{:S(2)}) copy-start(bf16[256,256]{1,0:T(8,128)(2,1)} %get-tuple-element.110) | copy-start | bytes 393220
  323.0 8.4 %copy-start.57 = (bf16[256,256]{1,0:T(8,128)(2,1)S(1)}, bf16[256,256]{1,0:T(8,128)(2,1)}, u32[]{:S(2)}) copy-start(bf16[256,256]{1,0:T(8,128)(2,1)} %get-tuple-element.112) | copy-start | bytes 393220
  328.4 63.3 %collective-permute-start.11 = (f32[512,2304]{1,0:T(8,128)}, f32[512,2304]{1,0:T(8,128)}, u32[]{:S(2)}, u32[]{:S(2)}) collective-permute-start(f32[512,2304]{1,0:T(8,128)} %fusion.21), channel_id=1, source_target_pairs={{0,2},{2,0},{1,3},{3,1},{4,6},{6,4},{5,7},{7,5},{8,10},{10,8},{9,1... | collective-permute-start | bytes 14155784 | tf_op jit(solution)/shard_map/ppermute | solution.py:923
  333.7 11.5 %collective-permute-start.9 = (f32[512,1024]{1,0:T(8,128)}, f32[512,1024]{1,0:T(8,128)}, u32[]{:S(2)}, u32[]{:S(2)}) collective-permute-start(f32[512,1024]{1,0:T(8,128)} %fusion.18), channel_id=1, source_target_pairs={{0,2},{2,0},{1,3},{3,1},{4,6},{6,4},{5,7},{7,5},{8,10},{10,8},{9,1... | collective-permute-start | bytes 6291464 | tf_op jit(solution)/shard_map/ppermute | solution.py:923
  339.2 46.8 %collective-permute-start.14 = (f32[512,1024]{1,0:T(8,128)}, f32[512,1024]{1,0:T(8,128)}, u32[]{:S(2)}, u32[]{:S(2)}) collective-permute-start(f32[512,1024]{1,0:T(8,128)} %convolution_add_fusion.5), channel_id=1, source_target_pairs={{0,1},{1,0},{2,3},{3,2},{4,5},{5,4},{6,7},{7,6},{8,9},{9,8},{10,11... | collective-permute-start | bytes 6291464 | tf_op jit(solution)/shard_map/ppermute | solution.py:923
  340.2 45.8 %copy-start.6 = (bf16[512,1024]{1,0:T(8,128)(2,1)S(1)}, bf16[512,1024]{1,0:T(8,128)(2,1)}, u32[]{:S(2)}) copy-start(bf16[512,1024]{1,0:T(8,128)(2,1)} %param.27) | copy-start | bytes 3145732
  389.9 11.1 %collective-permute-start.12 = (f32[9,512]{0,1:T(8,128)}, f32[9,512]{0,1:T(8,128)}, u32[]{:S(2)}, u32[]{:S(2)}) collective-permute-start(f32[9,512]{0,1:T(8,128)} %copy.87), channel_id=1, source_target_pairs={{0,2},{2,0},{1,3},{3,1},{4,6},{6,4},{5,7},{7,5},{8,10},{10,8},{9,1... | collective-permute-start | bytes 55304 | tf_op jit(solution)/shard_map/ppermute | solution.py:923
  490.2 15.7 %copy-start.93 = (pred[384]{0:T(512)(128)(4,1)S(1)}, pred[384]{0:T(512)(128)(4,1)}, u32[]{:S(2)}) copy-start(pred[384]{0:T(512)(128)(4,1)} %constant.86) | copy-start | bytes 1156
  495.2 6.9 %collective-permute-start.15 = (f32[16,3328]{1,0:T(8,128)S(1)}, f32[16,3328]{1,0:T(8,128)S(1)}, u32[]{:S(2)}, u32[]{:S(2)}) collective-permute-start(f32[16,3328]{1,0:T(8,128)S(1)} %constant_dynamic-slice_fusion), channel_id=1, source_target_pairs={{0,16},{16,0},{1,17},{17,1},{2,18},{18,2},{3,19},{19,3},{4,20},{20... | collective-permute-start | bytes 638984 | tf_op jit(solution)/shard_map/ppermute | solution.py:923
  503.1 2.8 collective-permute-start.16
  506.6 6.5 collective-permute-start.17
  519.5 95.4 %all-to-all-start.1 = ((f32[16,32,3328]{2,1,0:T(8,128)}), f32[16,32,3328]{2,1,0:T(8,128)}, u32[]{:S(2)}, u32[]{:S(2)}) async-start(f32[16,32,3328]{2,1,0:T(8,128)} %broadcast_in_dim.63), calls=%async_computation.2 | async-start | bytes 13631488 | tf_op jit(solution)/shard_map/all_to_all | solution.py:1232
  528.6 42.6 %collective-permute-start.18 = (f32[512,1024]{1,0:T(8,128)S(1)}, f32[512,1024]{1,0:T(8,128)}, u32[]{:S(2)}, u32[]{:S(2)}) collective-permute-start(f32[512,1024]{1,0:T(8,128)S(1)} %fusion.66), channel_id=1, source_target_pairs={{0,1},{1,0},{2,3},{3,2},{4,5},{5,4},{6,7},{7,6},{8,9},{9,8},{10,11... | collective-permute-start | bytes 6291464 | tf_op jit(solution)/shard_map/ppermute | solution.py:923
  614.8 24.3 %collective-permute-start.19 = (f32[512,3328]{1,0:T(8,128)}, f32[512,3328]{1,0:T(8,128)}, u32[]{:S(2)}, u32[]{:S(2)}) collective-permute-start(f32[512,3328]{1,0:T(8,128)} %bitcast.19.own_ref), channel_id=1, source_target_pairs={{0,2},{2,0},{1,3},{3,1},{4,6},{6,4},{5,7},{7,5},{8,10},{10,8},{9,1... | collective-permute-start | bytes 20447240 | tf_op jit(solution)/shard_map/ppermute | solution.py:923
  651.9 8.0 %copy-start.36 = (f32[1024,128]{1,0:T(8,128)S(1)}, f32[1024,128]{1,0:T(8,128)}, u32[]{:S(2)}) copy-start(f32[1024,128]{1,0:T(8,128)} %get-tuple-element.163) | copy-start | bytes 1572868
  651.9 10.6 %copy-start.1 = (bf16[1024,1024]{1,0:T(8,128)(2,1)S(1)}, bf16[1024,1024]{1,0:T(8,128)(2,1)}, u32[]{:S(2)}) copy-start(bf16[1024,1024]{1,0:T(8,128)(2,1)} %param.47) | copy-start | bytes 6291460
  (80 other events, 250.6 us)
Sparse Core Ops, SparseCore 0:
  160.7 82.0 reduce-scatter.1
  251.6 96.9 all-gather.1

commit v5 on v4

--- a/solution.py
+++ b/solution.py
@@ -652,7 +652,6 @@
 
 
 def call(kernel, steps, out_shape, out_specs, scratch, operands, specs, flops):
-    moved = sum(o.size * o.dtype.itemsize for o in operands) + sum(o.size * o.dtype.itemsize for o in out_shape)
     return pl.pallas_call(
         kernel,
         grid=(steps,),
@@ -661,7 +660,7 @@
         out_specs=[s or whole_block(o.shape) for o, s in zip(out_shape, out_specs)],
         scratch_shapes=scratch,
         compiler_params=pltpu.CompilerParams(vmem_limit_bytes=VMEM_BYTES),
-        cost_estimate=pl.CostEstimate(flops=flops, bytes_accessed=moved, transcendentals=0),
+        cost_estimate=pl.CostEstimate(flops=flops, bytes_accessed=0, transcendentals=0),
     )(*operands)
 
 
@@ -699,7 +698,7 @@
     scratch = [pltpu.VMEM((rows + 8, LEN), jnp.float32), pltpu.VMEM((3, rows + 8, LEN), jnp.float32)]
     operands = (wide_in, small, cosine, sine, keep, conv_kernel, conv_bias, *rest)
     specs = [tile(rows, 0, steps), None, None, None, None, tile(4), tile(1)] + [None] * len(rest)
-    return call(prep_kernel, steps, outs, [tile(rows)] * 3 + [None] * 10, scratch, operands, specs, 10**9)
+    return call(prep_kernel, steps, outs, [tile(rows)] * 3 + [None] * 10, scratch, operands, specs, 0 * 10**9)
 
 
 def scan_forward(chunks, heads, wide_in, x, xb, *rest):
@@ -718,14 +717,14 @@
     specs = [tile(rows, at), tile(rows, at), tile((chunks[-1] + 1) * LEN)] + [None] * (len(rest) - 1) + [tile(1)]
     kernel = functools.partial(scan_kernel, chunks, heads)
     operands = (wide_in, x, xb, *rest)
-    return call(kernel, heads // 2 // GROUP, outs, [tile(rows), tile(rows), None], scratch, operands, specs, 2 * 10**9)
+    return call(kernel, heads // 2 // GROUP, outs, [tile(rows), tile(rows), None], scratch, operands, specs, 0 * 10**9)
 
 
 def attention_forward(chunks, q, kv, seg_col, seg_row):
     rows = LEN * len(chunks)
     outs = [b16(rows, q.shape[1]), f32(8, rows)]
     kernel = functools.partial(attention_kernel, chunks)
-    return call(kernel, 1, outs, [None] * 2, [], (q, kv, seg_col, seg_row), [None] * 4, 10**9)
+    return call(kernel, 1, outs, [None] * 2, [], (q, kv, seg_col, seg_row), [None] * 4, 0 * 10**9)
 
 
 def attention_backward(chunks, final, *operands):
@@ -739,7 +738,7 @@
         pltpu.VMEM((HEAD_DIM, rows), jnp.bfloat16),
     ]
     kernel = functools.partial(attention_back_kernel, chunks, final)
-    return call(kernel, 1, outs, [None] * len(outs), scratch, operands, [None] * len(operands), 2 * 10**9)
+    return call(kernel, 1, outs, [None] * len(outs), scratch, operands, [None] * len(operands), 0 * 10**9)
 
 
 def scan_backward(chunks, heads, *operands):
@@ -771,7 +770,7 @@
     specs += [None, None, None, tile(1), None, None, tile(HEAD_ROWS)]
     out_specs = [tile(rows), tile(rows), tile(sources), None, None, None, tile(8)]
     kernel = functools.partial(scan_back_kernel, chunks, heads)
-    return call(kernel, heads // 2 // GROUP, outs, out_specs, scratch, operands, specs, 4 * 10**9)
+    return call(kernel, heads // 2 // GROUP, outs, out_specs, scratch, operands, specs, 30 * 10**9)
 
 
 def scan_end(heads, *operands):
@@ -797,77 +796,420 @@
     specs += [tile(rows, 0, steps)] + [None] * 4 + [tile(1), None, None, None, tile(HEAD_ROWS), tile(4), None]
     out_specs = [tile(rows), None, None, tile(8), None, None]
     kernel = functools.partial(scan_end_kernel, heads)
-    return call(kernel, steps, outs, out_specs, scratch, operands, specs, 2 * 10**9)
+    return call(kernel, steps, outs, out_specs, scratch, operands, specs, 30 * 10**9)
+
+
+def inverse_rms(rows):
+    return lax.rsqrt(jnp.mean(rows * rows, axis=-1, keepdims=True) + norm_eps)
+
+
+def ffn_kernel(
+    tokens_ref,
+    part_ref,
+    far_ref,
+    gain_ref,
+    gate_ref,
+    up_ref,
+    down_ref,
+    cotangent_ref,
+    hidden_ref,
+    normed_ref,
+    activated_ref,
+    grad_gate_ref,
+    grad_up_ref,
+    back_ref,
+    out_ref,
+):
+    @pl.when(pl.program_id(0) == 0)
+    def _():
+        hidden = tokens_ref[...].astype(jnp.float32) + (part_ref[...] + far_ref[...])
+        hidden_ref[...] = hidden
+        normed_ref[...] = (hidden * inverse_rms(hidden) * gain_ref[...]).astype(jnp.bfloat16)
+        back_ref[...] = jnp.zeros(back_ref.shape, jnp.float32)
+        out_ref[...] = jnp.zeros(out_ref.shape, jnp.float32)
+
+    normed = normed_ref[...]
+    gate = dot_nn(normed, gate_ref[...])
+    up = dot_nn(normed, up_ref[...])
+    sig = sigmoid(gate)
+    act = gate * sig
+    activated = (act * up).astype(jnp.bfloat16)
+    activated_ref[...] = activated
+    grad = dot_nt(cotangent_ref[...], down_ref[...])
+    grad_gate = (grad * up * (sig * (1.0 + gate * (1.0 - sig)))).astype(jnp.bfloat16)
+    grad_up = (grad * act).astype(jnp.bfloat16)
+    grad_gate_ref[...] = grad_gate
+    grad_up_ref[...] = grad_up
+    back_ref[...] = back_ref[...] + (dot_nt(grad_gate, gate_ref[...]) + dot_nt(grad_up, up_ref[...]))
+    out_ref[...] = out_ref[...] + dot_nn(activated, down_ref[...])
+
+
+def ffn(chunks, tokens, part, far, gain, gate, up, down, cotangent):
+    rows, model_width = part.shape
+    at = chunks[0] // len(chunks)
+    hidden_width = gate.shape[1]
+    steps = hidden_width // 256
+    outs = [f32(rows, model_width), b16(rows, model_width)] + [b16(rows, hidden_width)] * 3
+    outs += [f32(rows, model_width)] * 2
+    rows_of = pl.BlockSpec((rows, model_width), lambda step: (at, 0), pipeline_mode=pl.Buffered(1))
+    columns = pl.BlockSpec((model_width, 256), lambda step: (0, step))
+    tiles = pl.BlockSpec((rows, 256), lambda step: (0, step))
+    specs = [rows_of, None, None, None, columns, columns]
+    specs += [pl.BlockSpec((256, model_width), lambda step: (step, 0)), rows_of]
+    operands = (tokens, part, far, gain, gate, up, down, cotangent)
+    return call(ffn_kernel, steps, outs, [None, None, tiles, tiles, tiles, None, None], [], operands, specs, 0 * 10**9)
+
+
+def middle_kernel(
+    hidden_ref,
+    part_ref,
+    far_ref,
+    cotangent_ref,
+    gain_ref,
+    gated_ref,
+    square_a_ref,
+    square_b_ref,
+    gated_gain_ref,
+    mixer_out_ref,
+    attn_out_ref,
+    grad_hidden_ref,
+    grad_branch_ref,
+    grad_rows_ref,
+    grad_attended_ref,
+    dot_ref,
+    gain_sum_ref,
+):
+    hidden = hidden_ref[...]
+    inv = inverse_rms(hidden)
+    unit = hidden * inv
+    grad_normed = part_ref[...] + far_ref[...]
+    gain_sum_ref[0:1, :] = jnp.sum(grad_normed * unit, axis=0, keepdims=True)
+    grad_unit = grad_normed * gain_ref[...]
+    inner = jnp.mean(grad_unit * unit, axis=-1, keepdims=True)
+    grad_hidden = cotangent_ref[...].astype(jnp.float32) + inv * (grad_unit - unit * inner)
+    grad_hidden_ref[...] = grad_hidden
+    grad_branch = grad_hidden.astype(jnp.bfloat16)
+    grad_branch_ref[...] = grad_branch
+    grad_rows = dot_nt(grad_branch, mixer_out_ref[...])
+    grad_rows_ref[...] = grad_rows
+    grad_attended_ref[...] = dot_nt(grad_branch, attn_out_ref[...]).astype(jnp.bfloat16)
+    total = jnp.sum(grad_rows * gated_gain_ref[...] * gated_ref[...], axis=-1, keepdims=True)
+    for i in range(hidden.shape[0] // LEN):
+        at = block(i)
+        inv_gated = lax.rsqrt((square_a_ref[:, at] + square_b_ref[:, at]) / DSSM + norm_eps)
+        dot_ref[0:1, at] = jnp.broadcast_to(total[at], (LEN, LEN)).T[0:1] * inv_gated
+
+
+def middle(chunks, hidden, part, far, cotangent, gain, gated, square_a, square_b, gated_gain, mixer_out, attn_out):
+    rows, model_width = part.shape
+    at = chunks[0] // len(chunks)
+    width, inner = mixer_out.shape[0], attn_out.shape[0]
+    outs = [
+        f32(rows, model_width),
+        b16(rows, model_width),
+        f32(rows, width),
+        b16(rows, inner),
+        f32(1, rows),
+        f32(8, model_width),
+    ]
+    rows_of = pl.BlockSpec((rows, model_width), lambda step: (at, 0), pipeline_mode=pl.Buffered(1))
+    specs = [None, None, None, rows_of] + [None] * 7
+    operands = (hidden, part, far, cotangent, gain, gated, square_a, square_b, gated_gain, mixer_out, attn_out)
+    return call(middle_kernel, 1, outs, [None] * 6, [], operands, specs, 0 * 10**9)
+
+
+def core_call(kernel, steps, core, out_shape, out_spec, scratch, operands, specs, flops):
+    return pl.pallas_call(
+        kernel,
+        grid_spec=pltpu.PrefetchScalarGridSpec(
+            num_scalar_prefetch=1, grid=(steps,), in_specs=specs, out_specs=out_spec, scratch_shapes=scratch
+        ),
+        out_shape=out_shape,
+        compiler_params=pltpu.CompilerParams(vmem_limit_bytes=VMEM_BYTES),
+        cost_estimate=pl.CostEstimate(flops=flops, bytes_accessed=0, transcendentals=0),
+    )(core, *operands)
+
+
+def clip_tile(rows, columns, first, last):
+    return pl.BlockSpec((rows, columns), lambda step, core_ref: (0, jnp.clip(step - first, 0, last - first - 1)))
+
+
+def ffn_weights_kernel(add, core_ref, *refs):
+    refs = list(refs)
+    normed_a, normed_b, act_a, act_b, gate_a, gate_b, up_a, up_b, cot_a, cot_b = refs[:10]
+    far_ref = refs[10] if add else None
+    out_ref, left_ref = refs[-2:]
+    step = pl.program_id(0)
+    third = pl.num_programs(0) // 3
+    half = normed_a.shape[0]
+
+    def turn(first, second):
+        left_ref[:, :half] = first[...].T
+        left_ref[:, half:] = second[...].T
+
+    @pl.when(step == 0)
+    def _():
+        turn(normed_a, normed_b)
+
+    @pl.when(step == 2 * third)
+    def _():
+        turn(act_a, act_b)
+
+    def product(first, second):
+        result = dot_nn(left_ref[:, :half], first[...]) + dot_nn(left_ref[:, half:], second[...])
+        out_ref[...] = result + far_ref[...] if add else result
+
+    @pl.when(step < third)
+    def _():
+        product(gate_a, gate_b)
+
+    @pl.when((step >= third) & (step < 2 * third))
+    def _():
+        product(up_a, up_b)
+
+    @pl.when(step >= 2 * third)
+    def _():
+        product(cot_a, cot_b)
+
+
+def ffn_weights(core, far, normed_a, normed_b, act_a, act_b, gate_a, gate_b, up_a, up_b, cotangent):
+    half, columns = normed_a.shape
+    kept = columns // 2
+    tile_width = 512
+    third = columns // tile_width
+    left = pl.BlockSpec((half, kept), lambda step, core_ref: (0, core_ref[0]), pipeline_mode=pl.Buffered(1))
+    specs = [left] * 4 + [clip_tile(half, tile_width, 0, third)] * 2
+    specs += [clip_tile(half, tile_width, third, 2 * third)] * 2
+
+    def cot_rows(at):
+        return pl.BlockSpec(
+            (half, tile_width), lambda step, core_ref: (at, jnp.clip(step - 2 * third, 0, third - 1))
+        )
+
+    specs += [cot_rows(0), cot_rows(1)]
+    out = pl.BlockSpec((kept, tile_width), lambda step, core_ref: (0, step))
+    operands = [normed_a, normed_b, act_a, act_b, gate_a, gate_b, up_a, up_b, cotangent, cotangent]
+    if far is not None:
+        operands.append(far)
+        specs.append(out)
+    return core_call(
+        functools.partial(ffn_weights_kernel, far is not None),
+        3 * third,
+        core,
+        f32(kept, 3 * columns),
+        out,
+        [pltpu.VMEM((kept, 2 * half), jnp.bfloat16)],
+        operands,
+        specs,
+        0 * 10**9,
+    )
+
+
+def mixer_weights_kernel(add, core_ref, *refs):
+    refs = list(refs)
+    (
+        rows_a,
+        rows_b,
+        edge_a,
+        edge_b,
+        att_a,
+        att_b,
+        normed_ref,
+        branch_a,
+        branch_b,
+        gate_a,
+        gate_b,
+        conv_ref,
+        query_a,
+        query_b,
+        state_ref,
+        pair_ref,
+        step_ref,
+    ) = refs[:17]
+    far_ref = refs[17] if add else None
+    table_ref = refs[18] if add else None
+    out_ref, left_ref = refs[-2:]
+    step = pl.program_id(0)
+    half = rows_a.shape[0]
+    kept = left_ref.shape[0]
+    middle_row = kept // 2
+
+    @pl.when((step == 0) & (core_ref[0] == 0))
+    def _():
+        left_ref[:, :half] = rows_a[...].T
+        left_ref[:, half:] = rows_b[...].T
+
+    @pl.when((step == 0) & (core_ref[0] == 1))
+    def _():
+        left_ref[:middle_row, :half] = edge_a[...].T
+        left_ref[:middle_row, half:] = edge_b[...].T
+        left_ref[middle_row:, :half] = att_a[...].T
+        left_ref[middle_row:, half:] = att_b[...].T
+
+    @pl.when(step == 4)
+    def _():
+        left_ref[...] = normed_ref[...].T
+
+    def write(value, lanes=slice(None)):
+        out_ref[:, lanes] = value + far_ref[:, lanes] if add else value
+
+    def two(first, second):
+        write(dot_nn(left_ref[:, :half], first[...]) + dot_nn(left_ref[:, half:], second[...]))
+
+    @pl.when(step < 4)
+    def _():
+        two(branch_a, branch_b)
+
+    @pl.when((step >= 4) & (step < 7))
+    def _():
+        two(gate_a, gate_b)
+
+    @pl.when((step >= 7) & (step < 10))
+    def _():
+        write(dot_nn(left_ref[...], conv_ref[...]))
+
+    @pl.when(step == 10)
+    def _():
+        two(query_a, query_b)
+
+    @pl.when(step == 11)
+    def _():
+        write(dot_nn(left_ref[...], state_ref[...]))
+
+    @pl.when(step == 12)
+    def _():
+        write(dot_nn(left_ref[...], pair_ref[...]), slice(0, LEN))
+        steps = dot_nn(left_ref[...], step_ref[...])
+        write(steps + table_ref[...] if add else steps, slice(LEN, 2 * LEN))
+
+
+def mixer_weights(core, far, table, rows_a, rows_b, att_a, att_b, normed, branch_a, branch_b, gate_a, gate_b, conv, query_a, query_b, state, pair, step):
+    half, width = rows_a.shape
+    rows, model_width = normed.shape
+    kept = model_width // 2
+    tile_width = 256
+    steps = 13
+
+    def fixed(shape, column=0):
+        return pl.BlockSpec(shape, lambda step, core_ref: (0, column), pipeline_mode=pl.Buffered(1))
+
+    specs = [fixed((half, kept))] * 2
+    specs += [fixed((half, width - kept), kept // (width - kept))] * 2
+    specs += [fixed(att_a.shape)] * 2
+    specs += [pl.BlockSpec((rows, kept), lambda step, core_ref: (0, core_ref[0]), pipeline_mode=pl.Buffered(1))]
+    specs += [clip_tile(half, tile_width, 0, 4)] * 2
+    specs += [clip_tile(half, tile_width, 4, 7)] * 2
+    specs += [clip_tile(rows, tile_width, 7, 10)]
+    specs += [fixed(query_a.shape)] * 2 + [fixed(state.shape), fixed(pair.shape), fixed(step.shape)]
+    operands = [rows_a, rows_b, rows_a, rows_b, att_a, att_b, normed, branch_a, branch_b, gate_a, gate_b, conv]
+    operands += [query_a, query_b, state, pair, step]
+    out = pl.BlockSpec((kept, tile_width), lambda step, core_ref: (0, step))
+    if far is not None:
+        operands += [far, table]
+        specs += [out, fixed(table.shape)]
+    return core_call(
+        functools.partial(mixer_weights_kernel, far is not None),
+        steps,
+        core,
+        f32(kept, steps * tile_width),
+        out,
+        [pltpu.VMEM((kept, rows), jnp.bfloat16)],
+        operands,
+        specs,
+        0 * 10**9,
+    )
+
+
+def normed_back_kernel(
+    gate_a,
+    gate_b,
+    conv_ref,
+    query_a,
+    query_b,
+    state_ref,
+    pair_ref,
+    step_ref,
+    wide_ref,
+    small_ref,
+    tokens_ref,
+    inv_ref,
+    out_ref,
+    sum_ref,
+):
+    half, width = gate_a.shape
+    query_width = query_a.shape[1]
+    gate_w, conv_w = wide_ref[:, :width], wide_ref[:, width:]
+    state_w = small_ref[:, : 2 * LEN]
+    query_w = small_ref[:, 2 * LEN : 2 * LEN + query_width]
+    pair_w = small_ref[:, 2 * LEN + query_width : 3 * LEN + query_width]
+    step_w = small_ref[:, 3 * LEN + query_width :]
+    total = jnp.zeros((1, out_ref.shape[1]), jnp.float32)
+    for k, (gate, query) in enumerate(((gate_a, query_a), (gate_b, query_b))):
+        at = slice(k * half, (k + 1) * half)
+        grad = dot_nt(gate[...], gate_w) + dot_nt(conv_ref[at, :], conv_w) + dot_nt(query[...], query_w)
+        grad = grad + dot_nt(state_ref[at, :], state_w) + dot_nt(pair_ref[at, :], pair_w) + dot_nt(step_ref[at, :], step_w)
+        out_ref[at, :] = grad
+        unit = tokens_ref[at, :].astype(jnp.float32) * inv_ref[at, :]
+        total = total + jnp.sum(grad * unit, axis=0, keepdims=True)
+    sum_ref[0:1, :] = total
+
+
+def normed_back(gate_a, gate_b, conv, query_a, query_b, state, pair, step, wide_proj, small_proj, tokens, inv):
+    rows, model_width = tokens.shape
+    tile_width = 256
+    operands = (gate_a, gate_b, conv, query_a, query_b, state, pair, step, wide_proj, small_proj, tokens, inv)
+
+    def weights(count):
+        return pl.BlockSpec((tile_width, count), lambda step: (step, 0))
+
+    columns = pl.BlockSpec((rows, tile_width), lambda step: (0, step))
+    specs = [None] * 8 + [weights(wide_proj.shape[1]), weights(small_proj.shape[1]), columns, None]
+    out_specs = [columns, pl.BlockSpec((8, tile_width), lambda step: (0, step))]
+    outs = [f32(rows, model_width), f32(8, model_width)]
+    return call(normed_back_kernel, model_width // tile_width, outs, out_specs, [], operands, specs, 0 * 10**9)
 
 
 def assemble_kernel(
-    core_ref, own_ref, far_ref, mixer_out_ref, attn_out_ref, mixer_proj_ref, query_ref, pair_ref, state_ref, step_ref
+    source, mixer_out_ref, attn_out_ref, mixer_proj_ref, query_ref, pair_ref, state_ref, step_ref
 ):
-    at = pl.program_id(0)
-    count = pl.num_programs(0)
     width = mixer_proj_ref.shape[2]
     model_width = mixer_out_ref.shape[1]
-    split = mixer_out_count(width)
-
-    def write(source):
-        @pl.when(at < split)
-        def _():
-            mixer_out_ref[...] = source[:, :model_width]
-
-        @pl.when(at >= split)
-        def _():
-            attn_out_ref[...] = source[:, :model_width]
-
-        start = model_width
-        mixer_proj_ref[:, 0, :] = source[:, start : start + width]
-        start += width
-        query_ref[...] = source[:, start : start + query_ref.shape[1]]
-        start += query_ref.shape[1]
-        pair_ref[:, 0, :] = source[:, start : start + LEN]
-        start += LEN
-        mixer_proj_ref[:, 1, :] = source[:, start : start + width]
-        start += width
-        state_ref[...] = source[:, start : start + 2 * LEN]
-        step_ref[...] = source[:, start + 2 * LEN :]
-
-    mine = at // (count // 2) == core_ref[0]
-
-    @pl.when(mine)
-    def _():
-        write(own_ref)
-
-    @pl.when(jnp.logical_not(mine))
-    def _():
-        write(far_ref)
-
-
-def mixer_out_count(width):
-    return width // LEN
-
-
-def assemble(own, far, width, query_width):
-    half, columns = own.shape
-    rows = 2 * half
-    blocks = rows // LEN
-    split = mixer_out_count(width)
-    core = lax.axis_index("core").astype(jnp.int32).reshape(1)
-
-    def source(flip):
-        def index(at, core_ref):
-            first = (blocks // 2) * jnp.where(flip, 1 - core_ref[0], core_ref[0])
-            return (jnp.clip(at - first, 0, blocks // 2 - 1), 0)
-
-        return pl.BlockSpec((LEN, columns), index)
+    split = width // LEN
+
+    @pl.when(pl.program_id(0) < split)
+    def _():
+        mixer_out_ref[...] = source[:, :model_width]
+
+    @pl.when(pl.program_id(0) >= split)
+    def _():
+        attn_out_ref[...] = source[:, :model_width]
+
+    start = model_width
+    mixer_proj_ref[:, 0, :] = source[:, start : start + width]
+    start += width
+    mixer_proj_ref[:, 1, :] = source[:, start : start + width]
+    start += width
+    query_ref[...] = source[:, start : start + query_ref.shape[1]]
+    start += query_ref.shape[1]
+    state_ref[...] = source[:, start : start + 2 * LEN]
+    start += 2 * LEN
+    pair_ref[:, 0, :] = source[:, start : start + LEN]
+    step_ref[...] = source[:, start + LEN :]
+
+
+def assemble(values, width, query_width):
+    rows, columns = values.shape
+    split = width // LEN
 
     def plain(count):
-        return pl.BlockSpec((LEN, count), lambda at, core_ref: (at, 0))
+        return pl.BlockSpec((LEN, count), lambda at: (at, 0))
 
     out_specs = [
-        pl.BlockSpec((LEN, rows), lambda at, core_ref: (jnp.minimum(at, split - 1), 0)),
-        pl.BlockSpec((LEN, rows), lambda at, core_ref: (jnp.maximum(at - split, 0), 0)),
-        pl.BlockSpec((LEN, 2, width), lambda at, core_ref: (at, 0, 0)),
+        pl.BlockSpec((LEN, rows), lambda at: (jnp.minimum(at, split - 1), 0)),
+        pl.BlockSpec((LEN, rows), lambda at: (jnp.maximum(at - split, 0), 0)),
+        pl.BlockSpec((LEN, 2, width), lambda at: (at, 0, 0)),
         plain(query_width),
-        pl.BlockSpec((LEN, 1, LEN), lambda at, core_ref: (at, 0, 0)),
+        pl.BlockSpec((LEN, 1, LEN), lambda at: (at, 0, 0)),
         plain(2 * LEN),
         plain(LEN),
     ]
@@ -880,20 +1222,7 @@
         f32(rows, 2 * LEN),
         f32(rows, LEN),
     ]
-    return pl.pallas_call(
-        assemble_kernel,
-        grid_spec=pltpu.PrefetchScalarGridSpec(
-            num_scalar_prefetch=1, grid=(blocks,), in_specs=[source(False), source(True)], out_specs=out_specs
-        ),
-        out_shape=out_shape,
-        compiler_params=pltpu.CompilerParams(vmem_limit_bytes=VMEM_BYTES),
-        cost_estimate=pl.CostEstimate(flops=0, bytes_accessed=16 * own.size, transcendentals=0),
-    )(core, own, far)
-
-
-def silu_slope(argument):
-    logistic = jax.nn.sigmoid(argument)
-    return logistic * (1.0 + argument * (1.0 - logistic))
+    return call(assemble_kernel, rows // LEN, out_shape, out_specs, [], (values,), [plain(columns)], 0)
 
 
 def rope_tables(rows):
@@ -930,10 +1259,6 @@
 def core_rows(values, index):
     half = values.shape[1] // 2
     return lax.dynamic_slice_in_dim(values, index * half, half, 1)
-
-
-def rows_dot(left, right, index):
-    return lax.dot_general(core_rows(left, index), right, (((0,), (0,)), ((), ())), preferred_element_type=jnp.float32)
 
 
 def on_device(
@@ -969,6 +1294,9 @@
     query_width = query_proj.shape[1]
     pair_width = key_value_weight.shape[2]
     place = lax.axis_index("core")
+    zh = lax.axis_index("zh")
+    core = place.astype(jnp.int32).reshape(1)
+    far_core = 1 - core
     cosine, sine = rope_tables(rows)
     select = np.arange(HEAD_ROWS)[:, None] == np.arange(width)[None, :] // HEAD_DIM
     select = jnp.asarray(select.astype(np.float32)).astype(jnp.bfloat16)
@@ -1041,87 +1369,58 @@
         h["branch_far"] = swap(h["part"], "tensor")
         ready = h["part"]
 
-    ready = None
+    a, b = half[early], half[late]
+    gain_ffn = ffn_gain[None, :]
+    names = ("hidden", "normed", "activated", "grad_gate_rows", "grad_up_rows", "back", "down")
     for chunks in (late, early):
         h = half[chunks]
-        span = h["span"]
-        far = h["branch_far"] if ready is None else after(h["branch_far"], ready)
-        hidden = tokens[span] + (h["part"] + far)
-        inv_rms_ffn = lax.rsqrt(jnp.mean(hidden * hidden, axis=-1, keepdims=True) + norm_eps)
-        unit_ffn = hidden * inv_rms_ffn
-        normed_ffn = (unit_ffn * ffn_gain).astype(jnp.bfloat16)
-        gate_rows = dot32(normed_ffn, ffn_gate)
-        up_rows = dot32(normed_ffn, ffn_up)
-        gate_silu = jax.nn.silu(gate_rows)
-        activated = (gate_silu * up_rows).astype(jnp.bfloat16)
-        grad_activated = dot32(cotangent[span], ffn_down.T)
-        grad_gate_rows = (grad_activated * up_rows * silu_slope(gate_rows)).astype(jnp.bfloat16)
-        grad_up_rows = (grad_activated * gate_silu).astype(jnp.bfloat16)
-        partial_ffn = dot32(grad_gate_rows, ffn_gate.T) + dot32(grad_up_rows, ffn_up.T)
-        h["part_ffn"] = partial_ffn
-        h["ffn_far"] = swap(partial_ffn, "tensor")
-        ready = partial_ffn
-        h.update(
-            hidden=hidden,
-            unit_ffn=unit_ffn,
-            inv_rms_ffn=inv_rms_ffn,
-            normed_ffn=normed_ffn,
-            activated=activated,
-            grad_gate_rows=grad_gate_rows,
-            grad_up_rows=grad_up_rows,
-        )
-
-    def whole(name):
-        return jnp.concatenate([half[early][name], half[late][name]], axis=0)
-
-    grad_ffn_gain = 0.0
-    ready = half[early]["part_ffn"]
+        far = h["branch_far"] if chunks == late else after(h["branch_far"], b["back"])
+        operands = (layer_input, h["part"], far, gain_ffn, ffn_gate, ffn_up, ffn_down, cotangent)
+        h.update(zip(names, ffn(chunks, *operands)))
+        h["back_far"] = swap(h["back"], "tensor")
+
+    sides = (after(a["normed"], b["back_far"]), b["normed"], a["activated"], b["activated"])
+    sides += (a["grad_gate_rows"], b["grad_gate_rows"], a["grad_up_rows"], b["grad_up_rows"], cotangent)
+    first = swap(ffn_weights(far_core, None, *sides), "core")
+
     for chunks in (late, early):
         h = half[chunks]
-        span = h["span"]
-        grad_normed_ffn = h["part_ffn"] + after(h["ffn_far"], ready)
-        grad_ffn_gain = grad_ffn_gain + jnp.sum(grad_normed_ffn * h["unit_ffn"], axis=0)
-        h["grad_hidden"] = cotangent[span].astype(jnp.float32) + norm_backward(
-            grad_normed_ffn * ffn_gain, h["unit_ffn"], h["inv_rms_ffn"]
+        far = h["back_far"] if chunks == late else after(h["back_far"], first)
+        h["grad_hidden"], h["grad_branch"], h["grad_rows"], grad_attended, h["dot"], h["gain_sum"] = middle(
+            chunks,
+            h["hidden"],
+            h["back"],
+            far,
+            cotangent,
+            gain_ffn,
+            h["gated"],
+            h["square"],
+            h["square_far"],
+            gain_row,
+            mixer_out,
+            attn_out,
         )
-        grad_branch = h["grad_hidden"].astype(jnp.bfloat16)
-        h["grad_branch"] = grad_branch
-        grad_mixer_rows = dot32(grad_branch, mixer_out.T)
-        unit_gated = h["gated"] * h["inv_gated"]
-        gated_dot = jnp.sum(grad_mixer_rows * gated_gain * unit_gated, axis=-1)[None, :]
-        dot_far = swap(gated_dot, "tensor")
-        grad_attended = dot32(after(grad_branch, gated_dot), attn_out.T).astype(jnp.bfloat16)
         operands = (queries, pairs, grad_attended, h["lse"], seg_col, seg_row, cosine, sine)
         if chunks == late:
             h["grad_queries"], grad_keys, grad_values = attention_backward(chunks, False, *operands)
-            normed_ffn = after(whole("normed_ffn"), grad_keys)
-            sides = [
-                (normed_ffn, whole("grad_gate_rows")),
-                (normed_ffn, whole("grad_up_rows")),
-                (after(whole("activated"), grad_keys), cotangent),
-            ]
-            sent = [swap(rows_dot(left, right, 1 - place), "core") for left, right in sides]
-            kept = [rows_dot(left, right, place) for left, right in sides]
-            first = jnp.concatenate([a + b for a, b in zip(kept, sent)], axis=1)
+            first = ffn_weights(core, after(first, grad_keys), *sides)
             first_sum = lax.psum_scatter(first, ("y", "x"), scatter_dimension=0, tiled=True)
-            depth = first_sum.shape[0] // 2
-            zh = lax.axis_index("zh")
-            first_own = lax.dynamic_slice_in_dim(first_sum, zh * depth, depth, 0) + swap(
-                lax.dynamic_slice_in_dim(first_sum, (1 - zh) * depth, depth, 0), "zh"
-            )
-            first_all = lax.all_gather(first_own, ("core", "y", "x", "zh"), axis=0, tiled=True)
-            dot_far = after(dot_far, first)
         else:
+            dots = jnp.concatenate([a["dot"], b["dot"]], axis=1)
+            dots_far = swap(dots, "tensor")
             h["grad_queries"], grad_pairs = attention_backward(chunks, True, *operands, grad_keys, grad_values)
+    dots_far = after(dots_far, grad_pairs)
+    for chunks in (late, early):
+        h = half[chunks]
         h["grad_gate"], h["gy"], h["dx"], h["p"], h["grad_in"], h["grad_out"], h["sums"] = scan_backward(
             chunks,
             heads,
-            grad_mixer_rows,
+            h["grad_rows"],
             h["gated"],
             h["square"],
             h["square_far"],
-            gated_dot,
-            after(dot_far, h["grad_queries"]),
+            h["dot"],
+            dots_far[:, h["span"]],
             gain_row,
             wide_in,
             h["y"],
@@ -1135,10 +1434,10 @@
             seg_row,
             select,
         )
-        ready = h["p"]
+    down = jnp.concatenate([a["down"], b["down"]], axis=0)
     ends = []
     for name in ("gy", "dx", "p", "grad_in", "grad_out"):
-        ends += [half[early][name], half[late][name]]
+        ends += [a[name], b[name]]
     grad_conv, grad_state, grad_step, conv_sum, state_sum, step_sum = scan_end(
         heads,
         *ends,
@@ -1159,19 +1458,15 @@
         state_kernel,
     )
 
-    grad_queries, grad_gate = whole("grad_queries"), whole("grad_gate")
-    outer = jnp.concatenate([whole("mixer_rows"), whole("attended")], axis=1)
-    grad_branch = whole("grad_branch")
-    right = jnp.concatenate([grad_gate, grad_queries, grad_pairs, grad_conv, grad_state, grad_step], axis=1)
-    far_outer = swap(rows_dot(outer, grad_branch, 1 - place), "core")
-    far_inner = swap(rows_dot(normed_input, right, 1 - place), "core")
-
-    wide_grad = jnp.concatenate([grad_gate, grad_conv], axis=1)
-    small_grad = jnp.concatenate([grad_state, grad_queries, grad_pairs, grad_step], axis=1)
-    partial_normed = dot32(wide_grad, wide_proj.T) + dot32(small_grad, small_proj.T)
-    normed_far = swap(after(partial_normed, first_own), "tensor")
-    sums = half[early]["sums"] + half[late]["sums"]
-    over_tensor = [jnp.sum(partial_normed * unit_in, axis=0), state_sum[:4], state_sum[4]]
+    grads = (a["grad_gate"], b["grad_gate"], grad_conv, a["grad_queries"], b["grad_queries"])
+    grads += (grad_state, grad_pairs, grad_step)
+    sides = (a["mixer_rows"], b["mixer_rows"], a["attended"], b["attended"], normed_input)
+    sides += (a["grad_branch"], b["grad_branch"], *grads)
+    second_far = swap(mixer_weights(far_core, None, None, *sides), "core")
+    partial_normed, input_gain_sum = normed_back(*grads, wide_proj, small_proj, layer_input, inv_rms_in)
+
+    sums = a["sums"] + b["sums"]
+    over_tensor = [input_gain_sum[0], state_sum[:4], state_sum[4]]
     alone = [
         step_sum[:heads, 0],
         step_sum[HEAD_ROWS : HEAD_ROWS + heads, 0],
@@ -1179,7 +1474,7 @@
         conv_sum[:4],
         conv_sum[4],
         sums[1],
-        grad_ffn_gain,
+        a["gain_sum"][0] + b["gain_sum"][0],
     ]
 
     def packed(values):
@@ -1200,41 +1495,35 @@
     table_end = heads + table.shape[0]
     table = (core_rows(table, place) + swap(core_rows(table, 1 - place), "core")).T
     table = jnp.pad(table, ((0, 0), (heads, LEN - table_end)))
-    kept_outer, kept_inner = rows_dot(outer, grad_branch, place), rows_dot(normed_input, right, place)
-    at_step = model_width + 2 * width + query_width + pair_width + 2 * state_size
-    inner = kept_inner + far_inner
-    inner_end = at_step - model_width
-    second = jnp.concatenate([kept_outer + far_outer, inner[:, :inner_end], inner[:, inner_end:] + table], axis=1)
+    second = mixer_weights(core, second_far, table, *sides)
+    first_own = exchange(after(first_sum, second), "zh")
+    first_all = lax.all_gather(first_own, ("core", "y", "x"), axis=0, tiled=True)
+    down_far = swap(after(down, first_own), "tensor")
+    at_state = model_width + 2 * width + query_width
+    at_step = at_state + 2 * state_size + pair_width
     peers = 16
     peer_rows = second.shape[0] // peers
     columns = second.shape[1]
     second = after(second, first_own)
     second = lax.all_to_all(second.reshape(peers, peer_rows, columns), ("y", "x"), 0, 0, tiled=True)
-    second = after(second, normed_far)
-    second = jnp.sum(second, axis=0)
-    depth = peer_rows // 2
-    second = lax.dynamic_slice_in_dim(second, zh * depth, depth, 0) + swap(
-        lax.dynamic_slice_in_dim(second, (1 - zh) * depth, depth, 0), "zh"
-    )
-    at_state = at_step - 2 * state_size
+
+    second = jnp.sum(after(second, down_far), axis=0)
     both = second[:, at_state:]
     summed = exchange(both, "tensor")
-    lane = np.arange(both.shape[1]) - 2 * state_size
-    is_shared = (lane < 0) | ((lane >= heads) & (lane < shared_end))
+    lane = np.arange(both.shape[1])
+    in_table = lane - 2 * state_size - pair_width
+    is_shared = (lane < 2 * state_size) | ((in_table >= heads) & (in_table < shared_end))
     second = jnp.concatenate([second[:, :at_state], jnp.where(is_shared[None, :], summed, both)], axis=1)
-    other = swap(second, "zh")
-    second = jnp.where(
-        zh == 0, jnp.concatenate([second, other], axis=0), jnp.concatenate([other, second], axis=0)
+    second = exchange(second, "zh")
+    second = after(second, first_all)
+    normed_far = swap(after(partial_normed, second), "tensor")
+    second = lax.all_gather(second, ("core", "y", "x"), axis=0, tiled=True)
+    grad_mixer_out, grad_attn_out, grad_mixer_proj, grad_query_proj, grad_keyval, grad_state_proj, step_block = assemble(
+        second, width, query_width
     )
-    down = dot32(whole("activated"), ffn_down)
-    down_far = swap(after(down, second), "tensor")
-    second = jnp.broadcast_to(after(second, first_all)[None], (peers, peer_rows, columns))
-    second = lax.all_to_all(second, ("y", "x"), 0, 0, tiled=True)
-    second = after(second, down_far).reshape(peers * peer_rows, columns)
-    second_far = swap(second, "core")
-    grad_mixer_out, grad_attn_out, grad_mixer_proj, grad_query_proj, grad_keyval, grad_state_proj, step_block = assemble(
-        second, second_far, width, query_width
-    )
+
+    def whole(name):
+        return jnp.concatenate([a[name], b[name]], axis=0)
 
     grad_hidden = whole("grad_hidden")
     grad_normed = partial_normed + normed_far

time: 679 us -> 512 us (0.75)
  blocking collectives: 83.7 us -> 0 us
  Pallas kernels: 71.3 us -> 149 us
  matrix products: 68.2 us -> 10.6 us
  waiting for transfers between devices: 288 us -> 235 us
  other arithmetic: 45.6 us -> 19.7 us
  local copies, waits for them, and re-layouts: 58.9 us -> 40.7 us
    all_to_all x1 -> x0, blocking collectives: 83.7 us -> none  [on_device(): lax.all_to_all(second.reshape(peers, peer_rows, columns), ('y', 'x'), 0,...]
    reduce_scatter x1, waiting for transfers between devices: 82.1 us -> 4.8 us  [on_device(): lax.psum_scatter(first, ('y', 'x'), scatter_dimension=0, tiled=True)]
    pallas_call x10 -> x16, Pallas kernels: 58.5 us -> 106 us  [call(): pl.pallas_call(kernel, grid=(steps,), out_shape=out_shape, in_specs=[s or...]
    all_gather x1 -> x2, waiting for transfers between devices: 0.01 us -> 36.8 us  [the longest x1 33 us: on_device(): second = lax.all_gather(second, ('core', 'y', 'x'), axis=0, tiled=True)]
    dot_general x10 -> x0, matrix products: 31.4 us -> none  [rows_dot(): lax.dot_general(core_rows(left, index), right, (((0,), (0,)), ((), ())),...]
    pallas_call x1 -> x4, Pallas kernels: 12.8 us -> 42.8 us  [core_call(): pl.pallas_call(kernel, grid_spec=pltpu.PrefetchScalarGridSpec(num_scalar_...]
    ppermute x20 -> x14, waiting for transfers between devices: 162 us -> 133 us  [swap(): return lax.ppermute(values, name, PAIR)]
    dot_general x23 -> x6, matrix products: 36.8 us -> 10.6 us  [dot32(): return jnp.dot(left, right, preferred_element_type=jnp.float32)]
  transfers between devices with their start and end apart: 23 -> 18, of which waited for: 13 -> 14; matrix products, arithmetic and copies ran while one was open for 16% -> 6% of each run, Pallas kernels for 6% -> 22%
where the time goes in v5:
time: 512 us; the launch traced here: 502 us
  waiting for transfers between devices  235 us (46%)
  Pallas kernels  149 us (29%)
  local copies, waits for them, and re-layouts  40.7 us (8%)
  starting transfers between devices  31.8 us (6%)
  other arithmetic  19.7 us (4%)
  between operations  14.7 us (3%)
  matrix products  10.6 us (2%)
    ppermute x14, waiting for transfers between devices, swap(): return lax.ppermute(values, name, PAIR)  133 us
    pallas_call x16, Pallas kernels, call(): pl.pallas_call(kernel, grid=(steps,), out_shape=out_shape, in_specs=[s or...  106 us
    all_to_all x1, waiting for transfers between devices, on_device(): lax.all_to_all(second.reshape(peers, peer_rows, columns), ('y', 'x'), 0,...  60.3 us
    pallas_call x4, Pallas kernels, core_call(): pl.pallas_call(kernel, grid_spec=pltpu.PrefetchScalarGridSpec(num_scalar_...  42.8 us
    all_gather x1, waiting for transfers between devices, on_device(): second = lax.all_gather(second, ('core', 'y', 'x'), axis=0, tiled=True)  33 us
    ppermute x14, starting transfers between devices, swap(): return lax.ppermute(values, name, PAIR)  18 us
    unnamed x95, local copies, waits for them, and re-layouts  11.2 us
    dot_general x6, matrix products, dot32(): return jnp.dot(left, right, preferred_element_type=jnp.float32)  10.6 us
  transfers between devices with their start and end apart: 18, of which 14 were waited for; matrix products, arithmetic and copies ran while one was open for 6% of the time, Pallas kernels for 22%

profile of v5, /device:TPU:1, one launch (start us, length us, event | category | flops | bytes accessed | tf_op | source)
XLA Modules:
  0.0 501.7 jit_solution(17082562788081870819)
XLA Ops:
  7.2 1.5 fusion.9
  8.8 4.2 copy.90
  13.6 5.7 %fusion.26.conv_ref.gate_ref = f32[512,1536]{1,0:T(8,128)} fusion(bf16[512,1024]{1,0:T(8,128)(2,1)S(1)} %fusion.4.refs_6_, bf16[1024,1536]{1,0:T(8,128)(2,1)} %bitcast.51), kind=kOutput, calls=%fused_computation.71 | convolution fusion | flops 1610612736 | bytes 7340032 | tf_op jit(solution)/shard_map/dot_general | solution.py:1244
  19.6 2.1 fusion.27.small_ref
  26.1 6.5 %shard_map.426 = (f32[512,768]{1,0:T(8,128)}, bf16[512,768]{1,0:T(8,128)(2,1)}, f32[512,768]{1,0:T(8,128)}, f32[512,256]{1,0:T(8,128)}, f32[512,256]{1,0:T(8,128...) custom-call(f32[512,1536]{1,0:T(8,128)} %fusion.26.conv_ref.gate_ref, ...), custom_call_target="tpu_custom_call" | custom-call | tf_op jit(solution)/shard_map/pallas_call | solution.py:655
  32.6 4.4 shard_map.427
  37.0 5.3 %shard_map.428 = (f32[256,768]{1,0:T(8,128)}, f32[256,768]{1,0:T(8,128)}, f32[1,256]{1,0:T(1,128)}) custom-call(f32[512,1536]{1,0:T(8,128)} %fusion.26.conv_ref.gate_ref, f32[512,768]{1,0:T(8,128)} %get-tuple-element.119.x_ref, bf16[512,768]{1,0:T(8,128)(2,1)} %get-tuple-element.120.xb_ref, f32[512,256]{1,0:T(8,128)} %get-tuple-element.121.state_ref, ...), custom_call_target="tpu_custom_call" | custom-call | tf_op jit(solution)/shard_map/pallas_call | solution.py:655
  43.2 2.5 collective-permute-start
  45.6 4.7 shard_map.429
  54.6 4.0 shard_map.430
  59.7 1.5 collective-permute-start.1
  61.3 17.3 %collective-permute-done.2.far_ref = f32[256,1024]{1,0:T(8,128)} collective-permute-done((f32[256,1024]{1,0:T(8,128)}, f32[256,1024]{1,0:T(8,128)}, u32[]{:S(2)}, u32[]{:S(2)}) %collective-permute-start.2) | collective-permute-done | bytes 1048608 | tf_op jit(solution)/shard_map/ppermute | solution.py:1252
  78.6 9.7 %shard_map.431 = (f32[256,1024]{1,0:T(8,128)}, bf16[256,1024]{1,0:T(8,128)(2,1)}, bf16[256,1024]{1,0:T(8,128)(2,1)}, bf16[256,1024]{1,0:T(8,128)(2,1)}, bf16[256...) custom-call(bf16[512,1024]{1,0:T(8,128)(2,1)} %tokens_ref.5, ...), custom_call_target="tpu_custom_call" | custom-call | tf_op jit(solution)/shard_map/pallas_call | solution.py:655
  88.7 12.3 %collective-permute-done.1.far_ref = f32[256,1024]{1,0:T(8,128)S(1)} collective-permute-done((f32[256,1024]{1,0:T(8,128)S(1)}, f32[256,1024]{1,0:T(8,128)S(1)}, u32[]{:S(2)}, u32[]{:S(2)}) %collective-permute-start.1) | collective-permute-done | bytes 1048608 | tf_op jit(solution)/shard_map/ppermute | solution.py:1252
  101.9 9.7 %shard_map.432 = (f32[256,1024]{1,0:T(8,128)}, bf16[256,1024]{1,0:T(8,128)(2,1)}, bf16[256,1024]{1,0:T(8,128)(2,1)}, bf16[256,1024]{1,0:T(8,128)(2,1)}, bf16[256...) custom-call(bf16[512,1024]{1,0:T(8,128)(2,1)} %tokens_ref.5, f32[256,1024]{1,0:T(8,128)} %copy-done.11, ...), custom_call_target="tpu_custom_call" | custom-call | tf_op jit(solution)/shard_map/pallas_call | solution.py:655
  111.6 11.9 %collective-permute-done.3.far_ref = f32[256,1024]{1,0:T(8,128)} collective-permute-done((f32[256,1024]{1,0:T(8,128)}, f32[256,1024]{1,0:T(8,128)}, u32[]{:S(2)}, u32[]{:S(2)}) %collective-permute-start.3) | collective-permute-done | bytes 1048608 | tf_op jit(solution)/shard_map/ppermute | solution.py:1252
  123.5 7.8 %shard_map.433 = f32[512,3072]{1,0:T(8,128)} custom-call(s32[1]{0:T(128)S(6)} %sub.9.core_ref, bf16[256,1024]{1,0:T(8,128)(2,1)} %get-tuple-element.143.refs_0_, bf16[256,1024]{1,0:T(8,128)(2,1)} %get-tuple-element.144.refs_1_, bf16[256,1024]{1,0:T(8,128)(2,1)} %get-tuple-element.145.refs_2_, bf16[256,1024]{1,0:T(8,128)(2,1)} %get-tuple-element.146.refs_3_, ...), custom_call_target="tpu_custom_call" | custom-call | tf_op jit(solution)/shard_map/pallas_call | solution.py:922
  131.3 1.9 collective-permute-start.4
  134.3 5.1 %shard_map.434 = (f32[256,1024]{1,0:T(8,128)}, bf16[256,1024]{1,0:T(8,128)(2,1)}, f32[256,768]{1,0:T(8,128)}, bf16[256,256]{1,0:T(8,128)(2,1)}, f32[1,256]{1,0:T(1,128)}, /*index=5*/f32[8,1024]{1,0:T(8,128)}) custom-call(f32[256,1024]{1,0:T(8,128)} %get-tuple-element.139.hidden_ref, f32[256,1024]{1,0:T(8,128)} %get-tuple-element.136.part_ref, ...), custom_call_target="tpu_custom_call" | custom-call | tf_op jit(solution)/shard_map/pallas_call | solution.py:655
  139.4 4.6 shard_map.435
  144.0 9.2 %shard_map.436 = f32[512,3072]{1,0:T(8,128)} custom-call(s32[1]{0:T(128)} %bitcast.14.core_ref, bf16[256,1024]{1,0:T(8,128)(2,1)} %get-tuple-element.143.refs_0_, bf16[256,1024]{1,0:T(8,128)(2,1)} %get-tuple-element.144.refs_1_, bf16[256,1024]{1,0:T(8,128)(2,1)} %get-tuple-element.145.refs_2_, bf16[256,1024]{1,0:T(8,128)(2,1)} %get-tuple-element.146.refs_3_, ...), custom_call_target="tpu_custom_call" | custom-call | tf_op jit(solution)/shard_map/pallas_call | solution.py:922
  153.2 4.7 collective-permute-done.5.far_ref
  158.8 5.1 %shard_map.437 = (f32[256,1024]{1,0:T(8,128)}, bf16[256,1024]{1,0:T(8,128)(2,1)}, f32[256,768]{1,0:T(8,128)}, bf16[256,256]{1,0:T(8,128)(2,1)}, f32[1,256]{1,0:T(1,128)}, /*index=5*/f32[8,1024]{1,0:T(8,128)}) custom-call(f32[256,1024]{1,0:T(8,128)} %get-tuple-element.138.hidden_ref, f32[256,1024]{1,0:T(8,128)} %get-tuple-element.154.part_ref, ...), custom_call_target="tpu_custom_call" | custom-call | tf_op jit(solution)/shard_map/pallas_call | solution.py:655
  164.7 8.8 %all-gather.3.cloned.1.call-start = ((), (), s32[]{:S(2)}) async-start(), calls=%async_computation.3 | async-start | bytes 12976128 | tf_op jit(solution)/shard_map/all_gather | solution.py:1500
  173.6 4.4 shard_map.438
  178.5 6.6 %shard_map.439 = (bf16[256,768]{1,0:T(8,128)(2,1)}, f32[256,768]{1,0:T(8,128)}, f32[256,768]{1,0:T(8,128)}, f32[16,256]{1,0:T(8,128)}, f32[256,128]{1,0:T(8,128)}, /*index=5*/f32[256,128]{1,0:T(8,128)}, f32[8,768]{1,0:T(8,128)}) custom-call(f32[256,768]{1,0:T(8,128)} %get-tuple-element.158.gmr_ref, f32[256,768]{1,0:T(8,128)} %get-tuple-element.124.gated_ref, ...), custom_call_target="tpu_custom_call" | custom-call | flops 30000001024 | tf_op jit(solution)/shard_map/pallas_call | solution.py:655
  185.1 8.5 %shard_map.440 = (bf16[256,768]{1,0:T(8,128)(2,1)}, f32[256,768]{1,0:T(8,128)}, f32[512,768]{1,0:T(8,128)}, f32[16,256]{1,0:T(8,128)}, f32[512,128]{1,0:T(8,128)}, /*index=5*/f32[256,128]{1,0:T(8,128)}, f32[8,768]{1,0:T(8,128)}) custom-call(f32[256,768]{1,0:T(8,128)} %get-tuple-element.170.gmr_ref, f32[256,768]{1,0:T(8,128)} %get-tuple-element.132.gated_ref, ...), custom_call_target="tpu_custom_call" | custom-call | flops 30000001024 | tf_op jit(solution)/shard_map/pallas_call | solution.py:655
  193.6 8.7 %shard_map.441 = (bf16[512,768]{1,0:T(8,128)(2,1)}, bf16[512,256]{1,0:T(8,128)(2,1)}, bf16[512,128]{1,0:T(8,128)(2,1)}, f32[8,768]{1,0:T(8,128)}, f32[8,256]{1,0:T(8,128)}, /*index=5*/f32[32,128]{1,0:T(8,128)}) custom-call(f32[256,768]{1,0:T(8,128)} %get-tuple-element.173.gy_a_ref, f32[256,768]{1,0:T(8,128)} %get-tuple-element.174.gy_b_ref, ...), custom_call_target="tpu_custom_call" | custom-call | flops 30000001024 | tf_op jit(solution)/shard_map/pallas_call | solution.py:655
  202.3 11.9 %shard_map.442 = f32[512,3328]{1,0:T(8,128)} custom-call(s32[1]{0:T(128)S(6)} %sub.9.core_ref, bf16[256,768]{1,0:T(8,128)(2,1)} %copy-done.3, bf16[256,768]{1,0:T(8,128)(2,1)} %copy-done.4, bf16[256,768]{1,0:T(8,128)(2,1)} %copy-done.3, bf16[256,768]{1,0:T(8,128)(2,1)} %copy-done.4, bf16[256,256]{1,0:T(8,128)(2,1)} %get-tuple-element.135.refs_4_, ...), custom_call_target="tpu_custom_call" | custom-call | tf_op jit(solution)/shard_map/pallas_call | solution.py:922
  217.8 7.4 %shard_map.443 = (f32[512,1024]{1,0:T(8,128)}, f32[8,1024]{1,0:T(8,128)}) custom-call(bf16[256,768]{1,0:T(8,128)(2,1)} %get-tuple-element.169.refs_9_.gate_a, bf16[256,768]{1,0:T(8,128)(2,1)} %get-tuple-element.172.refs_10_.gate_b, bf16[512,768]{1,0:T(8,128)(2,1)} %get-tuple-element.187.refs_11_.conv_ref, ...), custom_call_target="tpu_custom_call" | custom-call | tf_op jit(solution)/shard_map/pallas_call | solution.py:655
  228.9 14.0 %shard_map.444 = f32[512,3328]{1,0:T(8,128)} custom-call(s32[1]{0:T(128)} %bitcast.14.core_ref, bf16[256,768]{1,0:T(8,128)(2,1)} %copy-done.3, bf16[256,768]{1,0:T(8,128)(2,1)} %copy-done.4, bf16[256,768]{1,0:T(8,128)(2,1)} %copy-done.3, bf16[256,768]{1,0:T(8,128)(2,1)} %copy-done.4, bf16[256,256]{1,0:T(8,128)(2,1)} %get-tuple-element.135.refs_4_, ...), custom_call_target="tpu_custom_call" | custom-call | tf_op jit(solution)/shard_map/pallas_call | solution.py:922
  242.9 4.8 reduce-scatter.2.cloned.1.call-done
  247.7 2.9 collective-permute-start.9
  250.6 7.7 %collective-permute-done.9 = f32[32,3072]{1,0:T(8,128)S(1)} collective-permute-done((f32[32,3072]{1,0:T(8,128)}, f32[32,3072]{1,0:T(8,128)S(1)}, u32[]{:S(2)}, u32[]{:S(2)}) %collective-permute-start.9) | collective-permute-done | bytes 393248 | tf_op jit(solution)/shard_map/ppermute | solution.py:1252
  258.2 1.8 add.115
  260.1 4.8 all-to-all-start
  268.9 43.0 %collective-permute-done.10 = f32[512,1024]{1,0:T(8,128)} collective-permute-done((f32[512,1024]{1,0:T(8,128)S(1)}, f32[512,1024]{1,0:T(8,128)}, u32[]{:S(2)}, u32[]{:S(2)}) %collective-permute-start.10) | collective-permute-done | bytes 2097184 | tf_op jit(solution)/shard_map/ppermute | solution.py:1252
  311.8 60.3 %all-to-all-done = f32[16,32,3328]{2,1,0:T(8,128)} async-done(((f32[16,32,3328]{2,1,0:T(8,128)}), f32[16,32,3328]{2,1,0:T(8,128)}, u32[]{:S(2)}, u32[]{:S(2)}) %all-to-all-start) | async-done | bytes 6815776 | tf_op jit(solution)/shard_map/all_to_all | solution.py:1508
  372.1 4.3 reduce_sum.38
  381.8 3.0 collective-permute-start.12
  384.9 5.6 %collective-permute-done.12 = f32[32,3328]{1,0:T(8,128)S(1)} collective-permute-done((f32[32,3328]{1,0:T(8,128)S(1)}, f32[32,3328]{1,0:T(8,128)S(1)}, u32[]{:S(2)}, u32[]{:S(2)}) %collective-permute-start.12) | collective-permute-done | bytes 426016 | tf_op jit(solution)/shard_map/ppermute | solution.py:1252
  391.2 3.8 all-gather.3.cloned.1.call-done
  396.4 4.1 fusion.10
  400.4 10.2 %fusion.21 = (f32[1024,1024]{1,0:T(8,128)}, f32[1024,1024]{1,0:T(8,128)}, f32[1024,1024]{1,0:T(8,128)}) fusion(f32[1024,3072]{1,0:T(8,128)} %all-gather.3.cloned.1.call-done), kind=kLoop, calls=%fused_computation.66 | loop fusion | bytes 25165824 | tf_op jit(solution)/shard_map/slice | solution.py:1557
  410.6 28.3 %collective-permute-done.13 = f32[512,1024]{1,0:T(8,128)S(1)} collective-permute-done((f32[512,1024]{1,0:T(8,128)S(1)}, f32[512,1024]{1,0:T(8,128)S(1)}, u32[]{:S(2)}, u32[]{:S(2)}) %collective-permute-start.13) | collective-permute-done | bytes 2097184 | tf_op jit(solution)/shard_map/ppermute | solution.py:1252
  439.5 2.0 fusion.8
  441.5 33.0 %all-gather.5.cloned.1.call-done.source = f32[1024,3328]{1,0:T(8,128)} async-done(((f32[32,3328]{1,0:T(8,128)}), f32[1024,3328]{1,0:T(8,128)}) %all-gather.5.cloned.1.call-update) | async-done | bytes 13631504 | tf_op jit(solution)/shard_map/all_gather | solution.py:1520
  474.5 11.8 %shard_map.445 = (f32[768,1024]{1,0:T(8,128)}, f32[256,1024]{1,0:T(8,128)}, f32[1024,2,768]{2,1,0:T(2,128)}, f32[1024,256]{1,0:T(8,128)}, f32[1024,1,128]{2,1,0:...) custom-call(f32[1024,3328]{1,0:T(8,128)} %all-gather.5.cloned.1.call-done.source), custom_call_target="tpu_custom_call" | custom-call | tf_op jit(solution)/shard_map/pallas_call | solution.py:655
  (185 shorter events, 44.0 us)
Async XLA Ops:
  7.2 240.5 %reduce-scatter.2.cloned.1.call-start = ((), (), s32[]{:S(2)}) async-start(), calls=%async_computation.2 | async-start | bytes 6684672 | tf_op jit(solution)/shard_map/reduce_scatter | solution.py:1407
  8.8 4.5 copy-start
  8.8 4.4 copy-start.27
  13.5 6.0 %copy-start.5 = (bf16[512,1024]{1,0:T(8,128)(2,1)}, bf16[512,1024]{1,0:T(8,128)(2,1)S(1)}, u32[]{:S(2)}) copy-start(bf16[512,1024]{1,0:T(8,128)(2,1)S(1)} %fusion.4.refs_6_) | copy-start | bytes 3145732
  13.6 5.8 %copy-start.23 = (bf16[1024,256]{1,0:T(8,128)(2,1)S(1)}, bf16[1024,256]{1,0:T(8,128)(2,1)}, u32[]{:S(2)}) copy-start(bf16[1024,256]{1,0:T(8,128)(2,1)} %param.42) | copy-start | bytes 1572868
  13.6 5.8 %copy-start.24 = (bf16[1024,256]{1,0:T(8,128)(2,1)S(1)}, bf16[1024,256]{1,0:T(8,128)(2,1)}, u32[]{:S(2)}) copy-start(bf16[1024,256]{1,0:T(8,128)(2,1)} %param.31) | copy-start | bytes 1572868
  13.6 5.8 %copy-start.26 = (bf16[1024,1,128]{2,0,1:T(8,128)(2,1)S(1)}, bf16[1024,1,128]{2,0,1:T(8,128)(2,1)}, u32[]{:S(2)}) copy-start(bf16[1024,1,128]{2,0,1:T(8,128)(2,1)} %param.43) | copy-start | bytes 786436
  19.6 4.4 copy-start.42
  19.6 5.8 %copy-start.40 = (f32[12]{0:T(128)S(1)}, f32[12]{0:T(128)}, u32[]{:S(2)}) copy-start(f32[12]{0:T(128)} %param.35) | copy-start | bytes 148
  37.0 5.3 %copy-start.35 = (f32[1,256]{1,0:T(1,128)S(1)}, f32[1,256]{1,0:T(1,128)}, u32[]{:S(2)}) copy-start(f32[1,256]{1,0:T(1,128)} %get-tuple-element.125.square_a_ref) | copy-start | bytes 3076
  37.0 13.3 %copy-start.13 = (f32[256,768]{1,0:T(8,128)S(1)}, f32[256,768]{1,0:T(8,128)}, u32[]{:S(2)}) copy-start(f32[256,768]{1,0:T(8,128)} %get-tuple-element.124.gated_ref) | copy-start | bytes 2359300
  37.0 13.3 %copy-start.32 = (f32[768]{0:T(1024)S(1)}, f32[768]{0:T(1024)}, u32[]{:S(2)}) copy-start(f32[768]{0:T(1024)} %param.40) | copy-start | bytes 9220
  42.3 9.4 %copy-start.2 = (bf16[768,1024]{1,0:T(8,128)(2,1)S(1)}, bf16[768,1024]{1,0:T(8,128)(2,1)}, u32[]{:S(2)}) copy-start(bf16[768,1024]{1,0:T(8,128)(2,1)} %mixer_out_ref.3) | copy-start | bytes 4718596
  43.2 7.1 %collective-permute-start = (f32[1,512]{1,0:T(1,128)S(1)}, f32[1,512]{1,0:T(1,128)S(1)}, u32[]{:S(2)}, u32[]{:S(2)}) collective-permute-start(f32[1,512]{1,0:T(1,128)S(1)} %constant_dynamic-update-slice_fusion), channel_id=1, source_target_pairs={{0,1},{1,0},{2,3},{3,2},{4,5},{5,4},{6,7},{7,6},{8,9},{9,8},{10,11... | collective-permute-start | bytes 6152 | tf_op jit(solution)/shard_map/ppermute | solution.py:1252
  51.7 6.8 %copy-start.3 = (bf16[256,768]{1,0:T(8,128)(2,1)}, bf16[256,768]{1,0:T(8,128)(2,1)S(1)}, u32[]{:S(2)}) copy-start(bf16[256,768]{1,0:T(8,128)(2,1)S(1)} %get-tuple-element.298.refs_0_.refs_2_) | copy-start | bytes 1179652
  54.3 24.3 %collective-permute-start.2 = (f32[256,1024]{1,0:T(8,128)}, f32[256,1024]{1,0:T(8,128)}, u32[]{:S(2)}, u32[]{:S(2)}) collective-permute-start(f32[256,1024]{1,0:T(8,128)} %convolution_add_fusion.1.part_ref), channel_id=1, source_target_pairs={{0,1},{1,0},{2,3},{3,2},{4,5},{5,4},{6,7},{7,6},{8,9},{9,8},{10,11... | collective-permute-start | bytes 3145736 | tf_op jit(solution)/shard_map/ppermute | solution.py:1252
  59.7 28.5 %copy-start.11 = (f32[256,1024]{1,0:T(8,128)}, f32[256,1024]{1,0:T(8,128)S(1)}, u32[]{:S(2)}) copy-start(f32[256,1024]{1,0:T(8,128)S(1)} %convolution_add_fusion.part_ref) | copy-start | bytes 3145732
  59.7 41.2 %collective-permute-start.1 = (f32[256,1024]{1,0:T(8,128)S(1)}, f32[256,1024]{1,0:T(8,128)S(1)}, u32[]{:S(2)}, u32[]{:S(2)}) collective-permute-start(f32[256,1024]{1,0:T(8,128)S(1)} %convolution_add_fusion.part_ref), channel_id=1, source_target_pairs={{0,1},{1,0},{2,3},{3,2},{4,5},{5,4},{6,7},{7,6},{8,9},{9,8},{10,11... | collective-permute-start | bytes 3145736 | tf_op jit(solution)/shard_map/ppermute | solution.py:1252
  88.3 35.2 %collective-permute-start.3 = (f32[256,1024]{1,0:T(8,128)}, f32[256,1024]{1,0:T(8,128)}, u32[]{:S(2)}, u32[]{:S(2)}) collective-permute-start(f32[256,1024]{1,0:T(8,128)} %get-tuple-element.136.part_ref), channel_id=1, source_target_pairs={{0,1},{1,0},{2,3},{3,2},{4,5},{5,4},{6,7},{7,6},{8,9},{9,8},{10,11... | collective-permute-start | bytes 3145736 | tf_op jit(solution)/shard_map/ppermute | solution.py:1252
  123.5 9.6 %copy-start.19 = (f32[256,1024]{1,0:T(8,128)S(1)}, f32[256,1024]{1,0:T(8,128)}, u32[]{:S(2)}) copy-start(f32[256,1024]{1,0:T(8,128)} %get-tuple-element.154.part_ref) | copy-start | bytes 3145732
  131.3 12.7 %collective-permute-start.4 = (f32[512,3072]{1,0:T(8,128)}, f32[512,3072]{1,0:T(8,128)}, u32[]{:S(2)}, u32[]{:S(2)}) collective-permute-start(f32[512,3072]{1,0:T(8,128)} %shard_map.433), channel_id=1, source_target_pairs={{0,2},{2,0},{1,3},{3,1},{4,6},{6,4},{5,7},{7,5},{8,10},{10,8},{9,1... | collective-permute-start | bytes 18874376 | tf_op jit(solution)/shard_map/ppermute | solution.py:1252
  133.1 24.7 %collective-permute-start.5 = (f32[256,1024]{1,0:T(8,128)S(1)}, f32[256,1024]{1,0:T(8,128)S(1)}, u32[]{:S(2)}, u32[]{:S(2)}) collective-permute-start(f32[256,1024]{1,0:T(8,128)S(1)} %copy-done.19), channel_id=1, source_target_pairs={{0,1},{1,0},{2,3},{3,2},{4,5},{5,4},{6,7},{7,6},{8,9},{9,8},{10,11... | collective-permute-start | bytes 3145736 | tf_op jit(solution)/shard_map/ppermute | solution.py:1252
  158.8 5.1 %copy-start.38 = (f32[1,256]{1,0:T(1,128)S(1)}, f32[1,256]{1,0:T(1,128)}, u32[]{:S(2)}) copy-start(f32[1,256]{1,0:T(1,128)} %get-tuple-element.160.dot_a_ref) | copy-start | bytes 3076
  164.7 13.3 %collective-permute-start.6 = (f32[1,512]{1,0:T(1,128)S(1)}, f32[1,512]{1,0:T(1,128)S(1)}, u32[]{:S(2)}, u32[]{:S(2)}) collective-permute-start(f32[1,512]{1,0:T(1,128)S(1)} %pad_maximum_fusion.2), channel_id=1, source_target_pairs={{0,1},{1,0},{2,3},{3,2},{4,5},{5,4},{6,7},{7,6},{8,9},{9,8},{10,11... | collective-permute-start | bytes 6152 | tf_op jit(solution)/shard_map/ppermute | solution.py:1252
  164.7 230.3 %all-gather.3.cloned.1.call-start = ((), (), s32[]{:S(2)}) async-start(), calls=%async_computation.3 | async-start | bytes 12976128 | tf_op jit(solution)/shard_map/all_gather | solution.py:1500
  202.3 14.9 %copy-start.30 = (f32[8,768]{1,0:T(8,128)S(1)}, f32[8,768]{1,0:T(8,128)}, u32[]{:S(2)}) copy-start(f32[8,768]{1,0:T(8,128)} %get-tuple-element.195) | copy-start | bytes 73732
  202.3 14.9 %copy-start.31 = (f32[8,768]{1,0:T(8,128)S(1)}, f32[8,768]{1,0:T(8,128)}, u32[]{:S(2)}) copy-start(f32[8,768]{1,0:T(8,128)} %get-tuple-element.196) | copy-start | bytes 73732
  202.3 15.2 %copy-start.34 = (f32[8,768]{1,0:T(8,128)S(1)}, f32[8,768]{1,0:T(8,128)}, u32[]{:S(2)}) copy-start(f32[8,768]{1,0:T(8,128)} %get-tuple-element.197) | copy-start | bytes 73732
  202.3 15.2 %copy-start.33 = (f32[32,128]{1,0:T(8,128)S(1)}, f32[32,128]{1,0:T(8,128)}, u32[]{:S(2)}) copy-start(f32[32,128]{1,0:T(8,128)} %get-tuple-element.194) | copy-start | bytes 49156
  202.3 15.4 %copy-start.37 = (f32[8,256]{1,0:T(8,128)S(1)}, f32[8,256]{1,0:T(8,128)}, u32[]{:S(2)}) copy-start(f32[8,256]{1,0:T(8,128)} %get-tuple-element.193) | copy-start | bytes 24580
  214.3 14.7 %collective-permute-start.7 = (f32[512,3328]{1,0:T(8,128)}, f32[512,3328]{1,0:T(8,128)}, u32[]{:S(2)}, u32[]{:S(2)}) collective-permute-start(f32[512,3328]{1,0:T(8,128)} %shard_map.442), channel_id=1, source_target_pairs={{0,2},{2,0},{1,3},{3,1},{4,6},{6,4},{5,7},{7,5},{8,10},{10,8},{9,1... | collective-permute-start | bytes 20447240 | tf_op jit(solution)/shard_map/ppermute | solution.py:1252
  226.2 1.8 collective-permute-start.8
  247.7 10.6 %collective-permute-start.9 = (f32[32,3072]{1,0:T(8,128)}, f32[32,3072]{1,0:T(8,128)S(1)}, u32[]{:S(2)}, u32[]{:S(2)}) collective-permute-start(f32[32,3072]{1,0:T(8,128)} %reduce-scatter.2.cloned.1.call-done), channel_id=1, source_target_pairs={{0,16},{16,0},{1,17},{17,1},{2,18},{18,2},{3,19},{19,3},{4,20},{20... | collective-permute-start | bytes 1179656 | tf_op jit(solution)/shard_map/ppermute | solution.py:1252
  260.1 4.9 copy-start.18
  260.1 112.0 %all-to-all-start = ((f32[16,32,3328]{2,1,0:T(8,128)}), f32[16,32,3328]{2,1,0:T(8,128)}, u32[]{:S(2)}, u32[]{:S(2)}) async-start(f32[16,32,3328]{2,1,0:T(8,128)} %bitcast.50), calls=%async_computation.1 | async-start | bytes 13631488 | tf_op jit(solution)/shard_map/all_to_all | solution.py:1508
  264.9 209.6 %all-gather.5.cloned.1.call-start = ((), (), s32[]{:S(2)}) async-start(), calls=%async_computation.4 | async-start | bytes 14057472 | tf_op jit(solution)/shard_map/all_gather | solution.py:1520
  267.6 113.4 %copy-start.39 = (pred[512]{0:T(512)(128)(4,1)S(1)}, pred[512]{0:T(512)(128)(4,1)}, u32[]{:S(2)}) copy-start(pred[512]{0:T(512)(128)(4,1)} %constant.71) | copy-start | bytes 1540
  267.6 44.3 %collective-permute-start.10 = (f32[512,1024]{1,0:T(8,128)S(1)}, f32[512,1024]{1,0:T(8,128)}, u32[]{:S(2)}, u32[]{:S(2)}) collective-permute-start(f32[512,1024]{1,0:T(8,128)S(1)} %constant_dynamic-update-slice_fusion.2), channel_id=1, source_target_pairs={{0,1},{1,0},{2,3},{3,2},{4,5},{5,4},{6,7},{7,6},{8,9},{9,8},{10,11... | collective-permute-start | bytes 6291464 | tf_op jit(solution)/shard_map/ppermute | solution.py:1252
  376.4 18.6 %copy-start.6 = (f32[512,1024]{1,0:T(8,128)S(1)}, f32[512,1024]{1,0:T(8,128)}, u32[]{:S(2)}) copy-start(f32[512,1024]{1,0:T(8,128)} %get-tuple-element.208) | copy-start | bytes 6291460
  376.4 19.9 %copy-start.12 = (f32[256,1024]{1,0:T(8,128)S(1)}, f32[256,1024]{1,0:T(8,128)}, u32[]{:S(2)}) copy-start(f32[256,1024]{1,0:T(8,128)} %get-tuple-element.139.hidden_ref) | copy-start | bytes 3145732
  377.4 3.5 collective-permute-start.11
  381.8 8.6 %collective-permute-start.12 = (f32[32,3328]{1,0:T(8,128)S(1)}, f32[32,3328]{1,0:T(8,128)S(1)}, u32[]{:S(2)}, u32[]{:S(2)}) collective-permute-start(f32[32,3328]{1,0:T(8,128)S(1)} %pad_maximum_fusion), channel_id=1, source_target_pairs={{0,16},{16,0},{1,17},{17,1},{2,18},{18,2},{3,19},{19,3},{4,20},{20... | collective-permute-start | bytes 1277960 | tf_op jit(solution)/shard_map/ppermute | solution.py:1252
  395.1 43.8 %collective-permute-start.13 = (f32[512,1024]{1,0:T(8,128)S(1)}, f32[512,1024]{1,0:T(8,128)S(1)}, u32[]{:S(2)}, u32[]{:S(2)}) collective-permute-start(f32[512,1024]{1,0:T(8,128)S(1)} %copy-done.6), channel_id=1, source_target_pairs={{0,1},{1,0},{2,3},{3,2},{4,5},{5,4},{6,7},{7,6},{8,9},{9,8},{10,11... | collective-permute-start | bytes 6291464 | tf_op jit(solution)/shard_map/ppermute | solution.py:1252
  400.4 38.5 %copy-start.1 = (bf16[512,1024]{1,0:T(8,128)(2,1)S(1)}, bf16[512,1024]{1,0:T(8,128)(2,1)}, u32[]{:S(2)}) copy-start(bf16[512,1024]{1,0:T(8,128)(2,1)} %tokens_ref.5) | copy-start | bytes 3145732
  400.4 38.5 %copy-start.28 = (f32[1024]{0:T(1024)S(1)}, f32[1024]{0:T(1024)}, u32[]{:S(2)}) copy-start(f32[1024]{0:T(1024)} %param.29) | copy-start | bytes 12292
  410.6 28.9 %copy-start.21 = (f32[256,1024]{1,0:T(8,128)S(1)}, f32[256,1024]{1,0:T(8,128)}, u32[]{:S(2)}) copy-start(f32[256,1024]{1,0:T(8,128)} %get-tuple-element.203) | copy-start | bytes 3145732
  410.6 28.9 %copy-start.22 = (f32[256,1024]{1,0:T(8,128)S(1)}, f32[256,1024]{1,0:T(8,128)}, u32[]{:S(2)}) copy-start(f32[256,1024]{1,0:T(8,128)} %get-tuple-element.202) | copy-start | bytes 3145732
  486.3 6.1 %copy-start.10 = (f32[1024,128]{1,0:T(8,128)S(1)}, f32[1024,128]{1,0:T(8,128)}, u32[]{:S(2)}) copy-start(f32[1024,128]{1,0:T(8,128)} %get-tuple-element.209) | copy-start | bytes 1572868
  (13 other events, 25.9 us)
Sparse Core Ops, SparseCore 0:
  164.8 82.8 reduce-scatter.1
  260.2 134.7 all-gather.2
  397.8 76.6 all-gather.4
